TPU v7x, 32 devices: a whole 2x2x4 slice. The times are simulated.
32 devices in a mesh: sec: 4 (over y, x), gx: 4 (over z), gz: 2 (over core).
Axes of the slice: x: 2, y: 2, z: 4, core: 2. Of those that a mesh axis runs over, the one named last changes fastest.
Arguments:
- fields: float32 [4, 5, 512, 256], P('sec', None, 'gx', 'gz'), may hold values from -6 to 6
- media: float32 [4, 3, 512, 256], P('sec', None, 'gx', 'gz'), may hold values from 0.5 to 2
- plane_rows: int32 [16], replicated, may hold values from 0 to 255, as said below
- box_offset: int32 [3], replicated, may hold values from 0 to 128
Outputs:
- evolved: float32 [4, 5, 512, 256], P('sec', None, 'gx', 'gz')
Inputs may be any that keep to these rules, and one draw needn't show every extreme that they name: `plane_rows`: entries 8 * j to 8 * j + 7 are distinct rows of the j-th depth block of 128 rows; row 0 and row 255 are always among them.
All inputs are finite; a program needn't handle non-finite values.
Results may differ from a plain program's by a relative error of at most 0.00013.
Values sent between devices are 32-bit elements; how exact they have to be, the bound alone decides.
No kernel may reach another device: no remote copies, remote signals or barrier semaphores. Data moves between devices by JAX's collectives and lax.ppermute only.
A program may use at most 64 MiB of HBM per device.

v0:
```python
import functools

import jax
import jax.numpy as jnp
from jax import lax
from jax.experimental import pallas as pl
from jax.experimental.pallas import tpu as pltpu
from jax.sharding import PartitionSpec as P

RADIUS = 4
STEPS = 5
NPD = 8

STENCIL = (0.8, -0.2, 4.0 / 105.0, -1.0 / 280.0)
TIME_STEP = 0.2
COUPLING = 0.5
RELAXATION = (0.9, 0.5)
MEMORY_WEIGHT = (0.15, 0.1)


def padded_2(block, sides, width):
    for axis, dim in sides:
        count = lax.axis_size(axis)
        forward = [(i, i + 1) for i in range(count - 1)]
        backward = [(target, source) for source, target in forward]
        low = lax.ppermute(
            lax.slice_in_dim(block, block.shape[dim] - width, None, axis=dim), axis, forward
        )
        high = lax.ppermute(lax.slice_in_dim(block, 0, width, axis=dim), axis, backward)
        block = jnp.concatenate([low, block, high], axis=dim)
    return block


def broadcast(value, axis, source):
    kept = jnp.where(lax.axis_index(axis) == source, value, 0).astype(value.dtype)
    return lax.psum(kept, axis)


def along_x(padded, anchor, count_x, count_z):
    summed = jnp.zeros(padded.shape[:-2] + (count_x, count_z), jnp.float32)
    for offset, stencil_tap in enumerate(STENCIL, 1):
        forward = padded[
            ..., anchor + offset : anchor + offset + count_x, anchor : anchor + count_z
        ]
        backward = padded[
            ..., anchor - offset : anchor - offset + count_x, anchor : anchor + count_z
        ]
        summed = summed + stencil_tap * (forward - backward)
    return summed


def along_z(padded, anchor, count_x, count_z):
    summed = jnp.zeros(padded.shape[:-2] + (count_x, count_z), jnp.float32)
    for offset, stencil_tap in enumerate(STENCIL, 1):
        forward = padded[
            ..., anchor : anchor + count_x, anchor + offset : anchor + offset + count_z
        ]
        backward = padded[
            ..., anchor : anchor + count_x, anchor - offset : anchor - offset + count_z
        ]
        summed = summed + stencil_tap * (forward - backward)
    return summed


def velocity_elastic(velocity, stresses, buoyancy, anchor, count_x, count_z):
    updated_x = velocity[0] + TIME_STEP * buoyancy * (
        along_x(stresses[0], anchor, count_x, count_z)
        + along_z(stresses[2], anchor, count_x, count_z)
    )
    updated_z = velocity[1] + TIME_STEP * buoyancy * (
        along_x(stresses[2], anchor, count_x, count_z)
        + along_z(stresses[1], anchor, count_x, count_z)
    )
    return jnp.stack([updated_x, updated_z])


def velocity_acoustic(velocity, stresses, buoyancy, anchor, count_x, count_z):
    updated_x = velocity[0] - TIME_STEP * buoyancy * along_x(stresses[0], anchor, count_x, count_z)
    updated_z = velocity[1] - TIME_STEP * buoyancy * along_z(stresses[0], anchor, count_x, count_z)
    return jnp.stack([updated_x, updated_z])


def stress_elastic(stresses, velocity_pad, material, anchor, count_x, count_z):
    strain_x = along_x(velocity_pad[0], anchor, count_x, count_z)
    strain_z = along_z(velocity_pad[1], anchor, count_x, count_z)
    strain_shear = along_z(velocity_pad[0], anchor, count_x, count_z) + along_x(
        velocity_pad[1], anchor, count_x, count_z
    )
    lame_first = material[1]
    shear_modulus = material[2]
    normal_x = stresses[0] + TIME_STEP * (
        (lame_first + 2.0 * shear_modulus) * strain_x + lame_first * strain_z
    )
    normal_z = stresses[1] + TIME_STEP * (
        lame_first * strain_x + (lame_first + 2.0 * shear_modulus) * strain_z
    )
    shear_new = stresses[2] + TIME_STEP * shear_modulus * strain_shear
    return jnp.stack([normal_x, normal_z, shear_new])


def stress_acoustic(stresses, velocity_pad, material, anchor, count_x, count_z):
    divergence = along_x(velocity_pad[0], anchor, count_x, count_z) + along_z(
        velocity_pad[1], anchor, count_x, count_z
    )
    loading = material[1] * divergence
    memory_one = (
        RELAXATION[0] * stresses[1]
        + (1.0 - RELAXATION[0]) * MEMORY_WEIGHT[0] * material[2] * loading
    )
    memory_two = (
        RELAXATION[1] * stresses[2]
        + (1.0 - RELAXATION[1]) * MEMORY_WEIGHT[1] * material[2] * loading
    )
    pressure = stresses[0] - TIME_STEP * (loading - memory_one - memory_two)
    return jnp.stack([pressure, memory_one, memory_two])


def local_stepwise(fields, media, plane_rows, box_offset):
    current = fields[0]
    material = media[0]
    count_x = current.shape[1]
    count_z = current.shape[2]
    section = lax.axis_index("sec")
    is_source = section == 0
    block_z = lax.axis_index("gz")
    local_rows = lax.dynamic_slice_in_dim(plane_rows, block_z * NPD, NPD) - block_z * count_z
    offset = lax.dynamic_slice_in_dim(box_offset, jnp.maximum(section - 1, 0), 1)[0]
    depth_ids = block_z * count_z + jnp.arange(count_z, dtype=jnp.int32)
    landing = offset + plane_rows // 2
    chosen = (landing[:, None] == depth_ids[None, :]).astype(jnp.float32)
    for step_index in range(STEPS):
        stress_pad = padded_2(current[2:5], (("gx", 1), ("gz", 2)), RADIUS)
        velocity = lax.cond(
            is_source,
            lambda: velocity_elastic(
                current[0:2], stress_pad, material[0], RADIUS, count_x, count_z
            ),
            lambda: velocity_acoustic(
                current[0:2], stress_pad, material[0], RADIUS, count_x, count_z
            ),
        )
        velocity_pad = padded_2(velocity, (("gx", 1), ("gz", 2)), RADIUS)
        stresses = lax.cond(
            is_source,
            lambda: stress_elastic(current[2:5], velocity_pad, material, RADIUS, count_x, count_z),
            lambda: stress_acoustic(current[2:5], velocity_pad, material, RADIUS, count_x, count_z),
        )
        current = jnp.concatenate([velocity, stresses], axis=0)
        picked = jnp.take(current, local_rows, axis=2)
        block_plane = jnp.transpose(
            jnp.stack([picked[0], picked[1], -0.5 * (picked[2] + picked[3])]), (0, 2, 1)
        )
        joined = lax.all_gather(block_plane, "gz", axis=1, tiled=True)
        gathered = broadcast(joined, "sec", 0)
        injected = jnp.einsum("ckx,kz->cxz", gathered, chosen, precision=lax.Precision.HIGHEST)
        far_state = jnp.concatenate([current[0:3] + COUPLING * injected, current[3:5]], axis=0)
        current = jnp.where(is_source, current, far_state)
    return current[None]


HALO = 2 * RADIUS * STEPS
CELLS = 128
HALF = CELLS // 2
WINDOW = HALF + 2 * HALO
DEPTH = 2 * CELLS
PART = HALF + HALO
NP = 2 * NPD
TRIM = (0, 0, 16, 16, 32)
WINDOWS = [WINDOW - 2 * amount for amount in sorted(set(TRIM))]
COUNTS = len(WINDOWS)
ROWS = 192
GROUPS = CELLS // NP
SLOT = (
    ((0, 0), (1, 0), (2, 0)),
    ((3, 0), (4, 0), (5, 0)),
    ((6, 0), (7, 0), (6, 96)),
    ((3, 112), (4, 112), (5, 112)),
    ((0, 128), (1, 128), (2, 128)),
)
SCALE = 840.0
TAPS = (672.0, -168.0, 32.0, -3.0)


def banded(distance):
    values = jnp.zeros(distance.shape, jnp.float32)
    for offset, tap in enumerate(TAPS, 1):
        values = jnp.where(distance == offset, tap, values)
        values = jnp.where(distance == -offset, -tap, values)
    return values.astype(jnp.bfloat16)


def halves(values):
    high = values.astype(jnp.bfloat16)
    low = (values - high.astype(jnp.float32)).astype(jnp.bfloat16)
    return high, low


def dot(left, right):
    return jnp.dot(left, right, preferred_element_type=jnp.float32)


def diff_x(bands, parts):
    return dot(bands[parts[0].shape[0]][...], jnp.concatenate(parts, axis=0))


def along_depth(matrix, parts):
    return dot(jnp.concatenate(parts, axis=1), matrix[...])


def trimmed(arrays, amount):
    if amount == 0:
        return arrays
    return [array[amount:-amount] for array in arrays]


def lanes_of(shape):
    return lax.broadcasted_iota(jnp.int32, shape, 1) // NP


def assemble(window, block, ahead, behind, other):
    core = lax.axis_index("gz")

    @pl.when(core == 0)
    def _():
        for index in range(8):
            window[index, :HALO, :CELLS] = ahead[index]
            window[index, :HALO, CELLS:] = behind[index]
            window[index, HALO:, :CELLS] = block[index, :PART]
            window[index, HALO:, CELLS:] = other[index]

    @pl.when(core == 1)
    def _():
        for index in range(8):
            window[index, :PART, CELLS:] = block[index, CELLS - PART :]
            window[index, :PART, :CELLS] = other[index]
            window[index, PART:, CELLS:] = ahead[index]
            window[index, PART:, :CELLS] = behind[index]


def place(state, held, sent):
    start = HALO - TRIM[-1]
    core = lax.axis_index("gz")
    state = [array[start : start + HALF] for array in state]

    @pl.when(core == 0)
    def _():
        for index in range(5):
            held[index] = state[index][:, :CELLS]
            sent[index] = state[index][:, CELLS:]

    @pl.when(core == 1)
    def _():
        for index in range(5):
            held[index] = state[index][:, CELLS:]
            sent[index] = state[index][:, :CELLS]


def acoustic(state, bands):
    vx, vz, pressure, one, two, light, kappa, loss_one, loss_two = state
    band_x, band_z = bands
    parts = halves(pressure)
    vx = vx - light * diff_x(band_x, parts)
    vz = vz - light * along_depth(band_z, parts)
    load = kappa * (diff_x(band_x, halves(vx)) + along_depth(band_z, halves(vz)))
    one = RELAXATION[0] * one + loss_one * load
    two = RELAXATION[1] * two + loss_two * load
    pressure = pressure - TIME_STEP * (load - one - two)
    return [vx, vz, pressure, one, two, light, kappa, loss_one, loss_two]


def constants_kernel(plane_rows, box_offset, *targets):
    *bands_x, band_z, pick, land = targets
    for target in bands_x:
        count = target.shape[0]
        row = lax.broadcasted_iota(jnp.int32, target.shape, 0)
        column = lax.broadcasted_iota(jnp.int32, target.shape, 1)
        target[...] = banded(jnp.where(column < count, column, column - count) - row)
    shape = (DEPTH, DEPTH)
    distance = lax.broadcasted_iota(jnp.int32, shape, 0) - lax.broadcasted_iota(jnp.int32, shape, 1)
    band_z[:DEPTH] = banded(distance)
    band_z[DEPTH:] = band_z[:DEPTH]
    row = plane_rows[...]
    lane = lax.broadcasted_iota(jnp.int32, box_offset.shape, 1)
    offset = jnp.where(lane == lax.axis_index("sec") - 1, box_offset[...], 0)
    landing = row // 2 + jnp.sum(offset, axis=1, keepdims=True)
    depth = lax.broadcasted_iota(jnp.int32, (DEPTH, NP), 0)
    spread = lax.broadcasted_iota(jnp.int32, (NP, CELLS), 1) % NP
    spread = spread == lax.broadcasted_iota(jnp.int32, (NP, CELLS), 0)
    spread = jnp.where(spread, 1.0, 0.0).astype(jnp.bfloat16)
    hot = jnp.where(depth == row, 1.0, 0.0).astype(jnp.bfloat16)
    pick[:DEPTH] = dot(hot, spread).astype(jnp.bfloat16)
    pick[DEPTH:] = pick[:DEPTH]
    hot = jnp.where(depth == landing, 1.0, 0.0).astype(jnp.bfloat16)
    land[:, :CELLS] = dot(hot, spread).astype(jnp.bfloat16)
    land[:, CELLS:] = land[:, :CELLS]


def first_kernel(*refs):
    bands_x, (band_z, pick, block, ahead, behind, other) = refs[:COUNTS], refs[COUNTS:-4]
    held, sent, rows, carry = refs[-4:]
    band_x = {band.shape[0]: band for band in bands_x}
    assemble(carry, block, ahead, behind, other)
    section = lax.axis_index("sec")

    @pl.when(section == 0)
    def _():
        vx, vz, sxx, szz, sxz, light, lame, shear = [carry[index] for index in range(8)]
        light = light * (TIME_STEP / SCALE)
        both = (lame + 2.0 * shear) * (TIME_STEP / SCALE)
        lame = lame * (TIME_STEP / SCALE)
        shear = shear * (TIME_STEP / SCALE)
        at = 0
        for step in range(STEPS):
            cut = TRIM[step] - at
            at = TRIM[step]
            vx, vz, sxx, szz, sxz, light, both, lame, shear = trimmed(
                [vx, vz, sxx, szz, sxz, light, both, lame, shear], cut
            )
            parts_xx, parts_zz, parts_xz = halves(sxx), halves(szz), halves(sxz)
            vx = vx + light * (diff_x(band_x, parts_xx) + along_depth(band_z, parts_xz))
            vz = vz + light * (diff_x(band_x, parts_xz) + along_depth(band_z, parts_zz))
            parts_x, parts_z = halves(vx), halves(vz)
            strain_x, strain_z = diff_x(band_x, parts_x), along_depth(band_z, parts_z)
            sxx = sxx + (both * strain_x + lame * strain_z)
            szz = szz + (lame * strain_x + both * strain_z)
            sxz = sxz + shear * (along_depth(band_z, parts_x) + diff_x(band_x, parts_z))
            low = 2 * RADIUS * (step + 1) - at
            for component, (parts, factor) in enumerate(
                ((parts_x, COUPLING), (parts_z, COUPLING), (halves(sxx + szz), -0.5 * COUPLING))
            ):
                picked = factor * along_depth(pick, parts)
                picked = picked[low : picked.shape[0] - low]
                group, base = SLOT[step][component]
                spot = pl.ds(base, picked.shape[0])
                rows[spot] = jnp.where(lanes_of(picked.shape) == group, picked, rows[spot])
        place([vx, vz, sxx, szz, sxz], held, sent)

    @pl.when(section > 0)
    def _():
        vx, vz, pressure, one, two, light, kappa, loss = [carry[index] for index in range(8)]
        light = light * (TIME_STEP / SCALE)
        kappa = kappa * (1.0 / SCALE)
        loss_one = loss * ((1.0 - RELAXATION[0]) * MEMORY_WEIGHT[0])
        loss_two = loss * ((1.0 - RELAXATION[1]) * MEMORY_WEIGHT[1])
        state = [vx, vz, pressure, one, two, light, kappa, loss_one, loss_two]
        for index, array in enumerate(acoustic(state, (band_x, band_z))):
            carry[index] = array


def second_kernel(*refs):
    bands_x, (band_z, land, carry, rows, held_in, sent_in, held, sent) = refs[:COUNTS], refs[COUNTS:]
    band_x = {band.shape[0]: band for band in bands_x}
    section = lax.axis_index("sec")

    @pl.when(section == 0)
    def _():
        held[...] = held_in[...]
        sent[...] = sent_in[...]

    @pl.when(section > 0)
    def _():
        state = [carry[index] for index in range(9)]
        at = 0
        for step in range(STEPS):
            if step:
                state = trimmed(state, TRIM[step] - at)
                at = TRIM[step]
                state = acoustic(state, (band_x, band_z))
            low = 2 * RADIUS * (step + 1) - at
            high = WINDOW - 2 * at - low
            for component in range(3):
                group, base = SLOT[step][component]
                taken = rows[pl.ds(base, high - low)]
                taken = halves(jnp.where(lanes_of(taken.shape) == group, taken, 0.0))
                added = lax.dot_general(
                    jnp.concatenate(taken, axis=1),
                    land[...],
                    (((1,), (1,)), ((), ())),
                    preferred_element_type=jnp.float32,
                )
                array = state[component]
                state[component] = jnp.concatenate(
                    [array[:low], array[low:high] + added, array[high:]], axis=0
                )
        place(state[:5], held, sent)


def last_kernel(held, swapped, out, sems):
    core = lax.axis_index("gz")
    copies = [
        pltpu.make_async_copy(
            source, out.at[:, pl.ds(pl.multiple_of(HALF * half, HALF), HALF)], sems.at[index]
        )
        for index, (source, half) in enumerate(((held, core), (swapped, 1 - core)))
    ]
    for copy in copies:
        copy.start()
    for copy in copies:
        copy.wait()


def call(kernel, outs, operands, flops, place_out=pltpu.VMEM, scratch=()):
    return pl.pallas_call(
        kernel,
        out_shape=outs,
        in_specs=[pl.BlockSpec(memory_space=pltpu.VMEM)] * len(operands),
        out_specs=[pl.BlockSpec(memory_space=place_out)] * len(outs),
        scratch_shapes=scratch,
        compiler_params=pltpu.CompilerParams(vmem_limit_bytes=48 * 1024 * 1024),
        cost_estimate=pl.CostEstimate(
            flops=flops, bytes_accessed=2 * 1024 * 1024, transcendentals=0
        ),
    )(*operands)


def full(*shape):
    return jax.ShapeDtypeStruct(shape, jnp.float32)


def narrow(*shape):
    return jax.ShapeDtypeStruct(shape, jnp.bfloat16)


def local_window(columns, fields, media, plane_rows, box_offset):
    fields, media = fields[0], media[0]
    core = lax.axis_index("gz")
    is_first = core == 0
    block = lax.optimization_barrier(jnp.concatenate([fields, media], axis=0))
    top, bottom = block[:, :HALO], block[:, CELLS - HALO :]
    straight_pairs, crossed_pairs = [], []
    for column in range(columns):
        if column + 1 < columns:
            straight_pairs.append((2 * column, 2 * column + 2))
            crossed_pairs.append((2 * column + 1, 2 * column + 2))
        if column:
            straight_pairs.append((2 * column + 1, 2 * column - 1))
            crossed_pairs.append((2 * column, 2 * column - 1))
    turn = [(0, 1), (1, 0)]
    ahead = lax.ppermute(jnp.where(is_first, bottom, top), ("gx", "gz"), straight_pairs)
    behind = lax.ppermute(jnp.where(is_first, top, bottom), ("gx", "gz"), crossed_pairs)
    other = jnp.where(is_first, block[:, CELLS - PART :], block[:, :PART])
    joined = lax.all_gather(other, "gz")
    other = jnp.where(is_first, joined[1], joined[0])
    *bands, pick, land = call(
        constants_kernel,
        [narrow(count, 2 * count) for count in WINDOWS]
        + [narrow(2 * DEPTH, DEPTH), narrow(2 * DEPTH, CELLS), narrow(DEPTH, 2 * CELLS)],
        [plane_rows[None], box_offset[None]],
        1_000_000_000,
    )
    held, sent, rows, carry = call(
        first_kernel,
        [
            full(5, HALF, CELLS),
            full(5, HALF, CELLS),
            full(ROWS, CELLS),
            full(9, WINDOW, DEPTH),
        ],
        [*bands, pick, block, ahead, behind, other],
        4_000_000_000,
    )
    arrived = [lax.ppermute(rows, "sec", [(0, target)]) for target in (1, 2, 3)]
    rows = arrived[0] + arrived[1] + arrived[2]
    held, sent = call(
        second_kernel,
        [full(5, HALF, CELLS), full(5, HALF, CELLS)],
        [*bands, land, carry, rows, held, sent],
        4_000_000_000,
    )
    swapped = lax.ppermute(sent, "gz", turn)
    (out,) = call(
        last_kernel,
        [full(5, CELLS, CELLS)],
        [held, swapped],
        1000,
        pl.ANY,
        [pltpu.SemaphoreType.DMA((2,))],
    )
    return out[None]


def solution(mesh):
    in_specs = (P("sec", None, "gx", "gz"), P("sec", None, "gx", "gz"), P(), P())
    out_specs = P("sec", None, "gx", "gz")
    if mesh.shape["gz"] == 2:
        local = functools.partial(local_window, mesh.shape["gx"])
    else:
        local = local_stepwise
    return jax.shard_map(local, mesh=mesh, in_specs=in_specs, out_specs=out_specs, check_vma=False)
```

profile of v0, /device:TPU:19, one launch (start us, length us, event | category | flops | bytes accessed | tf_op | source)
XLA Modules:
  0.0 26.1 jit_solution(10813253547888806148)
XLA Ops:
  0.0 1.1 %pad_maximum_fusion.refs_5_ = f32[8,128,128]{2,1,0:T(8,128)S(1)} fusion(f32[3,128,128]{2,1,0:T(8,128)} %bitcast.8, f32[5,128,128]{2,1,0:T(8,128)} %bitcast.7), kind=kLoop, calls=%fused_computation | loop fusion | flops 131072 | bytes 1048576 | tf_op jit(solution)/shard_map/concatenate | solution.py:428
  1.2 3.8 %collective-permute-start.1 = (f32[8,40,128]{2,1,0:T(8,128)S(1)}, f32[8,40,128]{2,1,0:T(8,128)S(1)}, u32[]{:S(2)}, u32[]{:S(2)}) collective-permute-start(f32[8,40,128]{2,1,0:T(8,128)S(1)} %get-tuple-element.29), channel_id=1, source_target_pairs={{1,2},{3,4},{2,1},{5,6},{4,3},{6,5},{9,10},{11,12},{10,9},{13,14},... | collective-permute-start | bytes 491528 | tf_op jit(solution)/shard_map/ppermute | solution.py:440
  4.9 2.1 %collective-permute-start = (f32[8,40,128]{2,1,0:T(8,128)S(1)}, f32[8,40,128]{2,1,0:T(8,128)S(1)}, u32[]{:S(2)}, u32[]{:S(2)}) collective-permute-start(f32[8,40,128]{2,1,0:T(8,128)S(1)} %get-tuple-element.30), channel_id=1, source_target_pairs={{0,2},{2,4},{3,1},{4,6},{5,3},{7,5},{8,10},{10,12},{11,9},{12,14},... | collective-permute-start | bytes 491528 | tf_op jit(solution)/shard_map/ppermute | solution.py:439
  7.1 0.0 copy-start
  7.1 0.0 copy-start.1
  7.1 2.4 %all-gather = f32[16,104,128]{2,1,0:T(8,128)S(1)} all-gather(f32[8,104,128]{2,1,0:T(8,128)S(1)} %slice_select_fusion.1), channel_id=2, replica_groups=mesh['sec'=4,'gx'=4,'gz'=2] {'gz'}, dimensions={0}, use_global_device_ids=true | all-gather | bytes 1277952 | tf_op jit(solution)/shard_map/all_gather | solution.py:442
  9.5 0.0 copy-done
  9.6 0.0 copy-done.1
  9.6 0.4 %shard_map.46 = (bf16[144,288]{1,0:T(8,128)(2,1)S(1)}, bf16[112,224]{1,0:T(8,128)(2,1)S(1)}, bf16[80,160]{1,0:T(8,128)(2,1)S(1)}, bf16[512,256]{1,0:T(8,128)(2,1...) custom-call(s32[1,16]{1,0:T(1,128)S(1)} %bitcast.5, s32[1,3]{1,0:T(1,128)S(1)} %bitcast.6), custom_call_target="tpu_custom_call" | custom-call | flops 1000000000 | bytes 2097152 | tf_op jit(solution)/shard_map/pallas_call | solution.py:403
  10.0 0.0 collective-permute-done.1.refs_7_
  10.0 1.0 %collective-permute-done.refs_6_ = f32[8,40,128]{2,1,0:T(8,128)S(1)} collective-permute-done((f32[8,40,128]{2,1,0:T(8,128)S(1)}, f32[8,40,128]{2,1,0:T(8,128)S(1)}, u32[]{:S(2)}, u32[]{:S(2)}) %collective-permute-start) | collective-permute-done | bytes 163872 | tf_op jit(solution)/shard_map/ppermute | solution.py:439
  11.0 0.6 %shard_map.47 = (f32[5,64,128]{2,1,0:T(8,128)S(1)}, f32[5,64,128]{2,1,0:T(8,128)S(1)}, f32[192,128]{1,0:T(8,128)S(1)}, f32[9,144,256]{2,1,0:T(8,128)S(1)}) custom-call(bf16[144,288]{1,0:T(8,128)(2,1)S(1)} %get-tuple-element.17.refs_0_, bf16[112,224]{1,0:T(8,128)(2,1)S(1)} %get-tuple-element.18.refs_1_, bf16[80,160]{1,0:T(8,128)(2,1)S(1)} %get-tuple-element.19.refs_2_, ...), custom_call_target="tpu_custom_call" | custom-call | flops 4000000000 | bytes 2097152 | tf_op jit(solution)/shard_map/pallas_call | solution.py:403
  11.6 0.7 %collective-permute-start.4 = (f32[192,128]{1,0:T(8,128)S(1)}, f32[192,128]{1,0:T(8,128)S(1)}, u32[]{:S(2)}, u32[]{:S(2)}) collective-permute-start(f32[192,128]{1,0:T(8,128)S(1)} %get-tuple-element.24), channel_id=1, source_target_pairs={{0,24},{1,25},{2,26},{3,27},{4,28},{5,29},{6,30},{7,31}} | collective-permute-start | bytes 294920 | tf_op jit(solution)/shard_map/ppermute | solution.py:462
  12.3 0.7 %collective-permute-start.3 = (f32[192,128]{1,0:T(8,128)S(1)}, f32[192,128]{1,0:T(8,128)S(1)}, u32[]{:S(2)}, u32[]{:S(2)}) collective-permute-start(f32[192,128]{1,0:T(8,128)S(1)} %get-tuple-element.24), channel_id=1, source_target_pairs={{0,16},{1,17},{2,18},{3,19},{4,20},{5,21},{6,22},{7,23}} | collective-permute-start | bytes 294920 | tf_op jit(solution)/shard_map/ppermute | solution.py:462
  13.0 1.3 %collective-permute-start.2 = (f32[192,128]{1,0:T(8,128)S(1)}, f32[192,128]{1,0:T(8,128)S(1)}, u32[]{:S(2)}, u32[]{:S(2)}) collective-permute-start(f32[192,128]{1,0:T(8,128)S(1)} %get-tuple-element.24), channel_id=1, source_target_pairs={{0,8},{1,9},{2,10},{3,11},{4,12},{5,13},{6,14},{7,15}} | collective-permute-start | bytes 294920 | tf_op jit(solution)/shard_map/ppermute | solution.py:462
  14.3 0.0 collective-permute-done.4
  14.3 0.0 collective-permute-done.3
  14.3 7.2 %collective-permute-done.2 = f32[192,128]{1,0:T(8,128)S(1)} collective-permute-done((f32[192,128]{1,0:T(8,128)S(1)}, f32[192,128]{1,0:T(8,128)S(1)}, u32[]{:S(2)}, u32[]{:S(2)}) %collective-permute-start.2) | collective-permute-done | bytes 98336 | tf_op jit(solution)/shard_map/ppermute | solution.py:462
  21.5 2.0 %shard_map.48 = (f32[5,64,128]{2,1,0:T(8,128)S(1)}, f32[5,64,128]{2,1,0:T(8,128)S(1)}) custom-call(bf16[144,288]{1,0:T(8,128)(2,1)S(1)} %get-tuple-element.17.refs_0_, bf16[112,224]{1,0:T(8,128)(2,1)S(1)} %get-tuple-element.18.refs_1_, bf16[80,160]{1,0:T(8,128)(2,1)S(1)} %get-tuple-element.19.refs_2_, bf16[512,256]{1,0:T(8,128)(2,1)S(1)} %get-tuple-element.20.refs_3_, ...), custom_call_target="tpu_custom_call" | custom-call | flops 4000000000 | bytes 2097152 | tf_op jit(solution)/shard_map/pallas_call | solution.py:403
  23.6 0.8 %collective-permute-start.5 = (f32[5,64,128]{2,1,0:T(8,128)S(1)}, f32[5,64,128]{2,1,0:T(8,128)S(1)}, u32[]{:S(2)}, u32[]{:S(2)}) collective-permute-start(f32[5,64,128]{2,1,0:T(8,128)S(1)} %get-tuple-element.28), channel_id=1, source_target_pairs={{0,1},{1,0},{2,3},{3,2},{4,5},{5,4},{6,7},{7,6},{8,9},{9,8},{10,11... | collective-permute-start | bytes 491528 | tf_op jit(solution)/shard_map/ppermute | solution.py:470
  24.4 1.0 %collective-permute-done.5.swapped = f32[5,64,128]{2,1,0:T(8,128)S(1)} collective-permute-done((f32[5,64,128]{2,1,0:T(8,128)S(1)}, f32[5,64,128]{2,1,0:T(8,128)S(1)}, u32[]{:S(2)}, u32[]{:S(2)}) %collective-permute-start.5) | collective-permute-done | bytes 163872 | tf_op jit(solution)/shard_map/ppermute | solution.py:470
  25.4 0.7 %shard_map.49 = f32[5,128,128]{2,1,0:T(8,128)} custom-call(f32[5,64,128]{2,1,0:T(8,128)S(1)} %get-tuple-element.27.held, f32[5,64,128]{2,1,0:T(8,128)S(1)} %collective-permute-done.5.swapped), custom_call_target="tpu_custom_call" | custom-call | flops 1000 | bytes 2097152 | tf_op jit(solution)/shard_map/pallas_call | solution.py:403
  (4 shorter events, 0.1 us)
Async XLA Ops:
  1.2 8.9 %collective-permute-start.1 = (f32[8,40,128]{2,1,0:T(8,128)S(1)}, f32[8,40,128]{2,1,0:T(8,128)S(1)}, u32[]{:S(2)}, u32[]{:S(2)}) collective-permute-start(f32[8,40,128]{2,1,0:T(8,128)S(1)} %get-tuple-element.29), channel_id=1, source_target_pairs={{1,2},{3,4},{2,1},{5,6},{4,3},{6,5},{9,10},{11,12},{10,9},{13,14},... | collective-permute-start | bytes 491528 | tf_op jit(solution)/shard_map/ppermute | solution.py:440
  4.9 6.1 %collective-permute-start = (f32[8,40,128]{2,1,0:T(8,128)S(1)}, f32[8,40,128]{2,1,0:T(8,128)S(1)}, u32[]{:S(2)}, u32[]{:S(2)}) collective-permute-start(f32[8,40,128]{2,1,0:T(8,128)S(1)} %get-tuple-element.30), channel_id=1, source_target_pairs={{0,2},{2,4},{3,1},{4,6},{5,3},{7,5},{8,10},{10,12},{11,9},{12,14},... | collective-permute-start | bytes 491528 | tf_op jit(solution)/shard_map/ppermute | solution.py:439
  7.1 2.5 %copy-start = (s32[16]{0:T(128)S(1)}, s32[16]{0:T(128)}, u32[]{:S(2)}) copy-start(s32[16]{0:T(128)} %param.6) | copy-start | bytes 196
  7.1 2.5 %copy-start.1 = (s32[3]{0:T(128)S(1)}, s32[3]{0:T(128)}, u32[]{:S(2)}) copy-start(s32[3]{0:T(128)} %param.7) | copy-start | bytes 40
  11.6 2.7 %collective-permute-start.4 = (f32[192,128]{1,0:T(8,128)S(1)}, f32[192,128]{1,0:T(8,128)S(1)}, u32[]{:S(2)}, u32[]{:S(2)}) collective-permute-start(f32[192,128]{1,0:T(8,128)S(1)} %get-tuple-element.24), channel_id=1, source_target_pairs={{0,24},{1,25},{2,26},{3,27},{4,28},{5,29},{6,30},{7,31}} | collective-permute-start | bytes 294920 | tf_op jit(solution)/shard_map/ppermute | solution.py:462
  12.3 2.0 %collective-permute-start.3 = (f32[192,128]{1,0:T(8,128)S(1)}, f32[192,128]{1,0:T(8,128)S(1)}, u32[]{:S(2)}, u32[]{:S(2)}) collective-permute-start(f32[192,128]{1,0:T(8,128)S(1)} %get-tuple-element.24), channel_id=1, source_target_pairs={{0,16},{1,17},{2,18},{3,19},{4,20},{5,21},{6,22},{7,23}} | collective-permute-start | bytes 294920 | tf_op jit(solution)/shard_map/ppermute | solution.py:462
  13.0 8.6 %collective-permute-start.2 = (f32[192,128]{1,0:T(8,128)S(1)}, f32[192,128]{1,0:T(8,128)S(1)}, u32[]{:S(2)}, u32[]{:S(2)}) collective-permute-start(f32[192,128]{1,0:T(8,128)S(1)} %get-tuple-element.24), channel_id=1, source_target_pairs={{0,8},{1,9},{2,10},{3,11},{4,12},{5,13},{6,14},{7,15}} | collective-permute-start | bytes 294920 | tf_op jit(solution)/shard_map/ppermute | solution.py:462
  23.6 1.8 %collective-permute-start.5 = (f32[5,64,128]{2,1,0:T(8,128)S(1)}, f32[5,64,128]{2,1,0:T(8,128)S(1)}, u32[]{:S(2)}, u32[]{:S(2)}) collective-permute-start(f32[5,64,128]{2,1,0:T(8,128)S(1)} %get-tuple-element.28), channel_id=1, source_target_pairs={{0,1},{1,0},{2,3},{3,2},{4,5},{5,4},{6,7},{7,6},{8,9},{9,8},{10,11... | collective-permute-start | bytes 491528 | tf_op jit(solution)/shard_map/ppermute | solution.py:470
where the time goes:
time: 26.4 us; the launch traced here: 26.1 us
  starting transfers between devices  9.28 us (35%)
  waiting for transfers between devices  9.23 us (35%)
  Pallas kernels  3.81 us (14%)
  blocking collectives  2.42 us (9%)
  other arithmetic  1.23 us (5%)
    ppermute x3, waiting for transfers between devices, local_window(): arrived = [lax.ppermute(rows, 'sec', [(0, target)]) for target in (1, 2, 3)]  7.24 us
    pallas_call x4, Pallas kernels, call(): pl.pallas_call(kernel, out_shape=outs, in_specs=[pl.BlockSpec(memory_spac...  3.81 us
    ppermute x1, starting transfers between devices, local_window(): lax.ppermute(jnp.where(is_first, top, bottom), ('gx', 'gz'), crossed_pairs)  3.77 us
    ppermute x3, starting transfers between devices, local_window(): arrived = [lax.ppermute(rows, 'sec', [(0, target)]) for target in (1, 2, 3)]  2.63 us
    all_gather x1, blocking collectives, local_window(): joined = lax.all_gather(other, 'gz')  2.42 us
    ppermute x1, starting transfers between devices, local_window(): lax.ppermute(jnp.where(is_first, bottom, top), ('gx', 'gz'), straight_pairs)  2.08 us
    concatenate x1, other arithmetic, local_window(): block = lax.optimization_barrier(jnp.concatenate([fields, media], axis=0))  1.11 us
    ppermute x1, waiting for transfers between devices, local_window(): swapped = lax.ppermute(sent, 'gz', turn)  1.03 us
  transfers between devices with their start and end apart: 6, of which 3 were waited for; matrix products, arithmetic and copies ran while one was open for 0% of the time, Pallas kernels for 2%

commit v1 on v0

--- a/solution.py
+++ b/solution.py
@@ -459,8 +459,7 @@
         [*bands, pick, block, ahead, behind, other],
         4_000_000_000,
     )
-    arrived = [lax.ppermute(rows, "sec", [(0, target)]) for target in (1, 2, 3)]
-    rows = arrived[0] + arrived[1] + arrived[2]
+    rows = lax.all_gather(rows, "sec")[0]
     held, sent = call(
         second_kernel,
         [full(5, HALF, CELLS), full(5, HALF, CELLS)],

time: 26.4 us -> 26.9 us (1.019)
  blocking collectives: 2.42 us -> 12.3 us
  waiting for transfers between devices: 9.23 us -> 2 us
  starting transfers between devices: 9.28 us -> 7.21 us
    all_gather x0 -> x1, blocking collectives: none -> 9.91 us  [local_window(): rows = lax.all_gather(rows, 'sec')[0]]
    ppermute x3 -> x0, waiting for transfers between devices: 7.24 us -> none  [local_window(): arrived = [lax.ppermute(rows, 'sec', [(0, target)]) for target in (1, 2, 3)]]
    ppermute x3 -> x0, starting transfers between devices: 2.63 us -> none  [local_window(): arrived = [lax.ppermute(rows, 'sec', [(0, target)]) for target in (1, 2, 3)]]
    ppermute x1, starting transfers between devices: 0.82 us -> 1.36 us  [local_window(): swapped = lax.ppermute(sent, 'gz', turn)]
  transfers between devices with their start and end apart: 6 -> 3, of which waited for: 3 -> 2; matrix products, arithmetic and copies ran while one was open for 0% -> 0% of each run, Pallas kernels for 2% -> 2%
where the time goes in v1:
time: 26.9 us; the launch traced here: 26.7 us
  blocking collectives  12.3 us (46%)
  starting transfers between devices  7.21 us (27%)
  Pallas kernels  3.81 us (14%)
  waiting for transfers between devices  2 us (7%)
  other arithmetic  1.22 us (5%)
    all_gather x1, blocking collectives, local_window(): rows = lax.all_gather(rows, 'sec')[0]  9.91 us
    pallas_call x4, Pallas kernels, call(): pl.pallas_call(kernel, out_shape=outs, in_specs=[pl.BlockSpec(memory_spac...  3.81 us
    ppermute x1, starting transfers between devices, local_window(): lax.ppermute(jnp.where(is_first, top, bottom), ('gx', 'gz'), crossed_pairs)  3.77 us
    all_gather x1, blocking collectives, local_window(): joined = lax.all_gather(other, 'gz')  2.42 us
    ppermute x1, starting transfers between devices, local_window(): lax.ppermute(jnp.where(is_first, bottom, top), ('gx', 'gz'), straight_pairs)  2.08 us
    ppermute x1, starting transfers between devices, local_window(): swapped = lax.ppermute(sent, 'gz', turn)  1.36 us
    concatenate x1, other arithmetic, local_window(): block = lax.optimization_barrier(jnp.concatenate([fields, media], axis=0))  1.11 us
    ppermute x1, waiting for transfers between devices, local_window(): swapped = lax.ppermute(sent, 'gz', turn)  1.03 us
  transfers between devices with their start and end apart: 3, of which 2 were waited for; matrix products, arithmetic and copies ran while one was open for 0% of the time, Pallas kernels for 2%

profile of v1, /device:TPU:19, one launch (start us, length us, event | category | flops | bytes accessed | tf_op | source)
XLA Modules:
  0.0 26.7 jit_solution(12434996751167830818)
XLA Ops:
  0.0 1.1 %pad_maximum_fusion.refs_5_ = f32[8,128,128]{2,1,0:T(8,128)S(1)} fusion(f32[3,128,128]{2,1,0:T(8,128)} %bitcast.8, f32[5,128,128]{2,1,0:T(8,128)} %bitcast.7), kind=kLoop, calls=%fused_computation | loop fusion | flops 131072 | bytes 1048576 | tf_op jit(solution)/shard_map/concatenate | solution.py:428
  1.2 3.8 %collective-permute-start.1 = (f32[8,40,128]{2,1,0:T(8,128)S(1)}, f32[8,40,128]{2,1,0:T(8,128)S(1)}, u32[]{:S(2)}, u32[]{:S(2)}) collective-permute-start(f32[8,40,128]{2,1,0:T(8,128)S(1)} %get-tuple-element.29), channel_id=1, source_target_pairs={{1,2},{3,4},{2,1},{5,6},{4,3},{6,5},{9,10},{11,12},{10,9},{13,14},... | collective-permute-start | bytes 491528 | tf_op jit(solution)/shard_map/ppermute | solution.py:440
  4.9 2.1 %collective-permute-start = (f32[8,40,128]{2,1,0:T(8,128)S(1)}, f32[8,40,128]{2,1,0:T(8,128)S(1)}, u32[]{:S(2)}, u32[]{:S(2)}) collective-permute-start(f32[8,40,128]{2,1,0:T(8,128)S(1)} %get-tuple-element.30), channel_id=1, source_target_pairs={{0,2},{2,4},{3,1},{4,6},{5,3},{7,5},{8,10},{10,12},{11,9},{12,14},... | collective-permute-start | bytes 491528 | tf_op jit(solution)/shard_map/ppermute | solution.py:439
  7.1 0.0 copy-start
  7.1 0.0 copy-start.1
  7.1 2.4 %all-gather = f32[16,104,128]{2,1,0:T(8,128)S(1)} all-gather(f32[8,104,128]{2,1,0:T(8,128)S(1)} %slice_select_fusion.1), channel_id=2, replica_groups=mesh['sec'=4,'gx'=4,'gz'=2] {'gz'}, dimensions={0}, use_global_device_ids=true | all-gather | bytes 1277952 | tf_op jit(solution)/shard_map/all_gather | solution.py:442
  9.5 0.0 copy-done
  9.6 0.0 copy-done.1
  9.6 0.4 %shard_map.46 = (bf16[144,288]{1,0:T(8,128)(2,1)S(1)}, bf16[112,224]{1,0:T(8,128)(2,1)S(1)}, bf16[80,160]{1,0:T(8,128)(2,1)S(1)}, bf16[512,256]{1,0:T(8,128)(2,1...) custom-call(s32[1,16]{1,0:T(1,128)S(1)} %bitcast.5, s32[1,3]{1,0:T(1,128)S(1)} %bitcast.6), custom_call_target="tpu_custom_call" | custom-call | flops 1000000000 | bytes 2097152 | tf_op jit(solution)/shard_map/pallas_call | solution.py:403
  10.0 0.0 collective-permute-done.1.refs_7_
  10.0 1.0 %collective-permute-done.refs_6_ = f32[8,40,128]{2,1,0:T(8,128)S(1)} collective-permute-done((f32[8,40,128]{2,1,0:T(8,128)S(1)}, f32[8,40,128]{2,1,0:T(8,128)S(1)}, u32[]{:S(2)}, u32[]{:S(2)}) %collective-permute-start) | collective-permute-done | bytes 163872 | tf_op jit(solution)/shard_map/ppermute | solution.py:439
  11.0 0.6 %shard_map.47 = (f32[5,64,128]{2,1,0:T(8,128)S(1)}, f32[5,64,128]{2,1,0:T(8,128)S(1)}, f32[192,128]{1,0:T(8,128)S(1)}, f32[9,144,256]{2,1,0:T(8,128)S(1)}) custom-call(bf16[144,288]{1,0:T(8,128)(2,1)S(1)} %get-tuple-element.17.refs_0_, bf16[112,224]{1,0:T(8,128)(2,1)S(1)} %get-tuple-element.18.refs_1_, bf16[80,160]{1,0:T(8,128)(2,1)S(1)} %get-tuple-element.19.refs_2_, ...), custom_call_target="tpu_custom_call" | custom-call | flops 4000000000 | bytes 2097152 | tf_op jit(solution)/shard_map/pallas_call | solution.py:403
  11.6 9.9 %all-gather.1 = f32[768,128]{1,0:T(8,128)S(1)} all-gather(f32[192,128]{1,0:T(8,128)S(1)} %get-tuple-element.24), channel_id=3, replica_groups=mesh['sec'=4,'gx'=4,'gz'=2] {'sec'}, dimensions={0}, use_global_device_ids=true | all-gather | bytes 491520 | tf_op jit(solution)/shard_map/all_gather | solution.py:462
  21.5 2.0 %shard_map.48 = (f32[5,64,128]{2,1,0:T(8,128)S(1)}, f32[5,64,128]{2,1,0:T(8,128)S(1)}) custom-call(bf16[144,288]{1,0:T(8,128)(2,1)S(1)} %get-tuple-element.17.refs_0_, bf16[112,224]{1,0:T(8,128)(2,1)S(1)} %get-tuple-element.18.refs_1_, bf16[80,160]{1,0:T(8,128)(2,1)S(1)} %get-tuple-element.19.refs_2_, bf16[512,256]{1,0:T(8,128)(2,1)S(1)} %get-tuple-element.20.refs_3_, ...), custom_call_target="tpu_custom_call" | custom-call | flops 4000000000 | bytes 2097152 | tf_op jit(solution)/shard_map/pallas_call | solution.py:403
  23.6 1.4 %collective-permute-start.2 = (f32[5,64,128]{2,1,0:T(8,128)S(1)}, f32[5,64,128]{2,1,0:T(8,128)S(1)}, u32[]{:S(2)}, u32[]{:S(2)}) collective-permute-start(f32[5,64,128]{2,1,0:T(8,128)S(1)} %get-tuple-element.28), channel_id=1, source_target_pairs={{0,1},{1,0},{2,3},{3,2},{4,5},{5,4},{6,7},{7,6},{8,9},{9,8},{10,11... | collective-permute-start | bytes 491528 | tf_op jit(solution)/shard_map/ppermute | solution.py:469
  24.9 1.0 %collective-permute-done.2.swapped = f32[5,64,128]{2,1,0:T(8,128)S(1)} collective-permute-done((f32[5,64,128]{2,1,0:T(8,128)S(1)}, f32[5,64,128]{2,1,0:T(8,128)S(1)}, u32[]{:S(2)}, u32[]{:S(2)}) %collective-permute-start.2) | collective-permute-done | bytes 163872 | tf_op jit(solution)/shard_map/ppermute | solution.py:469
  26.0 0.7 %shard_map.49 = f32[5,128,128]{2,1,0:T(8,128)} custom-call(f32[5,64,128]{2,1,0:T(8,128)S(1)} %get-tuple-element.27.held, f32[5,64,128]{2,1,0:T(8,128)S(1)} %collective-permute-done.2.swapped), custom_call_target="tpu_custom_call" | custom-call | flops 1000 | bytes 2097152 | tf_op jit(solution)/shard_map/pallas_call | solution.py:403
  (4 shorter events, 0.1 us)
Async XLA Ops:
  1.2 8.9 %collective-permute-start.1 = (f32[8,40,128]{2,1,0:T(8,128)S(1)}, f32[8,40,128]{2,1,0:T(8,128)S(1)}, u32[]{:S(2)}, u32[]{:S(2)}) collective-permute-start(f32[8,40,128]{2,1,0:T(8,128)S(1)} %get-tuple-element.29), channel_id=1, source_target_pairs={{1,2},{3,4},{2,1},{5,6},{4,3},{6,5},{9,10},{11,12},{10,9},{13,14},... | collective-permute-start | bytes 491528 | tf_op jit(solution)/shard_map/ppermute | solution.py:440
  4.9 6.1 %collective-permute-start = (f32[8,40,128]{2,1,0:T(8,128)S(1)}, f32[8,40,128]{2,1,0:T(8,128)S(1)}, u32[]{:S(2)}, u32[]{:S(2)}) collective-permute-start(f32[8,40,128]{2,1,0:T(8,128)S(1)} %get-tuple-element.30), channel_id=1, source_target_pairs={{0,2},{2,4},{3,1},{4,6},{5,3},{7,5},{8,10},{10,12},{11,9},{12,14},... | collective-permute-start | bytes 491528 | tf_op jit(solution)/shard_map/ppermute | solution.py:439
  7.1 2.5 %copy-start = (s32[16]{0:T(128)S(1)}, s32[16]{0:T(128)}, u32[]{:S(2)}) copy-start(s32[16]{0:T(128)} %param.6) | copy-start | bytes 196
  7.1 2.5 %copy-start.1 = (s32[3]{0:T(128)S(1)}, s32[3]{0:T(128)}, u32[]{:S(2)}) copy-start(s32[3]{0:T(128)} %param.7) | copy-start | bytes 40
  23.6 2.4 %collective-permute-start.2 = (f32[5,64,128]{2,1,0:T(8,128)S(1)}, f32[5,64,128]{2,1,0:T(8,128)S(1)}, u32[]{:S(2)}, u32[]{:S(2)}) collective-permute-start(f32[5,64,128]{2,1,0:T(8,128)S(1)} %get-tuple-element.28), channel_id=1, source_target_pairs={{0,1},{1,0},{2,3},{3,2},{4,5},{5,4},{6,7},{7,6},{8,9},{9,8},{10,11... | collective-permute-start | bytes 491528 | tf_op jit(solution)/shard_map/ppermute | solution.py:469

commit v2 on v0

--- a/solution.py
+++ b/solution.py
@@ -165,8 +165,8 @@
 DEPTH = 2 * CELLS
 PART = HALF + HALO
 NP = 2 * NPD
-TRIM = (0, 0, 16, 16, 32)
-WINDOWS = [WINDOW - 2 * amount for amount in sorted(set(TRIM))]
+TRIM = (0, 8, 16, 24, 32)
+WINDOWS = [WINDOW - 2 * amount for amount in TRIM]
 COUNTS = len(WINDOWS)
 ROWS = 192
 GROUPS = CELLS // NP
@@ -217,24 +217,78 @@
     return lax.broadcasted_iota(jnp.int32, shape, 1) // NP
 
 
+BODY = HALO - 8
+WHOLE = (2, 4)
+PAIRED = ((0, 1), (3, 5))
+EDGE_ROWS = 8 * BODY + 8 * len(WHOLE) + 8 * len(PAIRED)
+
+
+def pack_edge(block, target, at_end):
+    body, rest = (CELLS - BODY, CELLS - HALO) if at_end else (0, BODY)
+    near = lax.broadcasted_iota(jnp.int32, (8, CELLS), 0) // 4 == int(at_end)
+    for index in range(8):
+        target[BODY * index : BODY * (index + 1)] = block[index, body : body + BODY]
+    row = 8 * BODY
+    for index in WHOLE:
+        target[row : row + 8] = block[index, rest : rest + 8]
+        row += 8
+    for one, two in PAIRED:
+        turned = pltpu.roll(block[two, rest : rest + 8], 4, 0)
+        target[row : row + 8] = jnp.where(near, block[one, rest : rest + 8], turned)
+        row += 8
+
+
+def unpack_edge(edge, window, lanes, before):
+    body, rest = (8, 0) if before else (PART, WINDOW - 8)
+    near = lax.broadcasted_iota(jnp.int32, (8, CELLS), 0) // 4 == int(before)
+    for index in range(8):
+        window[index, body : body + BODY, lanes] = edge[BODY * index : BODY * (index + 1)]
+    row = 8 * BODY
+    for index in WHOLE:
+        window[index, rest : rest + 8, lanes] = edge[row : row + 8]
+        row += 8
+    for one, two in PAIRED:
+        tile = edge[row : row + 8]
+        window[one, rest : rest + 8, lanes] = jnp.where(near, tile, 0.0)
+        window[two, rest : rest + 8, lanes] = jnp.where(near, pltpu.roll(tile, 4, 0), 0.0)
+        row += 8
+    for index in (6, 7):
+        window[index, rest : rest + 8, lanes] = jnp.zeros((8, CELLS), jnp.float32)
+
+
+def pack_kernel(block, straight, crossed, swap):
+    core = lax.axis_index("gz")
+
+    @pl.when(core == 0)
+    def _():
+        pack_edge(block, straight, True)
+        pack_edge(block, crossed, False)
+        swap[...] = block[:, CELLS - PART :]
+
+    @pl.when(core == 1)
+    def _():
+        pack_edge(block, straight, False)
+        pack_edge(block, crossed, True)
+        swap[...] = block[:, :PART]
+
+
 def assemble(window, block, ahead, behind, other):
     core = lax.axis_index("gz")
+    low, high = slice(0, CELLS), slice(CELLS, DEPTH)
 
     @pl.when(core == 0)
     def _():
-        for index in range(8):
-            window[index, :HALO, :CELLS] = ahead[index]
-            window[index, :HALO, CELLS:] = behind[index]
-            window[index, HALO:, :CELLS] = block[index, :PART]
-            window[index, HALO:, CELLS:] = other[index]
+        unpack_edge(ahead, window, low, True)
+        unpack_edge(behind, window, high, True)
+        window[:8, HALO:, low] = block[:, :PART]
+        window[:8, HALO:, high] = other[...]
 
     @pl.when(core == 1)
     def _():
-        for index in range(8):
-            window[index, :PART, CELLS:] = block[index, CELLS - PART :]
-            window[index, :PART, :CELLS] = other[index]
-            window[index, PART:, CELLS:] = ahead[index]
-            window[index, PART:, :CELLS] = behind[index]
+        window[:8, :PART, high] = block[:, CELLS - PART :]
+        window[:8, :PART, low] = other[...]
+        unpack_edge(ahead, window, high, False)
+        unpack_edge(behind, window, low, False)
 
 
 def place(state, held, sent):
@@ -426,7 +480,12 @@
     core = lax.axis_index("gz")
     is_first = core == 0
     block = lax.optimization_barrier(jnp.concatenate([fields, media], axis=0))
-    top, bottom = block[:, :HALO], block[:, CELLS - HALO :]
+    straight, crossed, swap = call(
+        pack_kernel,
+        [full(EDGE_ROWS, CELLS), full(EDGE_ROWS, CELLS), full(8, PART, CELLS)],
+        [block],
+        1000,
+    )
     straight_pairs, crossed_pairs = [], []
     for column in range(columns):
         if column + 1 < columns:
@@ -436,10 +495,9 @@
             straight_pairs.append((2 * column + 1, 2 * column - 1))
             crossed_pairs.append((2 * column, 2 * column - 1))
     turn = [(0, 1), (1, 0)]
-    ahead = lax.ppermute(jnp.where(is_first, bottom, top), ("gx", "gz"), straight_pairs)
-    behind = lax.ppermute(jnp.where(is_first, top, bottom), ("gx", "gz"), crossed_pairs)
-    other = jnp.where(is_first, block[:, CELLS - PART :], block[:, :PART])
-    joined = lax.all_gather(other, "gz")
+    ahead = lax.ppermute(straight, ("gx", "gz"), straight_pairs)
+    behind = lax.ppermute(crossed, ("gx", "gz"), crossed_pairs)
+    joined = lax.all_gather(swap, "gz")
     other = jnp.where(is_first, joined[1], joined[0])
     *bands, pick, land = call(
         constants_kernel,

time: 26.4 us -> 26.8 us (1.015)
  waiting for transfers between devices: 9.23 us -> 8.11 us
  starting transfers between devices: 9.28 us -> 9.98 us
  blocking collectives: 2.42 us -> 3.07 us
    ppermute x1, starting transfers between devices: 0.82 us -> 2.29 us  [local_window(): swapped = lax.ppermute(sent, 'gz', turn)]
    ppermute x2, waiting for transfers between devices: 0.97 us -> 0.12 us  [the longest x1 0.12 us: local_window(): behind = lax.ppermute(crossed, ('gx', 'gz'), crossed_pairs)]
    ppermute x2, starting transfers between devices: 5.84 us -> 5.06 us  [the longest x1 2.98 us: local_window(): behind = lax.ppermute(crossed, ('gx', 'gz'), crossed_pairs)]
    all_gather x1, blocking collectives: 2.42 us -> 3.07 us  [local_window(): joined = lax.all_gather(swap, 'gz')]
    ppermute x3, waiting for transfers between devices: 7.24 us -> 6.96 us  [local_window(): arrived = [lax.ppermute(rows, 'sec', [(0, target)]) for target in (1, 2, 3)]]
    pallas_call x4 -> x5, Pallas kernels: 3.81 us -> 3.88 us  [call(): pl.pallas_call(kernel, out_shape=outs, in_specs=[pl.BlockSpec(memory_spac...]
where the time goes in v2:
time: 26.8 us; the launch traced here: 26.4 us
  starting transfers between devices  9.98 us (37%)
  waiting for transfers between devices  8.11 us (30%)
  Pallas kernels  3.88 us (14%)
  blocking collectives  3.07 us (11%)
  other arithmetic  1.18 us (4%)
    ppermute x3, waiting for transfers between devices, local_window(): arrived = [lax.ppermute(rows, 'sec', [(0, target)]) for target in (1, 2, 3)]  6.96 us
    pallas_call x5, Pallas kernels, call(): pl.pallas_call(kernel, out_shape=outs, in_specs=[pl.BlockSpec(memory_spac...  3.88 us
    all_gather x1, blocking collectives, local_window(): joined = lax.all_gather(swap, 'gz')  3.07 us
    ppermute x1, starting transfers between devices, local_window(): behind = lax.ppermute(crossed, ('gx', 'gz'), crossed_pairs)  2.98 us
    ppermute x3, starting transfers between devices, local_window(): arrived = [lax.ppermute(rows, 'sec', [(0, target)]) for target in (1, 2, 3)]  2.63 us
    ppermute x1, starting transfers between devices, local_window(): swapped = lax.ppermute(sent, 'gz', turn)  2.29 us
    ppermute x1, starting transfers between devices, local_window(): ahead = lax.ppermute(straight, ('gx', 'gz'), straight_pairs)  2.08 us
    concatenate x1, other arithmetic, local_window(): block = lax.optimization_barrier(jnp.concatenate([fields, media], axis=0))  1.11 us
  transfers between devices with their start and end apart: 6, of which 3 were waited for; matrix products, arithmetic and copies ran while one was open for 0% of the time, Pallas kernels for 2%

profile of v2, /device:TPU:19, one launch (start us, length us, event | category | flops | bytes accessed | tf_op | source)
XLA Modules:
  0.0 26.4 jit_solution(1450090807103595763)
XLA Ops:
  0.0 1.1 %pad_maximum_fusion.block.refs_7_ = f32[8,128,128]{2,1,0:T(8,128)S(1)} fusion(f32[3,128,128]{2,1,0:T(8,128)} %bitcast.8, f32[5,128,128]{2,1,0:T(8,128)} %bitcast.7), kind=kLoop, calls=%fused_computation | loop fusion | flops 131072 | bytes 1048576 | tf_op jit(solution)/shard_map/concatenate | solution.py:482
  1.1 0.1 shard_map.47
  1.2 0.0 copy-start
  1.2 0.0 copy-start.1
  1.2 2.1 %collective-permute-start = (f32[288,128]{1,0:T(8,128)S(1)}, f32[288,128]{1,0:T(8,128)S(1)}, u32[]{:S(2)}, u32[]{:S(2)}) collective-permute-start(f32[288,128]{1,0:T(8,128)S(1)} %get-tuple-element.30), channel_id=1, source_target_pairs={{0,2},{2,4},{3,1},{4,6},{5,3},{7,5},{8,10},{10,12},{11,9},{12,14},... | collective-permute-start | bytes 442376 | tf_op jit(solution)/shard_map/ppermute | solution.py:498
  3.3 3.0 %collective-permute-start.1 = (f32[288,128]{1,0:T(8,128)S(1)}, f32[288,128]{1,0:T(8,128)S(1)}, u32[]{:S(2)}, u32[]{:S(2)}) collective-permute-start(f32[288,128]{1,0:T(8,128)S(1)} %get-tuple-element.31), channel_id=1, source_target_pairs={{1,2},{3,4},{2,1},{5,6},{4,3},{6,5},{9,10},{11,12},{10,9},{13,14},... | collective-permute-start | bytes 442376 | tf_op jit(solution)/shard_map/ppermute | solution.py:499
  6.3 3.1 %all-gather = f32[16,104,128]{2,1,0:T(8,128)S(1)} all-gather(f32[8,104,128]{2,1,0:T(8,128)S(1)} %get-tuple-element.32), channel_id=2, replica_groups=mesh['sec'=4,'gx'=4,'gz'=2] {'gz'}, dimensions={0}, use_global_device_ids=true | all-gather | bytes 1277952 | tf_op jit(solution)/shard_map/all_gather | solution.py:500
  9.4 0.0 copy-done
  9.4 0.0 copy-done.1
  9.4 0.5 %shard_map.46 = (bf16[144,288]{1,0:T(8,128)(2,1)S(1)}, bf16[128,256]{1,0:T(8,128)(2,1)S(1)}, bf16[112,224]{1,0:T(8,128)(2,1)S(1)}, bf16[96,192]{1,0:T(8,128)(2,1...) custom-call(s32[1,16]{1,0:T(1,128)S(1)} %bitcast.5, ...), custom_call_target="tpu_custom_call" | custom-call | flops 1000000000 | bytes 2097152 | tf_op jit(solution)/shard_map/pallas_call | solution.py:457
  9.9 0.0 collective-permute-done.refs_8_
  9.9 0.1 collective-permute-done.1.refs_9_
  10.1 0.6 %shard_map.48 = (f32[5,64,128]{2,1,0:T(8,128)S(1)}, f32[5,64,128]{2,1,0:T(8,128)S(1)}, f32[192,128]{1,0:T(8,128)S(1)}, f32[9,144,256]{2,1,0:T(8,128)S(1)}) custom-call(bf16[144,288]{1,0:T(8,128)(2,1)S(1)} %get-tuple-element.22.refs_0_, bf16[128,256]{1,0:T(8,128)(2,1)S(1)} %get-tuple-element.23.refs_1_, bf16[112,224]{1,0:T(8,128)(2,1)S(1)} %get-tuple-element.24.refs_2_, ...), custom_call_target="tpu_custom_call" | custom-call | flops 4000000000 | bytes 2097152 | tf_op jit(solution)/shard_map/pallas_call | solution.py:457
  10.7 0.7 %collective-permute-start.4 = (f32[192,128]{1,0:T(8,128)S(1)}, f32[192,128]{1,0:T(8,128)S(1)}, u32[]{:S(2)}, u32[]{:S(2)}) collective-permute-start(f32[192,128]{1,0:T(8,128)S(1)} %get-tuple-element.34), channel_id=1, source_target_pairs={{0,24},{1,25},{2,26},{3,27},{4,28},{5,29},{6,30},{7,31}} | collective-permute-start | bytes 294920 | tf_op jit(solution)/shard_map/ppermute | solution.py:520
  11.4 0.7 %collective-permute-start.3 = (f32[192,128]{1,0:T(8,128)S(1)}, f32[192,128]{1,0:T(8,128)S(1)}, u32[]{:S(2)}, u32[]{:S(2)}) collective-permute-start(f32[192,128]{1,0:T(8,128)S(1)} %get-tuple-element.34), channel_id=1, source_target_pairs={{0,16},{1,17},{2,18},{3,19},{4,20},{5,21},{6,22},{7,23}} | collective-permute-start | bytes 294920 | tf_op jit(solution)/shard_map/ppermute | solution.py:520
  12.0 1.3 %collective-permute-start.2 = (f32[192,128]{1,0:T(8,128)S(1)}, f32[192,128]{1,0:T(8,128)S(1)}, u32[]{:S(2)}, u32[]{:S(2)}) collective-permute-start(f32[192,128]{1,0:T(8,128)S(1)} %get-tuple-element.34), channel_id=1, source_target_pairs={{0,8},{1,9},{2,10},{3,11},{4,12},{5,13},{6,14},{7,15}} | collective-permute-start | bytes 294920 | tf_op jit(solution)/shard_map/ppermute | solution.py:520
  13.3 0.0 collective-permute-done.4
  13.3 0.0 collective-permute-done.3
  13.4 7.0 %collective-permute-done.2 = f32[192,128]{1,0:T(8,128)S(1)} collective-permute-done((f32[192,128]{1,0:T(8,128)S(1)}, f32[192,128]{1,0:T(8,128)S(1)}, u32[]{:S(2)}, u32[]{:S(2)}) %collective-permute-start.2) | collective-permute-done | bytes 98336 | tf_op jit(solution)/shard_map/ppermute | solution.py:520
  20.3 2.0 %shard_map.49 = (f32[5,64,128]{2,1,0:T(8,128)S(1)}, f32[5,64,128]{2,1,0:T(8,128)S(1)}) custom-call(bf16[144,288]{1,0:T(8,128)(2,1)S(1)} %get-tuple-element.22.refs_0_, bf16[128,256]{1,0:T(8,128)(2,1)S(1)} %get-tuple-element.23.refs_1_, bf16[112,224]{1,0:T(8,128)(2,1)S(1)} %get-tuple-element.24.refs_2_, bf16[96,192]{1,0:T(8,128)(2,1)S(1)} %get-tuple-element.25.refs_3_, ...), custom_call_target="tpu_custom_call" | custom-call | flops 4000000000 | bytes 2097152 | tf_op jit(solution)/shard_map/pallas_call | solution.py:457
  22.3 2.3 %collective-permute-start.5 = (f32[5,64,128]{2,1,0:T(8,128)S(1)}, f32[5,64,128]{2,1,0:T(8,128)S(1)}, u32[]{:S(2)}, u32[]{:S(2)}) collective-permute-start(f32[5,64,128]{2,1,0:T(8,128)S(1)} %get-tuple-element.38), channel_id=1, source_target_pairs={{0,1},{1,0},{2,3},{3,2},{4,5},{5,4},{6,7},{7,6},{8,9},{9,8},{10,11... | collective-permute-start | bytes 491528 | tf_op jit(solution)/shard_map/ppermute | solution.py:528
  24.6 1.0 %collective-permute-done.5.swapped = f32[5,64,128]{2,1,0:T(8,128)S(1)} collective-permute-done((f32[5,64,128]{2,1,0:T(8,128)S(1)}, f32[5,64,128]{2,1,0:T(8,128)S(1)}, u32[]{:S(2)}, u32[]{:S(2)}) %collective-permute-start.5) | collective-permute-done | bytes 163872 | tf_op jit(solution)/shard_map/ppermute | solution.py:528
  25.6 0.7 %shard_map.50 = f32[5,128,128]{2,1,0:T(8,128)} custom-call(f32[5,64,128]{2,1,0:T(8,128)S(1)} %get-tuple-element.37.held, f32[5,64,128]{2,1,0:T(8,128)S(1)} %collective-permute-done.5.swapped), custom_call_target="tpu_custom_call" | custom-call | flops 1000 | bytes 2097152 | tf_op jit(solution)/shard_map/pallas_call | solution.py:457
  (2 shorter events, 0.1 us)
Async XLA Ops:
  1.2 8.2 %copy-start = (s32[16]{0:T(128)S(1)}, s32[16]{0:T(128)}, u32[]{:S(2)}) copy-start(s32[16]{0:T(128)} %param.6) | copy-start | bytes 196
  1.2 8.2 %copy-start.1 = (s32[3]{0:T(128)S(1)}, s32[3]{0:T(128)}, u32[]{:S(2)}) copy-start(s32[3]{0:T(128)} %param.7) | copy-start | bytes 40
  1.2 8.7 %collective-permute-start = (f32[288,128]{1,0:T(8,128)S(1)}, f32[288,128]{1,0:T(8,128)S(1)}, u32[]{:S(2)}, u32[]{:S(2)}) collective-permute-start(f32[288,128]{1,0:T(8,128)S(1)} %get-tuple-element.30), channel_id=1, source_target_pairs={{0,2},{2,4},{3,1},{4,6},{5,3},{7,5},{8,10},{10,12},{11,9},{12,14},... | collective-permute-start | bytes 442376 | tf_op jit(solution)/shard_map/ppermute | solution.py:498
  3.3 6.8 %collective-permute-start.1 = (f32[288,128]{1,0:T(8,128)S(1)}, f32[288,128]{1,0:T(8,128)S(1)}, u32[]{:S(2)}, u32[]{:S(2)}) collective-permute-start(f32[288,128]{1,0:T(8,128)S(1)} %get-tuple-element.31), channel_id=1, source_target_pairs={{1,2},{3,4},{2,1},{5,6},{4,3},{6,5},{9,10},{11,12},{10,9},{13,14},... | collective-permute-start | bytes 442376 | tf_op jit(solution)/shard_map/ppermute | solution.py:499
  10.7 2.7 %collective-permute-start.4 = (f32[192,128]{1,0:T(8,128)S(1)}, f32[192,128]{1,0:T(8,128)S(1)}, u32[]{:S(2)}, u32[]{:S(2)}) collective-permute-start(f32[192,128]{1,0:T(8,128)S(1)} %get-tuple-element.34), channel_id=1, source_target_pairs={{0,24},{1,25},{2,26},{3,27},{4,28},{5,29},{6,30},{7,31}} | collective-permute-start | bytes 294920 | tf_op jit(solution)/shard_map/ppermute | solution.py:520
  11.4 2.0 %collective-permute-start.3 = (f32[192,128]{1,0:T(8,128)S(1)}, f32[192,128]{1,0:T(8,128)S(1)}, u32[]{:S(2)}, u32[]{:S(2)}) collective-permute-start(f32[192,128]{1,0:T(8,128)S(1)} %get-tuple-element.34), channel_id=1, source_target_pairs={{0,16},{1,17},{2,18},{3,19},{4,20},{5,21},{6,22},{7,23}} | collective-permute-start | bytes 294920 | tf_op jit(solution)/shard_map/ppermute | solution.py:520
  12.0 8.3 %collective-permute-start.2 = (f32[192,128]{1,0:T(8,128)S(1)}, f32[192,128]{1,0:T(8,128)S(1)}, u32[]{:S(2)}, u32[]{:S(2)}) collective-permute-start(f32[192,128]{1,0:T(8,128)S(1)} %get-tuple-element.34), channel_id=1, source_target_pairs={{0,8},{1,9},{2,10},{3,11},{4,12},{5,13},{6,14},{7,15}} | collective-permute-start | bytes 294920 | tf_op jit(solution)/shard_map/ppermute | solution.py:520
  22.3 3.3 %collective-permute-start.5 = (f32[5,64,128]{2,1,0:T(8,128)S(1)}, f32[5,64,128]{2,1,0:T(8,128)S(1)}, u32[]{:S(2)}, u32[]{:S(2)}) collective-permute-start(f32[5,64,128]{2,1,0:T(8,128)S(1)} %get-tuple-element.38), channel_id=1, source_target_pairs={{0,1},{1,0},{2,3},{3,2},{4,5},{5,4},{6,7},{7,6},{8,9},{9,8},{10,11... | collective-permute-start | bytes 491528 | tf_op jit(solution)/shard_map/ppermute | solution.py:528

commit v3 on v2

--- a/solution.py
+++ b/solution.py
@@ -350,7 +350,7 @@
 
 
 def first_kernel(*refs):
-    bands_x, (band_z, pick, block, ahead, behind, other) = refs[:COUNTS], refs[COUNTS:-4]
+    bands_x, (band_z, pick, block, behind, ahead, other) = refs[:COUNTS], refs[COUNTS:-4]
     held, sent, rows, carry = refs[-4:]
     band_x = {band.shape[0]: band for band in bands_x}
     assemble(carry, block, ahead, behind, other)
@@ -495,8 +495,8 @@
             straight_pairs.append((2 * column + 1, 2 * column - 1))
             crossed_pairs.append((2 * column, 2 * column - 1))
     turn = [(0, 1), (1, 0)]
+    behind = lax.ppermute(crossed, ("gx", "gz"), crossed_pairs)
     ahead = lax.ppermute(straight, ("gx", "gz"), straight_pairs)
-    behind = lax.ppermute(crossed, ("gx", "gz"), crossed_pairs)
     joined = lax.all_gather(swap, "gz")
     other = jnp.where(is_first, joined[1], joined[0])
     *bands, pick, land = call(
@@ -514,7 +514,7 @@
             full(ROWS, CELLS),
             full(9, WINDOW, DEPTH),
         ],
-        [*bands, pick, block, ahead, behind, other],
+        [*bands, pick, block, behind, ahead, other],
         4_000_000_000,
     )
     arrived = [lax.ppermute(rows, "sec", [(0, target)]) for target in (1, 2, 3)]

time: 26.8 us -> 26.2 us (0.978)
  waiting for transfers between devices: 8.11 us -> 9.07 us
  starting transfers between devices: 9.98 us -> 9.28 us
  blocking collectives: 3.07 us -> 2.42 us
    ppermute x1, starting transfers between devices: 2.29 us -> 0.81 us  [local_window(): swapped = lax.ppermute(sent, 'gz', turn)]
    ppermute x1, waiting for transfers between devices: 0.01 us -> 0.8 us  [local_window(): ahead = lax.ppermute(straight, ('gx', 'gz'), straight_pairs)]
    ppermute x1, starting transfers between devices: 2.98 us -> 3.77 us  [local_window(): behind = lax.ppermute(crossed, ('gx', 'gz'), crossed_pairs)]
    all_gather x1, blocking collectives: 3.07 us -> 2.42 us  [local_window(): joined = lax.all_gather(swap, 'gz')]
    ppermute x3, waiting for transfers between devices: 6.96 us -> 7.24 us  [local_window(): arrived = [lax.ppermute(rows, 'sec', [(0, target)]) for target in (1, 2, 3)]]
where the time goes in v3:
time: 26.2 us; the launch traced here: 26 us
  starting transfers between devices  9.28 us (35%)
  waiting for transfers between devices  9.07 us (35%)
  Pallas kernels  3.88 us (15%)
  blocking collectives  2.42 us (9%)
  other arithmetic  1.18 us (5%)
    ppermute x3, waiting for transfers between devices, local_window(): arrived = [lax.ppermute(rows, 'sec', [(0, target)]) for target in (1, 2, 3)]  7.24 us
    pallas_call x5, Pallas kernels, call(): pl.pallas_call(kernel, out_shape=outs, in_specs=[pl.BlockSpec(memory_spac...  3.88 us
    ppermute x1, starting transfers between devices, local_window(): behind = lax.ppermute(crossed, ('gx', 'gz'), crossed_pairs)  3.77 us
    ppermute x3, starting transfers between devices, local_window(): arrived = [lax.ppermute(rows, 'sec', [(0, target)]) for target in (1, 2, 3)]  2.63 us
    all_gather x1, blocking collectives, local_window(): joined = lax.all_gather(swap, 'gz')  2.42 us
    ppermute x1, starting transfers between devices, local_window(): ahead = lax.ppermute(straight, ('gx', 'gz'), straight_pairs)  2.08 us
    concatenate x1, other arithmetic, local_window(): block = lax.optimization_barrier(jnp.concatenate([fields, media], axis=0))  1.11 us
    ppermute x1, waiting for transfers between devices, local_window(): swapped = lax.ppermute(sent, 'gz', turn)  1.03 us
  transfers between devices with their start and end apart: 6, of which 3 were waited for; matrix products, arithmetic and copies ran while one was open for 0% of the time, Pallas kernels for 2%

profile of v3, /device:TPU:19, one launch (start us, length us, event | category | flops | bytes accessed | tf_op | source)
XLA Modules:
  0.0 26.0 jit_solution(8884284331245267508)
XLA Ops:
  0.0 1.1 %pad_maximum_fusion.block.refs_7_ = f32[8,128,128]{2,1,0:T(8,128)S(1)} fusion(f32[3,128,128]{2,1,0:T(8,128)} %bitcast.8, f32[5,128,128]{2,1,0:T(8,128)} %bitcast.7), kind=kLoop, calls=%fused_computation | loop fusion | flops 131072 | bytes 1048576 | tf_op jit(solution)/shard_map/concatenate | solution.py:482
  1.1 0.1 shard_map.47
  1.2 0.0 copy-start
  1.2 0.0 copy-start.1
  1.2 3.8 %collective-permute-start = (f32[288,128]{1,0:T(8,128)S(1)}, f32[288,128]{1,0:T(8,128)S(1)}, u32[]{:S(2)}, u32[]{:S(2)}) collective-permute-start(f32[288,128]{1,0:T(8,128)S(1)} %get-tuple-element.30), channel_id=1, source_target_pairs={{1,2},{3,4},{2,1},{5,6},{4,3},{6,5},{9,10},{11,12},{10,9},{13,14},... | collective-permute-start | bytes 442376 | tf_op jit(solution)/shard_map/ppermute | solution.py:498
  5.0 2.1 %collective-permute-start.1 = (f32[288,128]{1,0:T(8,128)S(1)}, f32[288,128]{1,0:T(8,128)S(1)}, u32[]{:S(2)}, u32[]{:S(2)}) collective-permute-start(f32[288,128]{1,0:T(8,128)S(1)} %get-tuple-element.31), channel_id=1, source_target_pairs={{0,2},{2,4},{3,1},{4,6},{5,3},{7,5},{8,10},{10,12},{11,9},{12,14},... | collective-permute-start | bytes 442376 | tf_op jit(solution)/shard_map/ppermute | solution.py:499
  7.1 2.4 %all-gather = f32[16,104,128]{2,1,0:T(8,128)S(1)} all-gather(f32[8,104,128]{2,1,0:T(8,128)S(1)} %get-tuple-element.32), channel_id=2, replica_groups=mesh['sec'=4,'gx'=4,'gz'=2] {'gz'}, dimensions={0}, use_global_device_ids=true | all-gather | bytes 1277952 | tf_op jit(solution)/shard_map/all_gather | solution.py:500
  9.5 0.0 copy-done
  9.6 0.0 copy-done.1
  9.6 0.5 %shard_map.46 = (bf16[144,288]{1,0:T(8,128)(2,1)S(1)}, bf16[128,256]{1,0:T(8,128)(2,1)S(1)}, bf16[112,224]{1,0:T(8,128)(2,1)S(1)}, bf16[96,192]{1,0:T(8,128)(2,1...) custom-call(s32[1,16]{1,0:T(1,128)S(1)} %bitcast.5, ...), custom_call_target="tpu_custom_call" | custom-call | flops 1000000000 | bytes 2097152 | tf_op jit(solution)/shard_map/pallas_call | solution.py:457
  10.1 0.0 collective-permute-done.refs_8_
  10.1 0.8 %collective-permute-done.1.refs_9_ = f32[288,128]{1,0:T(8,128)S(1)} collective-permute-done((f32[288,128]{1,0:T(8,128)S(1)}, f32[288,128]{1,0:T(8,128)S(1)}, u32[]{:S(2)}, u32[]{:S(2)}) %collective-permute-start.1) | collective-permute-done | bytes 147488 | tf_op jit(solution)/shard_map/ppermute | solution.py:499
  10.9 0.6 %shard_map.48 = (f32[5,64,128]{2,1,0:T(8,128)S(1)}, f32[5,64,128]{2,1,0:T(8,128)S(1)}, f32[192,128]{1,0:T(8,128)S(1)}, f32[9,144,256]{2,1,0:T(8,128)S(1)}) custom-call(bf16[144,288]{1,0:T(8,128)(2,1)S(1)} %get-tuple-element.22.refs_0_, bf16[128,256]{1,0:T(8,128)(2,1)S(1)} %get-tuple-element.23.refs_1_, bf16[112,224]{1,0:T(8,128)(2,1)S(1)} %get-tuple-element.24.refs_2_, ...), custom_call_target="tpu_custom_call" | custom-call | flops 4000000000 | bytes 2097152 | tf_op jit(solution)/shard_map/pallas_call | solution.py:457
  11.5 0.7 %collective-permute-start.4 = (f32[192,128]{1,0:T(8,128)S(1)}, f32[192,128]{1,0:T(8,128)S(1)}, u32[]{:S(2)}, u32[]{:S(2)}) collective-permute-start(f32[192,128]{1,0:T(8,128)S(1)} %get-tuple-element.34), channel_id=1, source_target_pairs={{0,24},{1,25},{2,26},{3,27},{4,28},{5,29},{6,30},{7,31}} | collective-permute-start | bytes 294920 | tf_op jit(solution)/shard_map/ppermute | solution.py:520
  12.2 0.7 %collective-permute-start.3 = (f32[192,128]{1,0:T(8,128)S(1)}, f32[192,128]{1,0:T(8,128)S(1)}, u32[]{:S(2)}, u32[]{:S(2)}) collective-permute-start(f32[192,128]{1,0:T(8,128)S(1)} %get-tuple-element.34), channel_id=1, source_target_pairs={{0,16},{1,17},{2,18},{3,19},{4,20},{5,21},{6,22},{7,23}} | collective-permute-start | bytes 294920 | tf_op jit(solution)/shard_map/ppermute | solution.py:520
  12.9 1.3 %collective-permute-start.2 = (f32[192,128]{1,0:T(8,128)S(1)}, f32[192,128]{1,0:T(8,128)S(1)}, u32[]{:S(2)}, u32[]{:S(2)}) collective-permute-start(f32[192,128]{1,0:T(8,128)S(1)} %get-tuple-element.34), channel_id=1, source_target_pairs={{0,8},{1,9},{2,10},{3,11},{4,12},{5,13},{6,14},{7,15}} | collective-permute-start | bytes 294920 | tf_op jit(solution)/shard_map/ppermute | solution.py:520
  14.2 0.0 collective-permute-done.4
  14.2 0.0 collective-permute-done.3
  14.2 7.2 %collective-permute-done.2 = f32[192,128]{1,0:T(8,128)S(1)} collective-permute-done((f32[192,128]{1,0:T(8,128)S(1)}, f32[192,128]{1,0:T(8,128)S(1)}, u32[]{:S(2)}, u32[]{:S(2)}) %collective-permute-start.2) | collective-permute-done | bytes 98336 | tf_op jit(solution)/shard_map/ppermute | solution.py:520
  21.4 2.0 %shard_map.49 = (f32[5,64,128]{2,1,0:T(8,128)S(1)}, f32[5,64,128]{2,1,0:T(8,128)S(1)}) custom-call(bf16[144,288]{1,0:T(8,128)(2,1)S(1)} %get-tuple-element.22.refs_0_, bf16[128,256]{1,0:T(8,128)(2,1)S(1)} %get-tuple-element.23.refs_1_, bf16[112,224]{1,0:T(8,128)(2,1)S(1)} %get-tuple-element.24.refs_2_, bf16[96,192]{1,0:T(8,128)(2,1)S(1)} %get-tuple-element.25.refs_3_, ...), custom_call_target="tpu_custom_call" | custom-call | flops 4000000000 | bytes 2097152 | tf_op jit(solution)/shard_map/pallas_call | solution.py:457
  23.4 0.8 %collective-permute-start.5 = (f32[5,64,128]{2,1,0:T(8,128)S(1)}, f32[5,64,128]{2,1,0:T(8,128)S(1)}, u32[]{:S(2)}, u32[]{:S(2)}) collective-permute-start(f32[5,64,128]{2,1,0:T(8,128)S(1)} %get-tuple-element.38), channel_id=1, source_target_pairs={{0,1},{1,0},{2,3},{3,2},{4,5},{5,4},{6,7},{7,6},{8,9},{9,8},{10,11... | collective-permute-start | bytes 491528 | tf_op jit(solution)/shard_map/ppermute | solution.py:528
  24.2 1.0 %collective-permute-done.5.swapped = f32[5,64,128]{2,1,0:T(8,128)S(1)} collective-permute-done((f32[5,64,128]{2,1,0:T(8,128)S(1)}, f32[5,64,128]{2,1,0:T(8,128)S(1)}, u32[]{:S(2)}, u32[]{:S(2)}) %collective-permute-start.5) | collective-permute-done | bytes 163872 | tf_op jit(solution)/shard_map/ppermute | solution.py:528
  25.2 0.7 %shard_map.50 = f32[5,128,128]{2,1,0:T(8,128)} custom-call(f32[5,64,128]{2,1,0:T(8,128)S(1)} %get-tuple-element.37.held, f32[5,64,128]{2,1,0:T(8,128)S(1)} %collective-permute-done.5.swapped), custom_call_target="tpu_custom_call" | custom-call | flops 1000 | bytes 2097152 | tf_op jit(solution)/shard_map/pallas_call | solution.py:457
  (2 shorter events, 0.1 us)
Async XLA Ops:
  1.2 8.4 %copy-start = (s32[16]{0:T(128)S(1)}, s32[16]{0:T(128)}, u32[]{:S(2)}) copy-start(s32[16]{0:T(128)} %param.6) | copy-start | bytes 196
  1.2 8.4 %copy-start.1 = (s32[3]{0:T(128)S(1)}, s32[3]{0:T(128)}, u32[]{:S(2)}) copy-start(s32[3]{0:T(128)} %param.7) | copy-start | bytes 40
  1.2 8.9 %collective-permute-start = (f32[288,128]{1,0:T(8,128)S(1)}, f32[288,128]{1,0:T(8,128)S(1)}, u32[]{:S(2)}, u32[]{:S(2)}) collective-permute-start(f32[288,128]{1,0:T(8,128)S(1)} %get-tuple-element.30), channel_id=1, source_target_pairs={{1,2},{3,4},{2,1},{5,6},{4,3},{6,5},{9,10},{11,12},{10,9},{13,14},... | collective-permute-start | bytes 442376 | tf_op jit(solution)/shard_map/ppermute | solution.py:498
  5.0 5.9 %collective-permute-start.1 = (f32[288,128]{1,0:T(8,128)S(1)}, f32[288,128]{1,0:T(8,128)S(1)}, u32[]{:S(2)}, u32[]{:S(2)}) collective-permute-start(f32[288,128]{1,0:T(8,128)S(1)} %get-tuple-element.31), channel_id=1, source_target_pairs={{0,2},{2,4},{3,1},{4,6},{5,3},{7,5},{8,10},{10,12},{11,9},{12,14},... | collective-permute-start | bytes 442376 | tf_op jit(solution)/shard_map/ppermute | solution.py:499
  11.5 2.7 %collective-permute-start.4 = (f32[192,128]{1,0:T(8,128)S(1)}, f32[192,128]{1,0:T(8,128)S(1)}, u32[]{:S(2)}, u32[]{:S(2)}) collective-permute-start(f32[192,128]{1,0:T(8,128)S(1)} %get-tuple-element.34), channel_id=1, source_target_pairs={{0,24},{1,25},{2,26},{3,27},{4,28},{5,29},{6,30},{7,31}} | collective-permute-start | bytes 294920 | tf_op jit(solution)/shard_map/ppermute | solution.py:520
  12.2 2.0 %collective-permute-start.3 = (f32[192,128]{1,0:T(8,128)S(1)}, f32[192,128]{1,0:T(8,128)S(1)}, u32[]{:S(2)}, u32[]{:S(2)}) collective-permute-start(f32[192,128]{1,0:T(8,128)S(1)} %get-tuple-element.34), channel_id=1, source_target_pairs={{0,16},{1,17},{2,18},{3,19},{4,20},{5,21},{6,22},{7,23}} | collective-permute-start | bytes 294920 | tf_op jit(solution)/shard_map/ppermute | solution.py:520
  12.9 8.6 %collective-permute-start.2 = (f32[192,128]{1,0:T(8,128)S(1)}, f32[192,128]{1,0:T(8,128)S(1)}, u32[]{:S(2)}, u32[]{:S(2)}) collective-permute-start(f32[192,128]{1,0:T(8,128)S(1)} %get-tuple-element.34), channel_id=1, source_target_pairs={{0,8},{1,9},{2,10},{3,11},{4,12},{5,13},{6,14},{7,15}} | collective-permute-start | bytes 294920 | tf_op jit(solution)/shard_map/ppermute | solution.py:520
  23.4 1.8 %collective-permute-start.5 = (f32[5,64,128]{2,1,0:T(8,128)S(1)}, f32[5,64,128]{2,1,0:T(8,128)S(1)}, u32[]{:S(2)}, u32[]{:S(2)}) collective-permute-start(f32[5,64,128]{2,1,0:T(8,128)S(1)} %get-tuple-element.38), channel_id=1, source_target_pairs={{0,1},{1,0},{2,3},{3,2},{4,5},{5,4},{6,7},{7,6},{8,9},{9,8},{10,11... | collective-permute-start | bytes 491528 | tf_op jit(solution)/shard_map/ppermute | solution.py:528

commit v4 on v3

--- a/solution.py
+++ b/solution.py
@@ -223,8 +223,9 @@
 EDGE_ROWS = 8 * BODY + 8 * len(WHOLE) + 8 * len(PAIRED)
 
 
-def pack_edge(block, target, at_end):
+def pack_edge(block, first, target, at_end):
     body, rest = (CELLS - BODY, CELLS - HALO) if at_end else (0, BODY)
+    body, rest = body - first, rest - first
     near = lax.broadcasted_iota(jnp.int32, (8, CELLS), 0) // 4 == int(at_end)
     for index in range(8):
         target[BODY * index : BODY * (index + 1)] = block[index, body : body + BODY]
@@ -238,14 +239,16 @@
         row += 8
 
 
-def unpack_edge(edge, window, lanes, before):
+def unpack_edge(edge, window, lanes, before, inside):
     body, rest = (8, 0) if before else (PART, WINDOW - 8)
     near = lax.broadcasted_iota(jnp.int32, (8, CELLS), 0) // 4 == int(before)
+    near = near & inside
     for index in range(8):
-        window[index, body : body + BODY, lanes] = edge[BODY * index : BODY * (index + 1)]
+        taken = edge[BODY * index : BODY * (index + 1)]
+        window[index, body : body + BODY, lanes] = jnp.where(inside, taken, 0.0)
     row = 8 * BODY
     for index in WHOLE:
-        window[index, rest : rest + 8, lanes] = edge[row : row + 8]
+        window[index, rest : rest + 8, lanes] = jnp.where(inside, edge[row : row + 8], 0.0)
         row += 8
     for one, two in PAIRED:
         tile = edge[row : row + 8]
@@ -256,39 +259,39 @@
         window[index, rest : rest + 8, lanes] = jnp.zeros((8, CELLS), jnp.float32)
 
 
-def pack_kernel(block, straight, crossed, swap):
+def pack_kernel(block, joined, edge):
     core = lax.axis_index("gz")
 
     @pl.when(core == 0)
     def _():
-        pack_edge(block, straight, True)
-        pack_edge(block, crossed, False)
-        swap[...] = block[:, CELLS - PART :]
+        pack_edge(block, 0, edge.at[0], False)
+        pack_edge(joined.at[1], 0, edge.at[1], False)
 
     @pl.when(core == 1)
     def _():
-        pack_edge(block, straight, False)
-        pack_edge(block, crossed, True)
-        swap[...] = block[:, :PART]
-
-
-def assemble(window, block, ahead, behind, other):
-    core = lax.axis_index("gz")
+        pack_edge(joined.at[0], CELLS - PART, edge.at[0], True)
+        pack_edge(block, 0, edge.at[1], True)
+
+
+def assemble(window, block, joined, edges):
+    core, column = lax.axis_index("gz"), lax.axis_index("gx")
     low, high = slice(0, CELLS), slice(CELLS, DEPTH)
 
     @pl.when(core == 0)
     def _():
-        unpack_edge(ahead, window, low, True)
-        unpack_edge(behind, window, high, True)
+        inside = column > 0
+        unpack_edge(edges.at[0, 0], window, low, True, inside)
+        unpack_edge(edges.at[0, 1], window, high, True, inside)
         window[:8, HALO:, low] = block[:, :PART]
-        window[:8, HALO:, high] = other[...]
+        window[:8, HALO:, high] = joined[1]
 
     @pl.when(core == 1)
     def _():
+        inside = column < lax.axis_size("gx") - 1
         window[:8, :PART, high] = block[:, CELLS - PART :]
-        window[:8, :PART, low] = other[...]
-        unpack_edge(ahead, window, high, False)
-        unpack_edge(behind, window, low, False)
+        window[:8, :PART, low] = joined[0]
+        unpack_edge(edges.at[1, 0], window, low, False, inside)
+        unpack_edge(edges.at[1, 1], window, high, False, inside)
 
 
 def place(state, held, sent):
@@ -350,10 +353,10 @@
 
 
 def first_kernel(*refs):
-    bands_x, (band_z, pick, block, behind, ahead, other) = refs[:COUNTS], refs[COUNTS:-4]
+    bands_x, (band_z, pick, block, joined, edges) = refs[:COUNTS], refs[COUNTS:-4]
     held, sent, rows, carry = refs[-4:]
     band_x = {band.shape[0]: band for band in bands_x}
-    assemble(carry, block, ahead, behind, other)
+    assemble(carry, block, joined, edges)
     section = lax.axis_index("sec")
 
     @pl.when(section == 0)
@@ -475,30 +478,31 @@
     return jax.ShapeDtypeStruct(shape, jnp.bfloat16)
 
 
+def pairs(columns):
+    def device(section, column, core):
+        return (section * columns + column) * 2 + core
+
+    groups = [
+        [device(section, column, 1), device(section, column + 1, 0)]
+        for section in range(4)
+        for column in range(columns - 1)
+    ]
+    for section in (0, 2):
+        for column, core in ((0, 0), (columns - 1, 1)):
+            groups.append([device(section, column, core), device(section + 1, column, core)])
+    return groups
+
+
 def local_window(columns, fields, media, plane_rows, box_offset):
     fields, media = fields[0], media[0]
     core = lax.axis_index("gz")
     is_first = core == 0
     block = lax.optimization_barrier(jnp.concatenate([fields, media], axis=0))
-    straight, crossed, swap = call(
-        pack_kernel,
-        [full(EDGE_ROWS, CELLS), full(EDGE_ROWS, CELLS), full(8, PART, CELLS)],
-        [block],
-        1000,
-    )
-    straight_pairs, crossed_pairs = [], []
-    for column in range(columns):
-        if column + 1 < columns:
-            straight_pairs.append((2 * column, 2 * column + 2))
-            crossed_pairs.append((2 * column + 1, 2 * column + 2))
-        if column:
-            straight_pairs.append((2 * column + 1, 2 * column - 1))
-            crossed_pairs.append((2 * column, 2 * column - 1))
+    swap = jnp.where(is_first, block[:, CELLS - PART :], block[:, :PART])
+    joined = lax.all_gather(swap, "gz")
+    (edge,) = call(pack_kernel, [full(2, EDGE_ROWS, CELLS)], [block, joined], 1000)
+    edges = lax.all_gather(edge, ("sec", "gx", "gz"), axis_index_groups=pairs(columns))
     turn = [(0, 1), (1, 0)]
-    behind = lax.ppermute(crossed, ("gx", "gz"), crossed_pairs)
-    ahead = lax.ppermute(straight, ("gx", "gz"), straight_pairs)
-    joined = lax.all_gather(swap, "gz")
-    other = jnp.where(is_first, joined[1], joined[0])
     *bands, pick, land = call(
         constants_kernel,
         [narrow(count, 2 * count) for count in WINDOWS]
@@ -514,7 +518,7 @@
             full(ROWS, CELLS),
             full(9, WINDOW, DEPTH),
         ],
-        [*bands, pick, block, behind, ahead, other],
+        [*bands, pick, block, joined, edges],
         4_000_000_000,
     )
     arrived = [lax.ppermute(rows, "sec", [(0, target)]) for target in (1, 2, 3)]

time: 26.2 us -> 26.9 us (1.027)
  the two profiles are of different devices: /device:TPU:19 before, /device:TPU:5 now
where the time goes in v4:
time: 26.9 us; the launch traced here: 26.7 us
  blocking collectives  9.84 us (37%)
  waiting for transfers between devices  7.26 us (27%)
  starting transfers between devices  4.47 us (17%)
  Pallas kernels  3.89 us (14%)
  other arithmetic  1.17 us (4%)
    all_gather x1, blocking collectives, local_window(): lax.all_gather(edge, ('sec', 'gx', 'gz'), axis_index_groups=pairs(columns))  7.12 us
    ppermute x3, waiting for transfers between devices, local_window(): arrived = [lax.ppermute(rows, 'sec', [(0, target)]) for target in (1, 2, 3)]  6.23 us
    pallas_call x5, Pallas kernels, call(): pl.pallas_call(kernel, out_shape=outs, in_specs=[pl.BlockSpec(memory_spac...  3.89 us
    all_gather x1, blocking collectives, local_window(): joined = lax.all_gather(swap, 'gz')  2.72 us
    ppermute x3, starting transfers between devices, local_window(): arrived = [lax.ppermute(rows, 'sec', [(0, target)]) for target in (1, 2, 3)]  2.63 us
    ppermute x1, starting transfers between devices, local_window(): swapped = lax.ppermute(sent, 'gz', turn)  1.85 us
    concatenate x1, other arithmetic, local_window(): block = lax.optimization_barrier(jnp.concatenate([fields, media], axis=0))  1.11 us
    ppermute x1, waiting for transfers between devices, local_window(): swapped = lax.ppermute(sent, 'gz', turn)  1.03 us
  transfers between devices with their start and end apart: 4, of which 2 were waited for; matrix products, arithmetic and copies ran while one was open for 0% of the time, Pallas kernels for 0%

profile of v4, /device:TPU:5, one launch (start us, length us, event | category | flops | bytes accessed | tf_op | source)
XLA Modules:
  0.0 26.7 jit_solution(723575760703789561)
XLA Ops:
  0.0 1.1 %pad_maximum_fusion.block.refs_7_ = f32[8,128,128]{2,1,0:T(8,128)S(1)} fusion(f32[3,128,128]{2,1,0:T(8,128)} %bitcast.13, f32[5,128,128]{2,1,0:T(8,128)} %bitcast.12), kind=kLoop, calls=%fused_computation | loop fusion | flops 131072 | bytes 1048576 | tf_op jit(solution)/shard_map/concatenate | solution.py:500
  1.2 2.7 %all-gather = f32[16,104,128]{2,1,0:T(8,128)S(1)} all-gather(f32[8,104,128]{2,1,0:T(8,128)S(1)} %slice_select_fusion), channel_id=2, replica_groups=mesh['sec'=4,'gx'=4,'gz'=2] {'gz'}, dimensions={0}, use_global_device_ids=true | all-gather | bytes 1277952 | tf_op jit(solution)/shard_map/all_gather | solution.py:502
  3.9 0.0 copy-start
  3.9 0.0 copy-start.1
  3.9 7.1 %all-gather.1 = f32[4,288,128]{2,1,0:T(8,128)S(1)} all-gather(f32[2,288,128]{2,1,0:T(8,128)S(1)} %shard_map.47), channel_id=3, replica_groups={{1,2},{3,4},{5,6},{9,10},{11,12},{13,14},{17,18},{19,20},{21,22},{25,26..., dimensions={0}, use_global_device_ids=true | all-gather | bytes 884736 | tf_op jit(solution)/shard_map/all_gather | solution.py:504
  11.0 0.0 copy-done
  11.0 0.0 copy-done.1
  11.0 0.5 %shard_map.46 = (bf16[144,288]{1,0:T(8,128)(2,1)S(1)}, bf16[128,256]{1,0:T(8,128)(2,1)S(1)}, bf16[112,224]{1,0:T(8,128)(2,1)S(1)}, bf16[96,192]{1,0:T(8,128)(2,1...) custom-call(s32[1,16]{1,0:T(1,128)S(1)} %bitcast.10, ...), custom_call_target="tpu_custom_call" | custom-call | flops 1000000000 | bytes 2097152 | tf_op jit(solution)/shard_map/pallas_call | solution.py:460
  11.5 0.6 %shard_map.48 = (f32[5,64,128]{2,1,0:T(8,128)S(1)}, f32[5,64,128]{2,1,0:T(8,128)S(1)}, f32[192,128]{1,0:T(8,128)S(1)}, f32[9,144,256]{2,1,0:T(8,128)S(1)}) custom-call(bf16[144,288]{1,0:T(8,128)(2,1)S(1)} %get-tuple-element.19.refs_0_, bf16[128,256]{1,0:T(8,128)(2,1)S(1)} %get-tuple-element.20.refs_1_, bf16[112,224]{1,0:T(8,128)(2,1)S(1)} %get-tuple-element.21.refs_2_, ...), custom_call_target="tpu_custom_call" | custom-call | flops 4000000000 | bytes 2097152 | tf_op jit(solution)/shard_map/pallas_call | solution.py:460
  12.2 0.7 %collective-permute-start.2 = (f32[192,128]{1,0:T(8,128)S(1)}, f32[192,128]{1,0:T(8,128)S(1)}, u32[]{:S(2)}, u32[]{:S(2)}) collective-permute-start(f32[192,128]{1,0:T(8,128)S(1)} %get-tuple-element.28), channel_id=1, source_target_pairs={{0,24},{1,25},{2,26},{3,27},{4,28},{5,29},{6,30},{7,31}} | collective-permute-start | bytes 294920 | tf_op jit(solution)/shard_map/ppermute | solution.py:524
  12.9 0.7 %collective-permute-start = (f32[192,128]{1,0:T(8,128)S(1)}, f32[192,128]{1,0:T(8,128)S(1)}, u32[]{:S(2)}, u32[]{:S(2)}) collective-permute-start(f32[192,128]{1,0:T(8,128)S(1)} %get-tuple-element.28), channel_id=1, source_target_pairs={{0,8},{1,9},{2,10},{3,11},{4,12},{5,13},{6,14},{7,15}} | collective-permute-start | bytes 294920 | tf_op jit(solution)/shard_map/ppermute | solution.py:524
  13.5 1.3 %collective-permute-start.1 = (f32[192,128]{1,0:T(8,128)S(1)}, f32[192,128]{1,0:T(8,128)S(1)}, u32[]{:S(2)}, u32[]{:S(2)}) collective-permute-start(f32[192,128]{1,0:T(8,128)S(1)} %get-tuple-element.28), channel_id=1, source_target_pairs={{0,16},{1,17},{2,18},{3,19},{4,20},{5,21},{6,22},{7,23}} | collective-permute-start | bytes 294920 | tf_op jit(solution)/shard_map/ppermute | solution.py:524
  14.8 0.0 collective-permute-done.2
  14.9 0.0 collective-permute-done
  14.9 6.2 %collective-permute-done.1 = f32[192,128]{1,0:T(8,128)S(1)} collective-permute-done((f32[192,128]{1,0:T(8,128)S(1)}, f32[192,128]{1,0:T(8,128)S(1)}, u32[]{:S(2)}, u32[]{:S(2)}) %collective-permute-start.1) | collective-permute-done | bytes 98336 | tf_op jit(solution)/shard_map/ppermute | solution.py:524
  21.1 2.0 %shard_map.49 = (f32[5,64,128]{2,1,0:T(8,128)S(1)}, f32[5,64,128]{2,1,0:T(8,128)S(1)}) custom-call(bf16[144,288]{1,0:T(8,128)(2,1)S(1)} %get-tuple-element.19.refs_0_, bf16[128,256]{1,0:T(8,128)(2,1)S(1)} %get-tuple-element.20.refs_1_, bf16[112,224]{1,0:T(8,128)(2,1)S(1)} %get-tuple-element.21.refs_2_, bf16[96,192]{1,0:T(8,128)(2,1)S(1)} %get-tuple-element.22.refs_3_, ...), custom_call_target="tpu_custom_call" | custom-call | flops 4000000000 | bytes 2097152 | tf_op jit(solution)/shard_map/pallas_call | solution.py:460
  23.1 1.8 %collective-permute-start.3 = (f32[5,64,128]{2,1,0:T(8,128)S(1)}, f32[5,64,128]{2,1,0:T(8,128)S(1)}, u32[]{:S(2)}, u32[]{:S(2)}) collective-permute-start(f32[5,64,128]{2,1,0:T(8,128)S(1)} %get-tuple-element.32), channel_id=1, source_target_pairs={{0,1},{1,0},{2,3},{3,2},{4,5},{5,4},{6,7},{7,6},{8,9},{9,8},{10,11... | collective-permute-start | bytes 491528 | tf_op jit(solution)/shard_map/ppermute | solution.py:532
  25.0 1.0 %collective-permute-done.3.swapped = f32[5,64,128]{2,1,0:T(8,128)S(1)} collective-permute-done((f32[5,64,128]{2,1,0:T(8,128)S(1)}, f32[5,64,128]{2,1,0:T(8,128)S(1)}, u32[]{:S(2)}, u32[]{:S(2)}) %collective-permute-start.3) | collective-permute-done | bytes 163872 | tf_op jit(solution)/shard_map/ppermute | solution.py:532
  26.0 0.7 %shard_map.50 = f32[5,128,128]{2,1,0:T(8,128)} custom-call(f32[5,64,128]{2,1,0:T(8,128)S(1)} %get-tuple-element.31.held, f32[5,64,128]{2,1,0:T(8,128)S(1)} %collective-permute-done.3.swapped), custom_call_target="tpu_custom_call" | custom-call | flops 1000 | bytes 2097152 | tf_op jit(solution)/shard_map/pallas_call | solution.py:460
  (3 shorter events, 0.1 us)
Async XLA Ops:
  3.9 7.2 %copy-start = (s32[16]{0:T(128)S(1)}, s32[16]{0:T(128)}, u32[]{:S(2)}) copy-start(s32[16]{0:T(128)} %param.6) | copy-start | bytes 196
  3.9 7.2 %copy-start.1 = (s32[3]{0:T(128)S(1)}, s32[3]{0:T(128)}, u32[]{:S(2)}) copy-start(s32[3]{0:T(128)} %param.7) | copy-start | bytes 40
  12.2 2.7 %collective-permute-start.2 = (f32[192,128]{1,0:T(8,128)S(1)}, f32[192,128]{1,0:T(8,128)S(1)}, u32[]{:S(2)}, u32[]{:S(2)}) collective-permute-start(f32[192,128]{1,0:T(8,128)S(1)} %get-tuple-element.28), channel_id=1, source_target_pairs={{0,24},{1,25},{2,26},{3,27},{4,28},{5,29},{6,30},{7,31}} | collective-permute-start | bytes 294920 | tf_op jit(solution)/shard_map/ppermute | solution.py:524
  12.9 2.0 %collective-permute-start = (f32[192,128]{1,0:T(8,128)S(1)}, f32[192,128]{1,0:T(8,128)S(1)}, u32[]{:S(2)}, u32[]{:S(2)}) collective-permute-start(f32[192,128]{1,0:T(8,128)S(1)} %get-tuple-element.28), channel_id=1, source_target_pairs={{0,8},{1,9},{2,10},{3,11},{4,12},{5,13},{6,14},{7,15}} | collective-permute-start | bytes 294920 | tf_op jit(solution)/shard_map/ppermute | solution.py:524
  13.5 7.5 %collective-permute-start.1 = (f32[192,128]{1,0:T(8,128)S(1)}, f32[192,128]{1,0:T(8,128)S(1)}, u32[]{:S(2)}, u32[]{:S(2)}) collective-permute-start(f32[192,128]{1,0:T(8,128)S(1)} %get-tuple-element.28), channel_id=1, source_target_pairs={{0,16},{1,17},{2,18},{3,19},{4,20},{5,21},{6,22},{7,23}} | collective-permute-start | bytes 294920 | tf_op jit(solution)/shard_map/ppermute | solution.py:524
  23.1 2.9 %collective-permute-start.3 = (f32[5,64,128]{2,1,0:T(8,128)S(1)}, f32[5,64,128]{2,1,0:T(8,128)S(1)}, u32[]{:S(2)}, u32[]{:S(2)}) collective-permute-start(f32[5,64,128]{2,1,0:T(8,128)S(1)} %get-tuple-element.32), channel_id=1, source_target_pairs={{0,1},{1,0},{2,3},{3,2},{4,5},{5,4},{6,7},{7,6},{8,9},{9,8},{10,11... | collective-permute-start | bytes 491528 | tf_op jit(solution)/shard_map/ppermute | solution.py:532

commit v5 on v3

--- a/solution.py
+++ b/solution.py
@@ -517,8 +517,8 @@
         [*bands, pick, block, behind, ahead, other],
         4_000_000_000,
     )
-    arrived = [lax.ppermute(rows, "sec", [(0, target)]) for target in (1, 2, 3)]
-    rows = arrived[0] + arrived[1] + arrived[2]
+    for groups in ([[0, 1], [2, 3]], [[0, 2], [1, 3]]):
+        rows = lax.all_gather(rows, "sec", axis_index_groups=groups)[0]
     held, sent = call(
         second_kernel,
         [full(5, HALF, CELLS), full(5, HALF, CELLS)],

time: 26.2 us -> 28.2 us (1.076)
  the two profiles are of different devices: /device:TPU:19 before, /device:TPU:0 now
where the time goes in v5:
time: 28.2 us; the launch traced here: 28 us
  blocking collectives  14.2 us (50%)
  starting transfers between devices  6.93 us (25%)
  Pallas kernels  4.23 us (15%)
  waiting for transfers between devices  1.39 us (5%)
  other arithmetic  1.16 us (4%)
    all_gather x2, blocking collectives, local_window(): rows = lax.all_gather(rows, 'sec', axis_index_groups=groups)[0]  11.8 us
    ppermute x1, starting transfers between devices, local_window(): ahead = lax.ppermute(straight, ('gx', 'gz'), straight_pairs)  6.19 us
    pallas_call x5, Pallas kernels, call(): pl.pallas_call(kernel, out_shape=outs, in_specs=[pl.BlockSpec(memory_spac...  4.23 us
    all_gather x1, blocking collectives, local_window(): joined = lax.all_gather(swap, 'gz')  2.42 us
    ppermute x1, waiting for transfers between devices, local_window(): swapped = lax.ppermute(sent, 'gz', turn)  1.38 us
    concatenate x1, other arithmetic, local_window(): block = lax.optimization_barrier(jnp.concatenate([fields, media], axis=0))  1.11 us
    ppermute x1, starting transfers between devices, local_window(): behind = lax.ppermute(crossed, ('gx', 'gz'), crossed_pairs)  0.67 us
  transfers between devices with their start and end apart: 3, of which 1 were waited for; matrix products, arithmetic and copies ran while one was open for 0% of the time, Pallas kernels for 2%

profile of v5, /device:TPU:0, one launch (start us, length us, event | category | flops | bytes accessed | tf_op | source)
XLA Modules:
  0.0 28.0 jit_solution(15265334710472965645)
XLA Ops:
  0.0 1.1 %pad_maximum_fusion.block.refs_7_ = f32[8,128,128]{2,1,0:T(8,128)S(1)} fusion(f32[3,128,128]{2,1,0:T(8,128)} %bitcast.8, f32[5,128,128]{2,1,0:T(8,128)} %bitcast.7), kind=kLoop, calls=%fused_computation | loop fusion | flops 131072 | bytes 1048576 | tf_op jit(solution)/shard_map/concatenate | solution.py:482
  1.1 0.1 shard_map.47
  1.2 0.0 copy-start
  1.2 0.0 copy-start.1
  1.2 0.7 %collective-permute-start = (f32[288,128]{1,0:T(8,128)S(1)}, f32[288,128]{1,0:T(8,128)S(1)}, u32[]{:S(2)}, u32[]{:S(2)}) collective-permute-start(f32[288,128]{1,0:T(8,128)S(1)} %get-tuple-element.30), channel_id=1, source_target_pairs={{1,2},{3,4},{2,1},{5,6},{4,3},{6,5},{9,10},{11,12},{10,9},{13,14},... | collective-permute-start | bytes 442376 | tf_op jit(solution)/shard_map/ppermute | solution.py:498
  1.9 6.2 %collective-permute-start.1 = (f32[288,128]{1,0:T(8,128)S(1)}, f32[288,128]{1,0:T(8,128)S(1)}, u32[]{:S(2)}, u32[]{:S(2)}) collective-permute-start(f32[288,128]{1,0:T(8,128)S(1)} %get-tuple-element.31), channel_id=1, source_target_pairs={{0,2},{2,4},{3,1},{4,6},{5,3},{7,5},{8,10},{10,12},{11,9},{12,14},... | collective-permute-start | bytes 442376 | tf_op jit(solution)/shard_map/ppermute | solution.py:499
  8.1 2.4 %all-gather = f32[16,104,128]{2,1,0:T(8,128)S(1)} all-gather(f32[8,104,128]{2,1,0:T(8,128)S(1)} %get-tuple-element.32), channel_id=2, replica_groups=mesh['sec'=4,'gx'=4,'gz'=2] {'gz'}, dimensions={0}, use_global_device_ids=true | all-gather | bytes 1277952 | tf_op jit(solution)/shard_map/all_gather | solution.py:500
  10.6 0.0 copy-done
  10.6 0.0 copy-done.1
  10.6 0.5 %shard_map.46 = (bf16[144,288]{1,0:T(8,128)(2,1)S(1)}, bf16[128,256]{1,0:T(8,128)(2,1)S(1)}, bf16[112,224]{1,0:T(8,128)(2,1)S(1)}, bf16[96,192]{1,0:T(8,128)(2,1...) custom-call(s32[1,16]{1,0:T(1,128)S(1)} %bitcast.5, ...), custom_call_target="tpu_custom_call" | custom-call | flops 1000000000 | bytes 2097152 | tf_op jit(solution)/shard_map/pallas_call | solution.py:457
  11.1 0.0 collective-permute-done.refs_8_
  11.1 0.0 collective-permute-done.1.refs_9_
  11.1 2.9 %shard_map.48 = (f32[5,64,128]{2,1,0:T(8,128)S(1)}, f32[5,64,128]{2,1,0:T(8,128)S(1)}, f32[192,128]{1,0:T(8,128)S(1)}, f32[9,144,256]{2,1,0:T(8,128)S(1)}) custom-call(bf16[144,288]{1,0:T(8,128)(2,1)S(1)} %get-tuple-element.22.refs_0_, bf16[128,256]{1,0:T(8,128)(2,1)S(1)} %get-tuple-element.23.refs_1_, bf16[112,224]{1,0:T(8,128)(2,1)S(1)} %get-tuple-element.24.refs_2_, ...), custom_call_target="tpu_custom_call" | custom-call | flops 4000000000 | bytes 2097152 | tf_op jit(solution)/shard_map/pallas_call | solution.py:457
  14.0 6.3 %all-gather.1 = f32[384,128]{1,0:T(8,128)S(1)} all-gather(f32[192,128]{1,0:T(8,128)S(1)} %get-tuple-element.34), channel_id=3, replica_groups={{0,8},{16,24},{1,9},{17,25},{2,10},{18,26},{3,11},{19,27},{4,12},{20,28..., dimensions={0}, use_global_device_ids=true | all-gather | bytes 294912 | tf_op jit(solution)/shard_map/all_gather | solution.py:521
  20.3 5.5 %all-gather.2 = f32[384,128]{1,0:T(8,128)S(1)} all-gather(f32[192,128]{1,0:T(8,128)S(1)} %slice.22), channel_id=4, replica_groups={{0,16},{8,24},{1,17},{9,25},{2,18},{10,26},{3,19},{11,27},{4,20},{12,28..., dimensions={0}, use_global_device_ids=true | all-gather | bytes 294912 | tf_op jit(solution)/shard_map/all_gather | solution.py:521
  25.8 0.1 collective-permute-start.2
  25.9 1.4 %collective-permute-done.2.swapped = f32[5,64,128]{2,1,0:T(8,128)S(1)} collective-permute-done((f32[5,64,128]{2,1,0:T(8,128)S(1)}, f32[5,64,128]{2,1,0:T(8,128)S(1)}, u32[]{:S(2)}, u32[]{:S(2)}) %collective-permute-start.2) | collective-permute-done | bytes 163872 | tf_op jit(solution)/shard_map/ppermute | solution.py:528
  27.3 0.7 %shard_map.50 = f32[5,128,128]{2,1,0:T(8,128)} custom-call(f32[5,64,128]{2,1,0:T(8,128)S(1)} %get-tuple-element.37.held, f32[5,64,128]{2,1,0:T(8,128)S(1)} %collective-permute-done.2.swapped), custom_call_target="tpu_custom_call" | custom-call | flops 1000 | bytes 2097152 | tf_op jit(solution)/shard_map/pallas_call | solution.py:457
  (4 shorter events, 0.1 us)
Async XLA Ops:
  1.2 9.4 %copy-start = (s32[16]{0:T(128)S(1)}, s32[16]{0:T(128)}, u32[]{:S(2)}) copy-start(s32[16]{0:T(128)} %param.6) | copy-start | bytes 196
  1.2 9.4 %copy-start.1 = (s32[3]{0:T(128)S(1)}, s32[3]{0:T(128)}, u32[]{:S(2)}) copy-start(s32[3]{0:T(128)} %param.7) | copy-start | bytes 40
  1.2 9.9 %collective-permute-start = (f32[288,128]{1,0:T(8,128)S(1)}, f32[288,128]{1,0:T(8,128)S(1)}, u32[]{:S(2)}, u32[]{:S(2)}) collective-permute-start(f32[288,128]{1,0:T(8,128)S(1)} %get-tuple-element.30), channel_id=1, source_target_pairs={{1,2},{3,4},{2,1},{5,6},{4,3},{6,5},{9,10},{11,12},{10,9},{13,14},... | collective-permute-start | bytes 442376 | tf_op jit(solution)/shard_map/ppermute | solution.py:498
  1.9 9.2 %collective-permute-start.1 = (f32[288,128]{1,0:T(8,128)S(1)}, f32[288,128]{1,0:T(8,128)S(1)}, u32[]{:S(2)}, u32[]{:S(2)}) collective-permute-start(f32[288,128]{1,0:T(8,128)S(1)} %get-tuple-element.31), channel_id=1, source_target_pairs={{0,2},{2,4},{3,1},{4,6},{5,3},{7,5},{8,10},{10,12},{11,9},{12,14},... | collective-permute-start | bytes 442376 | tf_op jit(solution)/shard_map/ppermute | solution.py:499
  25.8 1.5 %collective-permute-start.2 = (f32[5,64,128]{2,1,0:T(8,128)S(1)}, f32[5,64,128]{2,1,0:T(8,128)S(1)}, u32[]{:S(2)}, u32[]{:S(2)}) collective-permute-start(f32[5,64,128]{2,1,0:T(8,128)S(1)} %get-tuple-element.38), channel_id=1, source_target_pairs={{0,1},{1,0},{2,3},{3,2},{4,5},{5,4},{6,7},{7,6},{8,9},{9,8},{10,11... | collective-permute-start | bytes 491528 | tf_op jit(solution)/shard_map/ppermute | solution.py:528

commit v6 on v3

--- a/solution.py
+++ b/solution.py
@@ -207,6 +207,13 @@
     return dot(jnp.concatenate(parts, axis=1), matrix[...])
 
 
+def pair_along_depth(matrix, one, two):
+    fields = [jnp.concatenate(parts, axis=1) for parts in (one, two)]
+    both = dot(jnp.concatenate(fields, axis=0), matrix[...])
+    count = one[0].shape[0]
+    return both[:count], both[count:]
+
+
 def trimmed(arrays, amount):
     if amount == 0:
         return arrays
@@ -256,8 +263,16 @@
         window[index, rest : rest + 8, lanes] = jnp.zeros((8, CELLS), jnp.float32)
 
 
-def pack_kernel(block, straight, crossed, swap):
+def pack_kernel(fields, media, block, straight, crossed, swap, sems):
     core = lax.axis_index("gz")
+    copies = [
+        pltpu.make_async_copy(fields, block.at[:5], sems.at[0]),
+        pltpu.make_async_copy(media, block.at[5:], sems.at[1]),
+    ]
+    for copy in copies:
+        copy.start()
+    for copy in copies:
+        copy.wait()
 
     @pl.when(core == 0)
     def _():
@@ -371,18 +386,22 @@
                 [vx, vz, sxx, szz, sxz, light, both, lame, shear], cut
             )
             parts_xx, parts_zz, parts_xz = halves(sxx), halves(szz), halves(sxz)
-            vx = vx + light * (diff_x(band_x, parts_xx) + along_depth(band_z, parts_xz))
-            vz = vz + light * (diff_x(band_x, parts_xz) + along_depth(band_z, parts_zz))
+            slope_xz, slope_zz = pair_along_depth(band_z, parts_xz, parts_zz)
+            vx = vx + light * (diff_x(band_x, parts_xx) + slope_xz)
+            vz = vz + light * (diff_x(band_x, parts_xz) + slope_zz)
             parts_x, parts_z = halves(vx), halves(vz)
-            strain_x, strain_z = diff_x(band_x, parts_x), along_depth(band_z, parts_z)
+            slope_x, strain_z = pair_along_depth(band_z, parts_x, parts_z)
+            strain_x = diff_x(band_x, parts_x)
             sxx = sxx + (both * strain_x + lame * strain_z)
             szz = szz + (lame * strain_x + both * strain_z)
-            sxz = sxz + shear * (along_depth(band_z, parts_x) + diff_x(band_x, parts_z))
+            sxz = sxz + shear * (slope_x + diff_x(band_x, parts_z))
+            rows_x, rows_z = pair_along_depth(pick, parts_x, parts_z)
+            stress = along_depth(pick, halves(sxx + szz))
             low = 2 * RADIUS * (step + 1) - at
-            for component, (parts, factor) in enumerate(
-                ((parts_x, COUPLING), (parts_z, COUPLING), (halves(sxx + szz), -0.5 * COUPLING))
+            for component, (picked, factor) in enumerate(
+                ((rows_x, COUPLING), (rows_z, COUPLING), (stress, -0.5 * COUPLING))
             ):
-                picked = factor * along_depth(pick, parts)
+                picked = factor * picked
                 picked = picked[low : picked.shape[0] - low]
                 group, base = SLOT[step][component]
                 spot = pl.ds(base, picked.shape[0])
@@ -453,11 +472,19 @@
         copy.wait()
 
 
-def call(kernel, outs, operands, flops, place_out=pltpu.VMEM, scratch=()):
+def call(
+    kernel,
+    outs,
+    operands,
+    flops,
+    place_in=pltpu.VMEM,
+    place_out=pltpu.VMEM,
+    scratch=(),
+):
     return pl.pallas_call(
         kernel,
         out_shape=outs,
-        in_specs=[pl.BlockSpec(memory_space=pltpu.VMEM)] * len(operands),
+        in_specs=[pl.BlockSpec(memory_space=place_in)] * len(operands),
         out_specs=[pl.BlockSpec(memory_space=place_out)] * len(outs),
         scratch_shapes=scratch,
         compiler_params=pltpu.CompilerParams(vmem_limit_bytes=48 * 1024 * 1024),
@@ -479,12 +506,18 @@
     fields, media = fields[0], media[0]
     core = lax.axis_index("gz")
     is_first = core == 0
-    block = lax.optimization_barrier(jnp.concatenate([fields, media], axis=0))
-    straight, crossed, swap = call(
+    block, straight, crossed, swap = call(
         pack_kernel,
-        [full(EDGE_ROWS, CELLS), full(EDGE_ROWS, CELLS), full(8, PART, CELLS)],
-        [block],
+        [
+            full(8, CELLS, CELLS),
+            full(EDGE_ROWS, CELLS),
+            full(EDGE_ROWS, CELLS),
+            full(8, PART, CELLS),
+        ],
+        [pltpu.with_memory_space_constraint(array, pltpu.HBM) for array in (fields, media)],
         1000,
+        place_in=pltpu.HBM,
+        scratch=[pltpu.SemaphoreType.DMA((2,))],
     )
     straight_pairs, crossed_pairs = [], []
     for column in range(columns):
@@ -531,8 +564,8 @@
         [full(5, CELLS, CELLS)],
         [held, swapped],
         1000,
-        pl.ANY,
-        [pltpu.SemaphoreType.DMA((2,))],
+        place_out=pl.ANY,
+        scratch=[pltpu.SemaphoreType.DMA((2,))],
     )
     return out[None]
 

time: 26.2 us -> 26.1 us (level)
  other arithmetic: 1.18 us -> 0.07 us
  Pallas kernels: 3.88 us -> 4.93 us
    concatenate x1 -> x0, other arithmetic: 1.11 us -> none  [local_window(): block = lax.optimization_barrier(jnp.concatenate([fields, media], axis=0))]
    pallas_call x5, Pallas kernels: 3.88 us -> 4.93 us  [call(): pl.pallas_call(kernel, out_shape=outs, in_specs=[pl.BlockSpec(memory_spac...]
where the time goes in v6:
time: 26.1 us; the launch traced here: 25.9 us
  starting transfers between devices  9.28 us (36%)
  waiting for transfers between devices  9.07 us (35%)
  Pallas kernels  4.93 us (19%)
  blocking collectives  2.42 us (9%)
    ppermute x3, waiting for transfers between devices, local_window(): arrived = [lax.ppermute(rows, 'sec', [(0, target)]) for target in (1, 2, 3)]  7.24 us
    pallas_call x5, Pallas kernels, call(): pl.pallas_call(kernel, out_shape=outs, in_specs=[pl.BlockSpec(memory_spac...  4.93 us
    ppermute x1, starting transfers between devices, local_window(): behind = lax.ppermute(crossed, ('gx', 'gz'), crossed_pairs)  3.77 us
    ppermute x3, starting transfers between devices, local_window(): arrived = [lax.ppermute(rows, 'sec', [(0, target)]) for target in (1, 2, 3)]  2.63 us
    all_gather x1, blocking collectives, local_window(): joined = lax.all_gather(swap, 'gz')  2.42 us
    ppermute x1, starting transfers between devices, local_window(): ahead = lax.ppermute(straight, ('gx', 'gz'), straight_pairs)  2.08 us
    ppermute x1, waiting for transfers between devices, local_window(): swapped = lax.ppermute(sent, 'gz', turn)  1.03 us
    ppermute x1, starting transfers between devices, local_window(): swapped = lax.ppermute(sent, 'gz', turn)  0.81 us
  transfers between devices with their start and end apart: 6, of which 3 were waited for; matrix products, arithmetic and copies ran while one was open for 0% of the time, Pallas kernels for 2%

profile of v6, /device:TPU:19, one launch (start us, length us, event | category | flops | bytes accessed | tf_op | source)
XLA Modules:
  0.0 25.9 jit_solution(9571743560630312935)
XLA Ops:
  0.0 1.1 %shard_map.47 = (f32[8,128,128]{2,1,0:T(8,128)S(1)}, f32[288,128]{1,0:T(8,128)S(1)}, f32[288,128]{1,0:T(8,128)S(1)}, f32[8,104,128]{2,1,0:T(8,128)S(1)}) custom-call(f32[5,128,128]{2,1,0:T(8,128)} %bitcast.7, f32[3,128,128]{2,1,0:T(8,128)} %bitcast.8), custom_call_target="tpu_custom_call" | custom-call | flops 1000 | bytes 2097152 | tf_op jit(solution)/shard_map/pallas_call | solution.py:484
  1.1 0.0 copy-start
  1.1 0.0 copy-start.1
  1.1 3.8 %collective-permute-start = (f32[288,128]{1,0:T(8,128)S(1)}, f32[288,128]{1,0:T(8,128)S(1)}, u32[]{:S(2)}, u32[]{:S(2)}) collective-permute-start(f32[288,128]{1,0:T(8,128)S(1)} %get-tuple-element.32), channel_id=1, source_target_pairs={{1,2},{3,4},{2,1},{5,6},{4,3},{6,5},{9,10},{11,12},{10,9},{13,14},... | collective-permute-start | bytes 442376 | tf_op jit(solution)/shard_map/ppermute | solution.py:531
  4.9 2.1 %collective-permute-start.1 = (f32[288,128]{1,0:T(8,128)S(1)}, f32[288,128]{1,0:T(8,128)S(1)}, u32[]{:S(2)}, u32[]{:S(2)}) collective-permute-start(f32[288,128]{1,0:T(8,128)S(1)} %get-tuple-element.33), channel_id=1, source_target_pairs={{0,2},{2,4},{3,1},{4,6},{5,3},{7,5},{8,10},{10,12},{11,9},{12,14},... | collective-permute-start | bytes 442376 | tf_op jit(solution)/shard_map/ppermute | solution.py:532
  7.0 2.4 %all-gather = f32[16,104,128]{2,1,0:T(8,128)S(1)} all-gather(f32[8,104,128]{2,1,0:T(8,128)S(1)} %get-tuple-element.34), channel_id=2, replica_groups=mesh['sec'=4,'gx'=4,'gz'=2] {'gz'}, dimensions={0}, use_global_device_ids=true | all-gather | bytes 1277952 | tf_op jit(solution)/shard_map/all_gather | solution.py:533
  9.5 0.0 copy-done
  9.5 0.0 copy-done.1
  9.5 0.5 %shard_map.46 = (bf16[144,288]{1,0:T(8,128)(2,1)S(1)}, bf16[128,256]{1,0:T(8,128)(2,1)S(1)}, bf16[112,224]{1,0:T(8,128)(2,1)S(1)}, bf16[96,192]{1,0:T(8,128)(2,1...) custom-call(s32[1,16]{1,0:T(1,128)S(1)} %bitcast.5, ...), custom_call_target="tpu_custom_call" | custom-call | flops 1000000000 | bytes 2097152 | tf_op jit(solution)/shard_map/pallas_call | solution.py:484
  10.0 0.0 collective-permute-done.refs_8_
  10.0 0.8 %collective-permute-done.1.refs_9_ = f32[288,128]{1,0:T(8,128)S(1)} collective-permute-done((f32[288,128]{1,0:T(8,128)S(1)}, f32[288,128]{1,0:T(8,128)S(1)}, u32[]{:S(2)}, u32[]{:S(2)}) %collective-permute-start.1) | collective-permute-done | bytes 147488 | tf_op jit(solution)/shard_map/ppermute | solution.py:532
  10.8 0.6 %shard_map.48 = (f32[5,64,128]{2,1,0:T(8,128)S(1)}, f32[5,64,128]{2,1,0:T(8,128)S(1)}, f32[192,128]{1,0:T(8,128)S(1)}, f32[9,144,256]{2,1,0:T(8,128)S(1)}) custom-call(bf16[144,288]{1,0:T(8,128)(2,1)S(1)} %get-tuple-element.23.refs_0_, bf16[128,256]{1,0:T(8,128)(2,1)S(1)} %get-tuple-element.24.refs_1_, bf16[112,224]{1,0:T(8,128)(2,1)S(1)} %get-tuple-element.25.refs_2_, ...), custom_call_target="tpu_custom_call" | custom-call | flops 4000000000 | bytes 2097152 | tf_op jit(solution)/shard_map/pallas_call | solution.py:484
  11.4 0.7 %collective-permute-start.4 = (f32[192,128]{1,0:T(8,128)S(1)}, f32[192,128]{1,0:T(8,128)S(1)}, u32[]{:S(2)}, u32[]{:S(2)}) collective-permute-start(f32[192,128]{1,0:T(8,128)S(1)} %get-tuple-element.36), channel_id=1, source_target_pairs={{0,24},{1,25},{2,26},{3,27},{4,28},{5,29},{6,30},{7,31}} | collective-permute-start | bytes 294920 | tf_op jit(solution)/shard_map/ppermute | solution.py:553
  12.1 0.7 %collective-permute-start.3 = (f32[192,128]{1,0:T(8,128)S(1)}, f32[192,128]{1,0:T(8,128)S(1)}, u32[]{:S(2)}, u32[]{:S(2)}) collective-permute-start(f32[192,128]{1,0:T(8,128)S(1)} %get-tuple-element.36), channel_id=1, source_target_pairs={{0,16},{1,17},{2,18},{3,19},{4,20},{5,21},{6,22},{7,23}} | collective-permute-start | bytes 294920 | tf_op jit(solution)/shard_map/ppermute | solution.py:553
  12.8 1.3 %collective-permute-start.2 = (f32[192,128]{1,0:T(8,128)S(1)}, f32[192,128]{1,0:T(8,128)S(1)}, u32[]{:S(2)}, u32[]{:S(2)}) collective-permute-start(f32[192,128]{1,0:T(8,128)S(1)} %get-tuple-element.36), channel_id=1, source_target_pairs={{0,8},{1,9},{2,10},{3,11},{4,12},{5,13},{6,14},{7,15}} | collective-permute-start | bytes 294920 | tf_op jit(solution)/shard_map/ppermute | solution.py:553
  14.1 0.0 collective-permute-done.4
  14.1 0.0 collective-permute-done.3
  14.1 7.2 %collective-permute-done.2 = f32[192,128]{1,0:T(8,128)S(1)} collective-permute-done((f32[192,128]{1,0:T(8,128)S(1)}, f32[192,128]{1,0:T(8,128)S(1)}, u32[]{:S(2)}, u32[]{:S(2)}) %collective-permute-start.2) | collective-permute-done | bytes 98336 | tf_op jit(solution)/shard_map/ppermute | solution.py:553
  21.3 2.0 %shard_map.49 = (f32[5,64,128]{2,1,0:T(8,128)S(1)}, f32[5,64,128]{2,1,0:T(8,128)S(1)}) custom-call(bf16[144,288]{1,0:T(8,128)(2,1)S(1)} %get-tuple-element.23.refs_0_, bf16[128,256]{1,0:T(8,128)(2,1)S(1)} %get-tuple-element.24.refs_1_, bf16[112,224]{1,0:T(8,128)(2,1)S(1)} %get-tuple-element.25.refs_2_, bf16[96,192]{1,0:T(8,128)(2,1)S(1)} %get-tuple-element.26.refs_3_, ...), custom_call_target="tpu_custom_call" | custom-call | flops 4000000000 | bytes 2097152 | tf_op jit(solution)/shard_map/pallas_call | solution.py:484
  23.3 0.8 %collective-permute-start.5 = (f32[5,64,128]{2,1,0:T(8,128)S(1)}, f32[5,64,128]{2,1,0:T(8,128)S(1)}, u32[]{:S(2)}, u32[]{:S(2)}) collective-permute-start(f32[5,64,128]{2,1,0:T(8,128)S(1)} %get-tuple-element.40), channel_id=1, source_target_pairs={{0,1},{1,0},{2,3},{3,2},{4,5},{5,4},{6,7},{7,6},{8,9},{9,8},{10,11... | collective-permute-start | bytes 491528 | tf_op jit(solution)/shard_map/ppermute | solution.py:561
  24.1 1.0 %collective-permute-done.5.swapped = f32[5,64,128]{2,1,0:T(8,128)S(1)} collective-permute-done((f32[5,64,128]{2,1,0:T(8,128)S(1)}, f32[5,64,128]{2,1,0:T(8,128)S(1)}, u32[]{:S(2)}, u32[]{:S(2)}) %collective-permute-start.5) | collective-permute-done | bytes 163872 | tf_op jit(solution)/shard_map/ppermute | solution.py:561
  25.2 0.7 %shard_map.50 = f32[5,128,128]{2,1,0:T(8,128)} custom-call(f32[5,64,128]{2,1,0:T(8,128)S(1)} %get-tuple-element.39.held, f32[5,64,128]{2,1,0:T(8,128)S(1)} %collective-permute-done.5.swapped), custom_call_target="tpu_custom_call" | custom-call | flops 1000 | bytes 2097152 | tf_op jit(solution)/shard_map/pallas_call | solution.py:484
  (2 shorter events, 0.1 us)
Async XLA Ops:
  1.1 8.4 %copy-start = (s32[16]{0:T(128)S(1)}, s32[16]{0:T(128)}, u32[]{:S(2)}) copy-start(s32[16]{0:T(128)} %param.6) | copy-start | bytes 196
  1.1 8.4 %copy-start.1 = (s32[3]{0:T(128)S(1)}, s32[3]{0:T(128)}, u32[]{:S(2)}) copy-start(s32[3]{0:T(128)} %param.7) | copy-start | bytes 40
  1.1 8.9 %collective-permute-start = (f32[288,128]{1,0:T(8,128)S(1)}, f32[288,128]{1,0:T(8,128)S(1)}, u32[]{:S(2)}, u32[]{:S(2)}) collective-permute-start(f32[288,128]{1,0:T(8,128)S(1)} %get-tuple-element.32), channel_id=1, source_target_pairs={{1,2},{3,4},{2,1},{5,6},{4,3},{6,5},{9,10},{11,12},{10,9},{13,14},... | collective-permute-start | bytes 442376 | tf_op jit(solution)/shard_map/ppermute | solution.py:531
  4.9 5.9 %collective-permute-start.1 = (f32[288,128]{1,0:T(8,128)S(1)}, f32[288,128]{1,0:T(8,128)S(1)}, u32[]{:S(2)}, u32[]{:S(2)}) collective-permute-start(f32[288,128]{1,0:T(8,128)S(1)} %get-tuple-element.33), channel_id=1, source_target_pairs={{0,2},{2,4},{3,1},{4,6},{5,3},{7,5},{8,10},{10,12},{11,9},{12,14},... | collective-permute-start | bytes 442376 | tf_op jit(solution)/shard_map/ppermute | solution.py:532
  11.4 2.7 %collective-permute-start.4 = (f32[192,128]{1,0:T(8,128)S(1)}, f32[192,128]{1,0:T(8,128)S(1)}, u32[]{:S(2)}, u32[]{:S(2)}) collective-permute-start(f32[192,128]{1,0:T(8,128)S(1)} %get-tuple-element.36), channel_id=1, source_target_pairs={{0,24},{1,25},{2,26},{3,27},{4,28},{5,29},{6,30},{7,31}} | collective-permute-start | bytes 294920 | tf_op jit(solution)/shard_map/ppermute | solution.py:553
  12.1 2.0 %collective-permute-start.3 = (f32[192,128]{1,0:T(8,128)S(1)}, f32[192,128]{1,0:T(8,128)S(1)}, u32[]{:S(2)}, u32[]{:S(2)}) collective-permute-start(f32[192,128]{1,0:T(8,128)S(1)} %get-tuple-element.36), channel_id=1, source_target_pairs={{0,16},{1,17},{2,18},{3,19},{4,20},{5,21},{6,22},{7,23}} | collective-permute-start | bytes 294920 | tf_op jit(solution)/shard_map/ppermute | solution.py:553
  12.8 8.6 %collective-permute-start.2 = (f32[192,128]{1,0:T(8,128)S(1)}, f32[192,128]{1,0:T(8,128)S(1)}, u32[]{:S(2)}, u32[]{:S(2)}) collective-permute-start(f32[192,128]{1,0:T(8,128)S(1)} %get-tuple-element.36), channel_id=1, source_target_pairs={{0,8},{1,9},{2,10},{3,11},{4,12},{5,13},{6,14},{7,15}} | collective-permute-start | bytes 294920 | tf_op jit(solution)/shard_map/ppermute | solution.py:553
  23.3 1.8 %collective-permute-start.5 = (f32[5,64,128]{2,1,0:T(8,128)S(1)}, f32[5,64,128]{2,1,0:T(8,128)S(1)}, u32[]{:S(2)}, u32[]{:S(2)}) collective-permute-start(f32[5,64,128]{2,1,0:T(8,128)S(1)} %get-tuple-element.40), channel_id=1, source_target_pairs={{0,1},{1,0},{2,3},{3,2},{4,5},{5,4},{6,7},{7,6},{8,9},{9,8},{10,11... | collective-permute-start | bytes 491528 | tf_op jit(solution)/shard_map/ppermute | solution.py:561

commit v7 on v6

--- a/solution.py
+++ b/solution.py
@@ -165,9 +165,6 @@
 DEPTH = 2 * CELLS
 PART = HALF + HALO
 NP = 2 * NPD
-TRIM = (0, 8, 16, 24, 32)
-WINDOWS = [WINDOW - 2 * amount for amount in TRIM]
-COUNTS = len(WINDOWS)
 ROWS = 192
 GROUPS = CELLS // NP
 SLOT = (
@@ -200,24 +197,11 @@
 
 
 def diff_x(bands, parts):
-    return dot(bands[parts[0].shape[0]][...], jnp.concatenate(parts, axis=0))
+    return dot(bands[...], jnp.concatenate(parts, axis=0))
 
 
 def along_depth(matrix, parts):
     return dot(jnp.concatenate(parts, axis=1), matrix[...])
-
-
-def pair_along_depth(matrix, one, two):
-    fields = [jnp.concatenate(parts, axis=1) for parts in (one, two)]
-    both = dot(jnp.concatenate(fields, axis=0), matrix[...])
-    count = one[0].shape[0]
-    return both[:count], both[count:]
-
-
-def trimmed(arrays, amount):
-    if amount == 0:
-        return arrays
-    return [array[amount:-amount] for array in arrays]
 
 
 def lanes_of(shape):
@@ -306,22 +290,25 @@
         unpack_edge(behind, window, low, False)
 
 
+def span(step):
+    gone = 2 * RADIUS * (step + 1)
+    return pl.ds(gone, WINDOW - 2 * gone)
+
+
 def place(state, held, sent):
-    start = HALO - TRIM[-1]
     core = lax.axis_index("gz")
-    state = [array[start : start + HALF] for array in state]
+    low, high = slice(0, CELLS), slice(CELLS, DEPTH)
+    own = span(STEPS - 1)
 
     @pl.when(core == 0)
     def _():
-        for index in range(5):
-            held[index] = state[index][:, :CELLS]
-            sent[index] = state[index][:, CELLS:]
+        held[...] = state[:5, own, low]
+        sent[...] = state[:5, own, high]
 
     @pl.when(core == 1)
     def _():
-        for index in range(5):
-            held[index] = state[index][:, CELLS:]
-            sent[index] = state[index][:, :CELLS]
+        held[...] = state[:5, own, high]
+        sent[...] = state[:5, own, low]
 
 
 def acoustic(state, bands):
@@ -338,12 +325,10 @@
 
 
 def constants_kernel(plane_rows, box_offset, *targets):
-    *bands_x, band_z, pick, land = targets
-    for target in bands_x:
-        count = target.shape[0]
-        row = lax.broadcasted_iota(jnp.int32, target.shape, 0)
-        column = lax.broadcasted_iota(jnp.int32, target.shape, 1)
-        target[...] = banded(jnp.where(column < count, column, column - count) - row)
+    band_x, band_z, pick, land = targets
+    row = lax.broadcasted_iota(jnp.int32, band_x.shape, 0)
+    column = lax.broadcasted_iota(jnp.int32, band_x.shape, 1)
+    band_x[...] = banded(jnp.where(column < WINDOW, column, column - WINDOW) - row)
     shape = (DEPTH, DEPTH)
     distance = lax.broadcasted_iota(jnp.int32, shape, 0) - lax.broadcasted_iota(jnp.int32, shape, 1)
     band_z[:DEPTH] = banded(distance)
@@ -364,49 +349,44 @@
     land[:, CELLS:] = land[:, :CELLS]
 
 
-def first_kernel(*refs):
-    bands_x, (band_z, pick, block, behind, ahead, other) = refs[:COUNTS], refs[COUNTS:-4]
-    held, sent, rows, carry = refs[-4:]
-    band_x = {band.shape[0]: band for band in bands_x}
+def first_kernel(
+    band_x, band_z, pick, block, behind, ahead, other, held, sent, rows, carry, picks
+):
     assemble(carry, block, ahead, behind, other)
     section = lax.axis_index("sec")
 
     @pl.when(section == 0)
     def _():
-        vx, vz, sxx, szz, sxz, light, lame, shear = [carry[index] for index in range(8)]
-        light = light * (TIME_STEP / SCALE)
-        both = (lame + 2.0 * shear) * (TIME_STEP / SCALE)
-        lame = lame * (TIME_STEP / SCALE)
-        shear = shear * (TIME_STEP / SCALE)
-        at = 0
-        for step in range(STEPS):
-            cut = TRIM[step] - at
-            at = TRIM[step]
-            vx, vz, sxx, szz, sxz, light, both, lame, shear = trimmed(
-                [vx, vz, sxx, szz, sxz, light, both, lame, shear], cut
-            )
+        light, lame, shear = carry[5], carry[6], carry[7]
+        carry[5] = light * (TIME_STEP / SCALE)
+        carry[6] = (lame + 2.0 * shear) * (TIME_STEP / SCALE)
+        carry[7] = lame * (TIME_STEP / SCALE)
+        carry[8] = shear * (TIME_STEP / SCALE)
+
+        @pl.loop(0, STEPS)
+        def _(step):
+            sxx, szz, sxz, light = carry[2], carry[3], carry[4], carry[5]
             parts_xx, parts_zz, parts_xz = halves(sxx), halves(szz), halves(sxz)
-            slope_xz, slope_zz = pair_along_depth(band_z, parts_xz, parts_zz)
-            vx = vx + light * (diff_x(band_x, parts_xx) + slope_xz)
-            vz = vz + light * (diff_x(band_x, parts_xz) + slope_zz)
+            vx = carry[0] + light * (diff_x(band_x, parts_xx) + along_depth(band_z, parts_xz))
+            vz = carry[1] + light * (diff_x(band_x, parts_xz) + along_depth(band_z, parts_zz))
+            carry[0], carry[1] = vx, vz
             parts_x, parts_z = halves(vx), halves(vz)
-            slope_x, strain_z = pair_along_depth(band_z, parts_x, parts_z)
-            strain_x = diff_x(band_x, parts_x)
+            strain_x, strain_z = diff_x(band_x, parts_x), along_depth(band_z, parts_z)
+            both, lame, shear = carry[6], carry[7], carry[8]
             sxx = sxx + (both * strain_x + lame * strain_z)
             szz = szz + (lame * strain_x + both * strain_z)
-            sxz = sxz + shear * (slope_x + diff_x(band_x, parts_z))
-            rows_x, rows_z = pair_along_depth(pick, parts_x, parts_z)
-            stress = along_depth(pick, halves(sxx + szz))
-            low = 2 * RADIUS * (step + 1) - at
-            for component, (picked, factor) in enumerate(
-                ((rows_x, COUPLING), (rows_z, COUPLING), (stress, -0.5 * COUPLING))
-            ):
-                picked = factor * picked
-                picked = picked[low : picked.shape[0] - low]
-                group, base = SLOT[step][component]
+            carry[2], carry[3] = sxx, szz
+            carry[4] = sxz + shear * (along_depth(band_z, parts_x) + diff_x(band_x, parts_z))
+            picks[3 * step] = COUPLING * along_depth(pick, parts_x)
+            picks[3 * step + 1] = COUPLING * along_depth(pick, parts_z)
+            picks[3 * step + 2] = (-0.5 * COUPLING) * along_depth(pick, halves(sxx + szz))
+
+        for step in range(STEPS):
+            for component, (group, base) in enumerate(SLOT[step]):
+                picked = picks[3 * step + component, span(step)]
                 spot = pl.ds(base, picked.shape[0])
                 rows[spot] = jnp.where(lanes_of(picked.shape) == group, picked, rows[spot])
-        place([vx, vz, sxx, szz, sxz], held, sent)
+        place(carry, held, sent)
 
     @pl.when(section > 0)
     def _():
@@ -420,10 +400,19 @@
             carry[index] = array
 
 
-def second_kernel(*refs):
-    bands_x, (band_z, land, carry, rows, held_in, sent_in, held, sent) = refs[:COUNTS], refs[COUNTS:]
-    band_x = {band.shape[0]: band for band in bands_x}
+def second_kernel(
+    band_x, band_z, land, carry, rows, held_in, sent_in, held, sent, state, picks
+):
     section = lax.axis_index("sec")
+
+    def inject(values, group):
+        added = lax.dot_general(
+            jnp.concatenate(halves(picks[group]), axis=1),
+            land[...],
+            (((1,), (1,)), ((), ())),
+            preferred_element_type=jnp.float32,
+        )
+        return values + added
 
     @pl.when(section == 0)
     def _():
@@ -432,30 +421,29 @@
 
     @pl.when(section > 0)
     def _():
-        state = [carry[index] for index in range(9)]
-        at = 0
         for step in range(STEPS):
-            if step:
-                state = trimmed(state, TRIM[step] - at)
-                at = TRIM[step]
-                state = acoustic(state, (band_x, band_z))
-            low = 2 * RADIUS * (step + 1) - at
-            high = WINDOW - 2 * at - low
-            for component in range(3):
-                group, base = SLOT[step][component]
-                taken = rows[pl.ds(base, high - low)]
-                taken = halves(jnp.where(lanes_of(taken.shape) == group, taken, 0.0))
-                added = lax.dot_general(
-                    jnp.concatenate(taken, axis=1),
-                    land[...],
-                    (((1,), (1,)), ((), ())),
-                    preferred_element_type=jnp.float32,
-                )
-                array = state[component]
-                state[component] = jnp.concatenate(
-                    [array[:low], array[low:high] + added, array[high:]], axis=0
-                )
-        place(state[:5], held, sent)
+            edge = 2 * RADIUS * (step + 1)
+            for component, (group, base) in enumerate(SLOT[step]):
+                taken = rows[pl.ds(base, WINDOW - 2 * edge)]
+                taken = jnp.where(lanes_of(taken.shape) == group, taken, 0.0)
+                index = 3 * step + component
+                picks[index, span(step)] = taken
+                picks[index, :edge] = jnp.zeros((edge, CELLS), jnp.float32)
+                picks[index, WINDOW - edge :] = jnp.zeros((edge, CELLS), jnp.float32)
+        for index in range(3):
+            state[index] = inject(carry[index], index)
+        state[3:] = carry[3:5]
+
+        @pl.loop(1, STEPS)
+        def _(step):
+            fields = [state[index] for index in range(5)]
+            media = [carry[index] for index in range(5, 9)]
+            fields = acoustic(fields + media, (band_x, band_z))
+            for index in range(3):
+                state[index] = inject(fields[index], 3 * step + index)
+            state[3], state[4] = fields[3], fields[4]
+
+        place(state, held, sent)
 
 
 def last_kernel(held, swapped, out, sems):
@@ -534,8 +522,12 @@
     other = jnp.where(is_first, joined[1], joined[0])
     *bands, pick, land = call(
         constants_kernel,
-        [narrow(count, 2 * count) for count in WINDOWS]
-        + [narrow(2 * DEPTH, DEPTH), narrow(2 * DEPTH, CELLS), narrow(DEPTH, 2 * CELLS)],
+        [
+            narrow(WINDOW, 2 * WINDOW),
+            narrow(2 * DEPTH, DEPTH),
+            narrow(2 * DEPTH, CELLS),
+            narrow(DEPTH, 2 * CELLS),
+        ],
         [plane_rows[None], box_offset[None]],
         1_000_000_000,
     )
@@ -549,6 +541,7 @@
         ],
         [*bands, pick, block, behind, ahead, other],
         4_000_000_000,
+        scratch=[pltpu.VMEM((3 * STEPS, WINDOW, CELLS), jnp.float32)],
     )
     arrived = [lax.ppermute(rows, "sec", [(0, target)]) for target in (1, 2, 3)]
     rows = arrived[0] + arrived[1] + arrived[2]
@@ -557,6 +550,10 @@
         [full(5, HALF, CELLS), full(5, HALF, CELLS)],
         [*bands, land, carry, rows, held, sent],
         4_000_000_000,
+        scratch=[
+            pltpu.VMEM((5, WINDOW, DEPTH), jnp.float32),
+            pltpu.VMEM((3 * STEPS, WINDOW, CELLS), jnp.float32),
+        ],
     )
     swapped = lax.ppermute(sent, "gz", turn)
     (out,) = call(

time: 26.1 us -> 27.5 us (1.054)
  waiting for transfers between devices: 9.07 us -> 10.2 us
  Pallas kernels: 4.93 us -> 5.33 us
    ppermute x3, waiting for transfers between devices: 7.24 us -> 8.24 us  [local_window(): arrived = [lax.ppermute(rows, 'sec', [(0, target)]) for target in (1, 2, 3)]]
    pallas_call x5, Pallas kernels: 4.93 us -> 5.33 us  [call(): pl.pallas_call(kernel, out_shape=outs, in_specs=[pl.BlockSpec(memory_spac...]
  transfers between devices with their start and end apart: 6 -> 6, of which waited for: 3 -> 3; matrix products, arithmetic and copies ran while one was open for 0% -> 0% of each run, Pallas kernels for 2% -> 1%
where the time goes in v7:
time: 27.5 us; the launch traced here: 27.3 us
  waiting for transfers between devices  10.2 us (37%)
  starting transfers between devices  9.1 us (33%)
  Pallas kernels  5.33 us (19%)
  blocking collectives  2.42 us (9%)
    ppermute x3, waiting for transfers between devices, local_window(): arrived = [lax.ppermute(rows, 'sec', [(0, target)]) for target in (1, 2, 3)]  8.24 us
    pallas_call x5, Pallas kernels, call(): pl.pallas_call(kernel, out_shape=outs, in_specs=[pl.BlockSpec(memory_spac...  5.33 us
    ppermute x1, starting transfers between devices, local_window(): behind = lax.ppermute(crossed, ('gx', 'gz'), crossed_pairs)  3.77 us
    ppermute x3, starting transfers between devices, local_window(): arrived = [lax.ppermute(rows, 'sec', [(0, target)]) for target in (1, 2, 3)]  2.63 us
    all_gather x1, blocking collectives, local_window(): joined = lax.all_gather(swap, 'gz')  2.42 us
    ppermute x1, starting transfers between devices, local_window(): ahead = lax.ppermute(straight, ('gx', 'gz'), straight_pairs)  2.08 us
    ppermute x1, waiting for transfers between devices, local_window(): swapped = lax.ppermute(sent, 'gz', turn)  1.03 us
    ppermute x1, waiting for transfers between devices, local_window(): ahead = lax.ppermute(straight, ('gx', 'gz'), straight_pairs)  0.95 us
  transfers between devices with their start and end apart: 6, of which 3 were waited for; matrix products, arithmetic and copies ran while one was open for 0% of the time, Pallas kernels for 1%

profile of v7, /device:TPU:19, one launch (start us, length us, event | category | flops | bytes accessed | tf_op | source)
XLA Modules:
  0.0 27.3 jit_solution(9616522873275688676)
XLA Ops:
  0.0 1.1 %shard_map.47 = (f32[8,128,128]{2,1,0:T(8,128)S(1)}, f32[288,128]{1,0:T(8,128)S(1)}, f32[288,128]{1,0:T(8,128)S(1)}, f32[8,104,128]{2,1,0:T(8,128)S(1)}) custom-call(f32[5,128,128]{2,1,0:T(8,128)} %bitcast.7, f32[3,128,128]{2,1,0:T(8,128)} %bitcast.8), custom_call_target="tpu_custom_call" | custom-call | flops 1000 | bytes 2097152 | tf_op jit(solution)/shard_map/pallas_call | solution.py:472
  1.1 0.0 copy-start
  1.1 0.0 copy-start.1
  1.1 3.8 %collective-permute-start = (f32[288,128]{1,0:T(8,128)S(1)}, f32[288,128]{1,0:T(8,128)S(1)}, u32[]{:S(2)}, u32[]{:S(2)}) collective-permute-start(f32[288,128]{1,0:T(8,128)S(1)} %get-tuple-element.24), channel_id=1, source_target_pairs={{1,2},{3,4},{2,1},{5,6},{4,3},{6,5},{9,10},{11,12},{10,9},{13,14},... | collective-permute-start | bytes 442376 | tf_op jit(solution)/shard_map/ppermute | solution.py:519
  4.9 2.1 %collective-permute-start.1 = (f32[288,128]{1,0:T(8,128)S(1)}, f32[288,128]{1,0:T(8,128)S(1)}, u32[]{:S(2)}, u32[]{:S(2)}) collective-permute-start(f32[288,128]{1,0:T(8,128)S(1)} %get-tuple-element.25), channel_id=1, source_target_pairs={{0,2},{2,4},{3,1},{4,6},{5,3},{7,5},{8,10},{10,12},{11,9},{12,14},... | collective-permute-start | bytes 442376 | tf_op jit(solution)/shard_map/ppermute | solution.py:520
  7.0 2.4 %all-gather = f32[16,104,128]{2,1,0:T(8,128)S(1)} all-gather(f32[8,104,128]{2,1,0:T(8,128)S(1)} %get-tuple-element.26), channel_id=2, replica_groups=mesh['sec'=4,'gx'=4,'gz'=2] {'gz'}, dimensions={0}, use_global_device_ids=true | all-gather | bytes 1277952 | tf_op jit(solution)/shard_map/all_gather | solution.py:521
  9.5 0.0 copy-done
  9.5 0.0 copy-done.1
  9.5 0.3 %shard_map.46 = (bf16[144,288]{1,0:T(8,128)(2,1)S(1)}, bf16[512,256]{1,0:T(8,128)(2,1)S(1)}, bf16[512,128]{1,0:T(8,128)(2,1)S(1)}, bf16[256,256]{1,0:T(8,128)(2,1)S(1)}) custom-call(s32[1,16]{1,0:T(1,128)S(1)} %bitcast.5, s32[1,3]{1,0:T(1,128)S(1)} %bitcast.6), custom_call_target="tpu_custom_call" | custom-call | flops 1000000000 | bytes 2097152 | tf_op jit(solution)/shard_map/pallas_call | solution.py:472
  9.8 0.0 collective-permute-done.behind
  9.8 1.0 %collective-permute-done.1.ahead = f32[288,128]{1,0:T(8,128)S(1)} collective-permute-done((f32[288,128]{1,0:T(8,128)S(1)}, f32[288,128]{1,0:T(8,128)S(1)}, u32[]{:S(2)}, u32[]{:S(2)}) %collective-permute-start.1) | collective-permute-done | bytes 147488 | tf_op jit(solution)/shard_map/ppermute | solution.py:520
  10.8 0.6 %shard_map.48 = (f32[5,64,128]{2,1,0:T(8,128)S(1)}, f32[5,64,128]{2,1,0:T(8,128)S(1)}, f32[192,128]{1,0:T(8,128)S(1)}, f32[9,144,256]{2,1,0:T(8,128)S(1)}) custom-call(bf16[144,288]{1,0:T(8,128)(2,1)S(1)} %get-tuple-element.19.band_x, bf16[512,256]{1,0:T(8,128)(2,1)S(1)} %get-tuple-element.20.band_z, bf16[512,128]{1,0:T(8,128)(2,1)S(1)} %get-tuple-element.22.pick, ...), custom_call_target="tpu_custom_call" | custom-call | flops 4000000000 | bytes 2097152 | tf_op jit(solution)/shard_map/pallas_call | solution.py:472
  11.4 0.7 %collective-permute-start.4 = (f32[192,128]{1,0:T(8,128)S(1)}, f32[192,128]{1,0:T(8,128)S(1)}, u32[]{:S(2)}, u32[]{:S(2)}) collective-permute-start(f32[192,128]{1,0:T(8,128)S(1)} %get-tuple-element.28), channel_id=1, source_target_pairs={{0,24},{1,25},{2,26},{3,27},{4,28},{5,29},{6,30},{7,31}} | collective-permute-start | bytes 294920 | tf_op jit(solution)/shard_map/ppermute | solution.py:546
  12.1 0.7 %collective-permute-start.3 = (f32[192,128]{1,0:T(8,128)S(1)}, f32[192,128]{1,0:T(8,128)S(1)}, u32[]{:S(2)}, u32[]{:S(2)}) collective-permute-start(f32[192,128]{1,0:T(8,128)S(1)} %get-tuple-element.28), channel_id=1, source_target_pairs={{0,16},{1,17},{2,18},{3,19},{4,20},{5,21},{6,22},{7,23}} | collective-permute-start | bytes 294920 | tf_op jit(solution)/shard_map/ppermute | solution.py:546
  12.8 1.3 %collective-permute-start.2 = (f32[192,128]{1,0:T(8,128)S(1)}, f32[192,128]{1,0:T(8,128)S(1)}, u32[]{:S(2)}, u32[]{:S(2)}) collective-permute-start(f32[192,128]{1,0:T(8,128)S(1)} %get-tuple-element.28), channel_id=1, source_target_pairs={{0,8},{1,9},{2,10},{3,11},{4,12},{5,13},{6,14},{7,15}} | collective-permute-start | bytes 294920 | tf_op jit(solution)/shard_map/ppermute | solution.py:546
  14.1 0.0 collective-permute-done.4
  14.1 0.0 collective-permute-done.3
  14.1 8.2 %collective-permute-done.2 = f32[192,128]{1,0:T(8,128)S(1)} collective-permute-done((f32[192,128]{1,0:T(8,128)S(1)}, f32[192,128]{1,0:T(8,128)S(1)}, u32[]{:S(2)}, u32[]{:S(2)}) %collective-permute-start.2) | collective-permute-done | bytes 98336 | tf_op jit(solution)/shard_map/ppermute | solution.py:546
  22.3 2.5 %shard_map.49 = (f32[5,64,128]{2,1,0:T(8,128)S(1)}, f32[5,64,128]{2,1,0:T(8,128)S(1)}) custom-call(bf16[144,288]{1,0:T(8,128)(2,1)S(1)} %get-tuple-element.19.band_x, bf16[512,256]{1,0:T(8,128)(2,1)S(1)} %get-tuple-element.20.band_z, bf16[256,256]{1,0:T(8,128)(2,1)S(1)} %get-tuple-element.21.land, f32[9,144,256]{2,1,0:T(8,128)S(1)} %get-tuple-element.27.carry, ...), custom_call_target="tpu_custom_call" | custom-call | flops 4000000000 | bytes 2097152 | tf_op jit(solution)/shard_map/pallas_call | solution.py:472
  24.9 0.6 %collective-permute-start.5 = (f32[5,64,128]{2,1,0:T(8,128)S(1)}, f32[5,64,128]{2,1,0:T(8,128)S(1)}, u32[]{:S(2)}, u32[]{:S(2)}) collective-permute-start(f32[5,64,128]{2,1,0:T(8,128)S(1)} %get-tuple-element.32), channel_id=1, source_target_pairs={{0,1},{1,0},{2,3},{3,2},{4,5},{5,4},{6,7},{7,6},{8,9},{9,8},{10,11... | collective-permute-start | bytes 491528 | tf_op jit(solution)/shard_map/ppermute | solution.py:558
  25.5 1.0 %collective-permute-done.5.swapped = f32[5,64,128]{2,1,0:T(8,128)S(1)} collective-permute-done((f32[5,64,128]{2,1,0:T(8,128)S(1)}, f32[5,64,128]{2,1,0:T(8,128)S(1)}, u32[]{:S(2)}, u32[]{:S(2)}) %collective-permute-start.5) | collective-permute-done | bytes 163872 | tf_op jit(solution)/shard_map/ppermute | solution.py:558
  26.5 0.7 %shard_map.50 = f32[5,128,128]{2,1,0:T(8,128)} custom-call(f32[5,64,128]{2,1,0:T(8,128)S(1)} %get-tuple-element.31.held, f32[5,64,128]{2,1,0:T(8,128)S(1)} %collective-permute-done.5.swapped), custom_call_target="tpu_custom_call" | custom-call | flops 1000 | bytes 2097152 | tf_op jit(solution)/shard_map/pallas_call | solution.py:472
  (2 shorter events, 0.1 us)
Async XLA Ops:
  1.1 8.4 %copy-start = (s32[16]{0:T(128)S(1)}, s32[16]{0:T(128)}, u32[]{:S(2)}) copy-start(s32[16]{0:T(128)} %param.6) | copy-start | bytes 196
  1.1 8.4 %copy-start.1 = (s32[3]{0:T(128)S(1)}, s32[3]{0:T(128)}, u32[]{:S(2)}) copy-start(s32[3]{0:T(128)} %param.7) | copy-start | bytes 40
  1.1 8.7 %collective-permute-start = (f32[288,128]{1,0:T(8,128)S(1)}, f32[288,128]{1,0:T(8,128)S(1)}, u32[]{:S(2)}, u32[]{:S(2)}) collective-permute-start(f32[288,128]{1,0:T(8,128)S(1)} %get-tuple-element.24), channel_id=1, source_target_pairs={{1,2},{3,4},{2,1},{5,6},{4,3},{6,5},{9,10},{11,12},{10,9},{13,14},... | collective-permute-start | bytes 442376 | tf_op jit(solution)/shard_map/ppermute | solution.py:519
  4.9 5.9 %collective-permute-start.1 = (f32[288,128]{1,0:T(8,128)S(1)}, f32[288,128]{1,0:T(8,128)S(1)}, u32[]{:S(2)}, u32[]{:S(2)}) collective-permute-start(f32[288,128]{1,0:T(8,128)S(1)} %get-tuple-element.25), channel_id=1, source_target_pairs={{0,2},{2,4},{3,1},{4,6},{5,3},{7,5},{8,10},{10,12},{11,9},{12,14},... | collective-permute-start | bytes 442376 | tf_op jit(solution)/shard_map/ppermute | solution.py:520
  11.4 2.7 %collective-permute-start.4 = (f32[192,128]{1,0:T(8,128)S(1)}, f32[192,128]{1,0:T(8,128)S(1)}, u32[]{:S(2)}, u32[]{:S(2)}) collective-permute-start(f32[192,128]{1,0:T(8,128)S(1)} %get-tuple-element.28), channel_id=1, source_target_pairs={{0,24},{1,25},{2,26},{3,27},{4,28},{5,29},{6,30},{7,31}} | collective-permute-start | bytes 294920 | tf_op jit(solution)/shard_map/ppermute | solution.py:546
  12.1 2.0 %collective-permute-start.3 = (f32[192,128]{1,0:T(8,128)S(1)}, f32[192,128]{1,0:T(8,128)S(1)}, u32[]{:S(2)}, u32[]{:S(2)}) collective-permute-start(f32[192,128]{1,0:T(8,128)S(1)} %get-tuple-element.28), channel_id=1, source_target_pairs={{0,16},{1,17},{2,18},{3,19},{4,20},{5,21},{6,22},{7,23}} | collective-permute-start | bytes 294920 | tf_op jit(solution)/shard_map/ppermute | solution.py:546
  12.8 9.6 %collective-permute-start.2 = (f32[192,128]{1,0:T(8,128)S(1)}, f32[192,128]{1,0:T(8,128)S(1)}, u32[]{:S(2)}, u32[]{:S(2)}) collective-permute-start(f32[192,128]{1,0:T(8,128)S(1)} %get-tuple-element.28), channel_id=1, source_target_pairs={{0,8},{1,9},{2,10},{3,11},{4,12},{5,13},{6,14},{7,15}} | collective-permute-start | bytes 294920 | tf_op jit(solution)/shard_map/ppermute | solution.py:546
  24.9 1.7 %collective-permute-start.5 = (f32[5,64,128]{2,1,0:T(8,128)S(1)}, f32[5,64,128]{2,1,0:T(8,128)S(1)}, u32[]{:S(2)}, u32[]{:S(2)}) collective-permute-start(f32[5,64,128]{2,1,0:T(8,128)S(1)} %get-tuple-element.32), channel_id=1, source_target_pairs={{0,1},{1,0},{2,3},{3,2},{4,5},{5,4},{6,7},{7,6},{8,9},{9,8},{10,11... | collective-permute-start | bytes 491528 | tf_op jit(solution)/shard_map/ppermute | solution.py:558

commit v8 on v6

--- a/solution.py
+++ b/solution.py
@@ -207,13 +207,6 @@
     return dot(jnp.concatenate(parts, axis=1), matrix[...])
 
 
-def pair_along_depth(matrix, one, two):
-    fields = [jnp.concatenate(parts, axis=1) for parts in (one, two)]
-    both = dot(jnp.concatenate(fields, axis=0), matrix[...])
-    count = one[0].shape[0]
-    return both[:count], both[count:]
-
-
 def trimmed(arrays, amount):
     if amount == 0:
         return arrays
@@ -360,8 +353,8 @@
     pick[:DEPTH] = dot(hot, spread).astype(jnp.bfloat16)
     pick[DEPTH:] = pick[:DEPTH]
     hot = jnp.where(depth == landing, 1.0, 0.0).astype(jnp.bfloat16)
-    land[:, :CELLS] = dot(hot, spread).astype(jnp.bfloat16)
-    land[:, CELLS:] = land[:, :CELLS]
+    land[:CELLS] = dot(hot, spread).T.astype(jnp.bfloat16)
+    land[CELLS:] = land[:CELLS]
 
 
 def first_kernel(*refs):
@@ -386,22 +379,18 @@
                 [vx, vz, sxx, szz, sxz, light, both, lame, shear], cut
             )
             parts_xx, parts_zz, parts_xz = halves(sxx), halves(szz), halves(sxz)
-            slope_xz, slope_zz = pair_along_depth(band_z, parts_xz, parts_zz)
-            vx = vx + light * (diff_x(band_x, parts_xx) + slope_xz)
-            vz = vz + light * (diff_x(band_x, parts_xz) + slope_zz)
+            vx = vx + light * (diff_x(band_x, parts_xx) + along_depth(band_z, parts_xz))
+            vz = vz + light * (diff_x(band_x, parts_xz) + along_depth(band_z, parts_zz))
             parts_x, parts_z = halves(vx), halves(vz)
-            slope_x, strain_z = pair_along_depth(band_z, parts_x, parts_z)
-            strain_x = diff_x(band_x, parts_x)
+            strain_x, strain_z = diff_x(band_x, parts_x), along_depth(band_z, parts_z)
             sxx = sxx + (both * strain_x + lame * strain_z)
             szz = szz + (lame * strain_x + both * strain_z)
-            sxz = sxz + shear * (slope_x + diff_x(band_x, parts_z))
-            rows_x, rows_z = pair_along_depth(pick, parts_x, parts_z)
-            stress = along_depth(pick, halves(sxx + szz))
+            sxz = sxz + shear * (along_depth(band_z, parts_x) + diff_x(band_x, parts_z))
             low = 2 * RADIUS * (step + 1) - at
-            for component, (picked, factor) in enumerate(
-                ((rows_x, COUPLING), (rows_z, COUPLING), (stress, -0.5 * COUPLING))
+            for component, (parts, factor) in enumerate(
+                ((parts_x, COUPLING), (parts_z, COUPLING), (halves(sxx + szz), -0.5 * COUPLING))
             ):
-                picked = factor * picked
+                picked = factor * along_depth(pick, parts)
                 picked = picked[low : picked.shape[0] - low]
                 group, base = SLOT[step][component]
                 spot = pl.ds(base, picked.shape[0])
@@ -445,12 +434,7 @@
                 group, base = SLOT[step][component]
                 taken = rows[pl.ds(base, high - low)]
                 taken = halves(jnp.where(lanes_of(taken.shape) == group, taken, 0.0))
-                added = lax.dot_general(
-                    jnp.concatenate(taken, axis=1),
-                    land[...],
-                    (((1,), (1,)), ((), ())),
-                    preferred_element_type=jnp.float32,
-                )
+                added = along_depth(land, taken)
                 array = state[component]
                 state[component] = jnp.concatenate(
                     [array[:low], array[low:high] + added, array[high:]], axis=0
@@ -535,7 +519,7 @@
     *bands, pick, land = call(
         constants_kernel,
         [narrow(count, 2 * count) for count in WINDOWS]
-        + [narrow(2 * DEPTH, DEPTH), narrow(2 * DEPTH, CELLS), narrow(DEPTH, 2 * CELLS)],
+        + [narrow(2 * DEPTH, DEPTH), narrow(2 * DEPTH, CELLS), narrow(2 * CELLS, DEPTH)],
         [plane_rows[None], box_offset[None]],
         1_000_000_000,
     )

time: 26.1 us -> 25.9 us (level)
  no operation moved by 1% of the time
where the time goes in v8:
time: 25.9 us; the launch traced here: 25.7 us
  starting transfers between devices  9.28 us (36%)
  waiting for transfers between devices  9.01 us (35%)
  Pallas kernels  4.79 us (18%)
  blocking collectives  2.42 us (9%)
    ppermute x3, waiting for transfers between devices, local_window(): arrived = [lax.ppermute(rows, 'sec', [(0, target)]) for target in (1, 2, 3)]  7.24 us
    pallas_call x5, Pallas kernels, call(): pl.pallas_call(kernel, out_shape=outs, in_specs=[pl.BlockSpec(memory_spac...  4.79 us
    ppermute x1, starting transfers between devices, local_window(): behind = lax.ppermute(crossed, ('gx', 'gz'), crossed_pairs)  3.77 us
    ppermute x3, starting transfers between devices, local_window(): arrived = [lax.ppermute(rows, 'sec', [(0, target)]) for target in (1, 2, 3)]  2.63 us
    all_gather x1, blocking collectives, local_window(): joined = lax.all_gather(swap, 'gz')  2.42 us
    ppermute x1, starting transfers between devices, local_window(): ahead = lax.ppermute(straight, ('gx', 'gz'), straight_pairs)  2.08 us
    ppermute x1, waiting for transfers between devices, local_window(): swapped = lax.ppermute(sent, 'gz', turn)  1.03 us
    ppermute x1, starting transfers between devices, local_window(): swapped = lax.ppermute(sent, 'gz', turn)  0.81 us
  transfers between devices with their start and end apart: 6, of which 3 were waited for; matrix products, arithmetic and copies ran while one was open for 0% of the time, Pallas kernels for 2%

profile of v8, /device:TPU:19, one launch (start us, length us, event | category | flops | bytes accessed | tf_op | source)
XLA Modules:
  0.0 25.7 jit_solution(17432292993739257509)
XLA Ops:
  0.0 1.1 %shard_map.47 = (f32[8,128,128]{2,1,0:T(8,128)S(1)}, f32[288,128]{1,0:T(8,128)S(1)}, f32[288,128]{1,0:T(8,128)S(1)}, f32[8,104,128]{2,1,0:T(8,128)S(1)}) custom-call(f32[5,128,128]{2,1,0:T(8,128)} %bitcast.7, f32[3,128,128]{2,1,0:T(8,128)} %bitcast.8), custom_call_target="tpu_custom_call" | custom-call | flops 1000 | bytes 2097152 | tf_op jit(solution)/shard_map/pallas_call | solution.py:468
  1.1 0.0 copy-start
  1.1 0.0 copy-start.1
  1.1 3.8 %collective-permute-start = (f32[288,128]{1,0:T(8,128)S(1)}, f32[288,128]{1,0:T(8,128)S(1)}, u32[]{:S(2)}, u32[]{:S(2)}) collective-permute-start(f32[288,128]{1,0:T(8,128)S(1)} %get-tuple-element.32), channel_id=1, source_target_pairs={{1,2},{3,4},{2,1},{5,6},{4,3},{6,5},{9,10},{11,12},{10,9},{13,14},... | collective-permute-start | bytes 442376 | tf_op jit(solution)/shard_map/ppermute | solution.py:515
  4.9 2.1 %collective-permute-start.1 = (f32[288,128]{1,0:T(8,128)S(1)}, f32[288,128]{1,0:T(8,128)S(1)}, u32[]{:S(2)}, u32[]{:S(2)}) collective-permute-start(f32[288,128]{1,0:T(8,128)S(1)} %get-tuple-element.33), channel_id=1, source_target_pairs={{0,2},{2,4},{3,1},{4,6},{5,3},{7,5},{8,10},{10,12},{11,9},{12,14},... | collective-permute-start | bytes 442376 | tf_op jit(solution)/shard_map/ppermute | solution.py:516
  7.0 2.4 %all-gather = f32[16,104,128]{2,1,0:T(8,128)S(1)} all-gather(f32[8,104,128]{2,1,0:T(8,128)S(1)} %get-tuple-element.34), channel_id=2, replica_groups=mesh['sec'=4,'gx'=4,'gz'=2] {'gz'}, dimensions={0}, use_global_device_ids=true | all-gather | bytes 1277952 | tf_op jit(solution)/shard_map/all_gather | solution.py:517
  9.5 0.0 copy-done
  9.5 0.0 copy-done.1
  9.5 0.6 %shard_map.46 = (bf16[144,288]{1,0:T(8,128)(2,1)S(1)}, bf16[128,256]{1,0:T(8,128)(2,1)S(1)}, bf16[112,224]{1,0:T(8,128)(2,1)S(1)}, bf16[96,192]{1,0:T(8,128)(2,1...) custom-call(s32[1,16]{1,0:T(1,128)S(1)} %bitcast.5, ...), custom_call_target="tpu_custom_call" | custom-call | flops 1000000000 | bytes 2097152 | tf_op jit(solution)/shard_map/pallas_call | solution.py:468
  10.0 0.0 collective-permute-done.refs_8_
  10.0 0.7 %collective-permute-done.1.refs_9_ = f32[288,128]{1,0:T(8,128)S(1)} collective-permute-done((f32[288,128]{1,0:T(8,128)S(1)}, f32[288,128]{1,0:T(8,128)S(1)}, u32[]{:S(2)}, u32[]{:S(2)}) %collective-permute-start.1) | collective-permute-done | bytes 147488 | tf_op jit(solution)/shard_map/ppermute | solution.py:516
  10.8 0.6 %shard_map.48 = (f32[5,64,128]{2,1,0:T(8,128)S(1)}, f32[5,64,128]{2,1,0:T(8,128)S(1)}, f32[192,128]{1,0:T(8,128)S(1)}, f32[9,144,256]{2,1,0:T(8,128)S(1)}) custom-call(bf16[144,288]{1,0:T(8,128)(2,1)S(1)} %get-tuple-element.23.refs_0_, bf16[128,256]{1,0:T(8,128)(2,1)S(1)} %get-tuple-element.24.refs_1_, bf16[112,224]{1,0:T(8,128)(2,1)S(1)} %get-tuple-element.25.refs_2_, ...), custom_call_target="tpu_custom_call" | custom-call | flops 4000000000 | bytes 2097152 | tf_op jit(solution)/shard_map/pallas_call | solution.py:468
  11.4 0.7 %collective-permute-start.4 = (f32[192,128]{1,0:T(8,128)S(1)}, f32[192,128]{1,0:T(8,128)S(1)}, u32[]{:S(2)}, u32[]{:S(2)}) collective-permute-start(f32[192,128]{1,0:T(8,128)S(1)} %get-tuple-element.36), channel_id=1, source_target_pairs={{0,24},{1,25},{2,26},{3,27},{4,28},{5,29},{6,30},{7,31}} | collective-permute-start | bytes 294920 | tf_op jit(solution)/shard_map/ppermute | solution.py:537
  12.1 0.7 %collective-permute-start.3 = (f32[192,128]{1,0:T(8,128)S(1)}, f32[192,128]{1,0:T(8,128)S(1)}, u32[]{:S(2)}, u32[]{:S(2)}) collective-permute-start(f32[192,128]{1,0:T(8,128)S(1)} %get-tuple-element.36), channel_id=1, source_target_pairs={{0,16},{1,17},{2,18},{3,19},{4,20},{5,21},{6,22},{7,23}} | collective-permute-start | bytes 294920 | tf_op jit(solution)/shard_map/ppermute | solution.py:537
  12.8 1.3 %collective-permute-start.2 = (f32[192,128]{1,0:T(8,128)S(1)}, f32[192,128]{1,0:T(8,128)S(1)}, u32[]{:S(2)}, u32[]{:S(2)}) collective-permute-start(f32[192,128]{1,0:T(8,128)S(1)} %get-tuple-element.36), channel_id=1, source_target_pairs={{0,8},{1,9},{2,10},{3,11},{4,12},{5,13},{6,14},{7,15}} | collective-permute-start | bytes 294920 | tf_op jit(solution)/shard_map/ppermute | solution.py:537
  14.1 0.0 collective-permute-done.4
  14.1 0.0 collective-permute-done.3
  14.1 7.2 %collective-permute-done.2 = f32[192,128]{1,0:T(8,128)S(1)} collective-permute-done((f32[192,128]{1,0:T(8,128)S(1)}, f32[192,128]{1,0:T(8,128)S(1)}, u32[]{:S(2)}, u32[]{:S(2)}) %collective-permute-start.2) | collective-permute-done | bytes 98336 | tf_op jit(solution)/shard_map/ppermute | solution.py:537
  21.3 1.8 %shard_map.49 = (f32[5,64,128]{2,1,0:T(8,128)S(1)}, f32[5,64,128]{2,1,0:T(8,128)S(1)}) custom-call(bf16[144,288]{1,0:T(8,128)(2,1)S(1)} %get-tuple-element.23.refs_0_, bf16[128,256]{1,0:T(8,128)(2,1)S(1)} %get-tuple-element.24.refs_1_, bf16[112,224]{1,0:T(8,128)(2,1)S(1)} %get-tuple-element.25.refs_2_, bf16[96,192]{1,0:T(8,128)(2,1)S(1)} %get-tuple-element.26.refs_3_, ...), custom_call_target="tpu_custom_call" | custom-call | flops 4000000000 | bytes 2097152 | tf_op jit(solution)/shard_map/pallas_call | solution.py:468
  23.1 0.8 %collective-permute-start.5 = (f32[5,64,128]{2,1,0:T(8,128)S(1)}, f32[5,64,128]{2,1,0:T(8,128)S(1)}, u32[]{:S(2)}, u32[]{:S(2)}) collective-permute-start(f32[5,64,128]{2,1,0:T(8,128)S(1)} %get-tuple-element.40), channel_id=1, source_target_pairs={{0,1},{1,0},{2,3},{3,2},{4,5},{5,4},{6,7},{7,6},{8,9},{9,8},{10,11... | collective-permute-start | bytes 491528 | tf_op jit(solution)/shard_map/ppermute | solution.py:545
  23.9 1.0 %collective-permute-done.5.swapped = f32[5,64,128]{2,1,0:T(8,128)S(1)} collective-permute-done((f32[5,64,128]{2,1,0:T(8,128)S(1)}, f32[5,64,128]{2,1,0:T(8,128)S(1)}, u32[]{:S(2)}, u32[]{:S(2)}) %collective-permute-start.5) | collective-permute-done | bytes 163872 | tf_op jit(solution)/shard_map/ppermute | solution.py:545
  25.0 0.7 %shard_map.50 = f32[5,128,128]{2,1,0:T(8,128)} custom-call(f32[5,64,128]{2,1,0:T(8,128)S(1)} %get-tuple-element.39.held, f32[5,64,128]{2,1,0:T(8,128)S(1)} %collective-permute-done.5.swapped), custom_call_target="tpu_custom_call" | custom-call | flops 1000 | bytes 2097152 | tf_op jit(solution)/shard_map/pallas_call | solution.py:468
  (2 shorter events, 0.1 us)
Async XLA Ops:
  1.1 8.4 %copy-start = (s32[16]{0:T(128)S(1)}, s32[16]{0:T(128)}, u32[]{:S(2)}) copy-start(s32[16]{0:T(128)} %param.6) | copy-start | bytes 196
  1.1 8.4 %copy-start.1 = (s32[3]{0:T(128)S(1)}, s32[3]{0:T(128)}, u32[]{:S(2)}) copy-start(s32[3]{0:T(128)} %param.7) | copy-start | bytes 40
  1.1 8.9 %collective-permute-start = (f32[288,128]{1,0:T(8,128)S(1)}, f32[288,128]{1,0:T(8,128)S(1)}, u32[]{:S(2)}, u32[]{:S(2)}) collective-permute-start(f32[288,128]{1,0:T(8,128)S(1)} %get-tuple-element.32), channel_id=1, source_target_pairs={{1,2},{3,4},{2,1},{5,6},{4,3},{6,5},{9,10},{11,12},{10,9},{13,14},... | collective-permute-start | bytes 442376 | tf_op jit(solution)/shard_map/ppermute | solution.py:515
  4.9 5.9 %collective-permute-start.1 = (f32[288,128]{1,0:T(8,128)S(1)}, f32[288,128]{1,0:T(8,128)S(1)}, u32[]{:S(2)}, u32[]{:S(2)}) collective-permute-start(f32[288,128]{1,0:T(8,128)S(1)} %get-tuple-element.33), channel_id=1, source_target_pairs={{0,2},{2,4},{3,1},{4,6},{5,3},{7,5},{8,10},{10,12},{11,9},{12,14},... | collective-permute-start | bytes 442376 | tf_op jit(solution)/shard_map/ppermute | solution.py:516
  11.4 2.7 %collective-permute-start.4 = (f32[192,128]{1,0:T(8,128)S(1)}, f32[192,128]{1,0:T(8,128)S(1)}, u32[]{:S(2)}, u32[]{:S(2)}) collective-permute-start(f32[192,128]{1,0:T(8,128)S(1)} %get-tuple-element.36), channel_id=1, source_target_pairs={{0,24},{1,25},{2,26},{3,27},{4,28},{5,29},{6,30},{7,31}} | collective-permute-start | bytes 294920 | tf_op jit(solution)/shard_map/ppermute | solution.py:537
  12.1 2.0 %collective-permute-start.3 = (f32[192,128]{1,0:T(8,128)S(1)}, f32[192,128]{1,0:T(8,128)S(1)}, u32[]{:S(2)}, u32[]{:S(2)}) collective-permute-start(f32[192,128]{1,0:T(8,128)S(1)} %get-tuple-element.36), channel_id=1, source_target_pairs={{0,16},{1,17},{2,18},{3,19},{4,20},{5,21},{6,22},{7,23}} | collective-permute-start | bytes 294920 | tf_op jit(solution)/shard_map/ppermute | solution.py:537
  12.8 8.6 %collective-permute-start.2 = (f32[192,128]{1,0:T(8,128)S(1)}, f32[192,128]{1,0:T(8,128)S(1)}, u32[]{:S(2)}, u32[]{:S(2)}) collective-permute-start(f32[192,128]{1,0:T(8,128)S(1)} %get-tuple-element.36), channel_id=1, source_target_pairs={{0,8},{1,9},{2,10},{3,11},{4,12},{5,13},{6,14},{7,15}} | collective-permute-start | bytes 294920 | tf_op jit(solution)/shard_map/ppermute | solution.py:537
  23.1 1.8 %collective-permute-start.5 = (f32[5,64,128]{2,1,0:T(8,128)S(1)}, f32[5,64,128]{2,1,0:T(8,128)S(1)}, u32[]{:S(2)}, u32[]{:S(2)}) collective-permute-start(f32[5,64,128]{2,1,0:T(8,128)S(1)} %get-tuple-element.40), channel_id=1, source_target_pairs={{0,1},{1,0},{2,3},{3,2},{4,5},{5,4},{6,7},{7,6},{8,9},{9,8},{10,11... | collective-permute-start | bytes 491528 | tf_op jit(solution)/shard_map/ppermute | solution.py:545

commit v9 on v8

--- a/solution.py
+++ b/solution.py
@@ -238,11 +238,9 @@
         row += 8
 
 
-def unpack_edge(edge, window, lanes, before):
-    body, rest = (8, 0) if before else (PART, WINDOW - 8)
+def unpack_rest(edge, window, lanes, before):
+    rest = 0 if before else WINDOW - 8
     near = lax.broadcasted_iota(jnp.int32, (8, CELLS), 0) // 4 == int(before)
-    for index in range(8):
-        window[index, body : body + BODY, lanes] = edge[BODY * index : BODY * (index + 1)]
     row = 8 * BODY
     for index in WHOLE:
         window[index, rest : rest + 8, lanes] = edge[row : row + 8]
@@ -286,17 +284,29 @@
 
     @pl.when(core == 0)
     def _():
-        unpack_edge(ahead, window, low, True)
-        unpack_edge(behind, window, high, True)
-        window[:8, HALO:, low] = block[:, :PART]
-        window[:8, HALO:, high] = other[...]
+        @pl.loop(0, 8)
+        def _(index):
+            body = pl.ds(pl.multiple_of(BODY * index, 8), BODY)
+            window[index, 8:HALO, low] = ahead[body]
+            window[index, 8:HALO, high] = behind[body]
+            window[index, HALO:, low] = block[index, :PART]
+            window[index, HALO:, high] = other[index]
+
+        unpack_rest(ahead, window, low, True)
+        unpack_rest(behind, window, high, True)
 
     @pl.when(core == 1)
     def _():
-        window[:8, :PART, high] = block[:, CELLS - PART :]
-        window[:8, :PART, low] = other[...]
-        unpack_edge(ahead, window, high, False)
-        unpack_edge(behind, window, low, False)
+        @pl.loop(0, 8)
+        def _(index):
+            body = pl.ds(pl.multiple_of(BODY * index, 8), BODY)
+            window[index, :PART, high] = block[index, CELLS - PART :]
+            window[index, :PART, low] = other[index]
+            window[index, PART : WINDOW - 8, high] = ahead[body]
+            window[index, PART : WINDOW - 8, low] = behind[body]
+
+        unpack_rest(ahead, window, high, False)
+        unpack_rest(behind, window, low, False)
 
 
 def place(state, held, sent):
@@ -363,6 +373,17 @@
     band_x = {band.shape[0]: band for band in bands_x}
     assemble(carry, block, ahead, behind, other)
     section = lax.axis_index("sec")
+
+    @pl.when(section > 0)
+    def _():
+        vx, vz, pressure, one, two, light, kappa, loss = [carry[index] for index in range(8)]
+        light = light * (TIME_STEP / SCALE)
+        kappa = kappa * (1.0 / SCALE)
+        loss_one = loss * ((1.0 - RELAXATION[0]) * MEMORY_WEIGHT[0])
+        loss_two = loss * ((1.0 - RELAXATION[1]) * MEMORY_WEIGHT[1])
+        state = [vx, vz, pressure, one, two, light, kappa, loss_one, loss_two]
+        for index, array in enumerate(acoustic(state, (band_x, band_z))):
+            carry[index] = array
 
     @pl.when(section == 0)
     def _():
@@ -397,17 +418,6 @@
                 rows[spot] = jnp.where(lanes_of(picked.shape) == group, picked, rows[spot])
         place([vx, vz, sxx, szz, sxz], held, sent)
 
-    @pl.when(section > 0)
-    def _():
-        vx, vz, pressure, one, two, light, kappa, loss = [carry[index] for index in range(8)]
-        light = light * (TIME_STEP / SCALE)
-        kappa = kappa * (1.0 / SCALE)
-        loss_one = loss * ((1.0 - RELAXATION[0]) * MEMORY_WEIGHT[0])
-        loss_two = loss * ((1.0 - RELAXATION[1]) * MEMORY_WEIGHT[1])
-        state = [vx, vz, pressure, one, two, light, kappa, loss_one, loss_two]
-        for index, array in enumerate(acoustic(state, (band_x, band_z))):
-            carry[index] = array
-
 
 def second_kernel(*refs):
     bands_x, (band_z, land, carry, rows, held_in, sent_in, held, sent) = refs[:COUNTS], refs[COUNTS:]

time: 25.9 us -> 25.9 us (level)
  no operation moved by 1% of the time
where the time goes in v9:
time: 25.9 us; the launch traced here: 25.7 us
  starting transfers between devices  9.29 us (36%)
  waiting for transfers between devices  9.01 us (35%)
  Pallas kernels  4.78 us (18%)
  blocking collectives  2.42 us (9%)
    ppermute x3, waiting for transfers between devices, local_window(): arrived = [lax.ppermute(rows, 'sec', [(0, target)]) for target in (1, 2, 3)]  7.24 us
    pallas_call x5, Pallas kernels, call(): pl.pallas_call(kernel, out_shape=outs, in_specs=[pl.BlockSpec(memory_spac...  4.78 us
    ppermute x1, starting transfers between devices, local_window(): behind = lax.ppermute(crossed, ('gx', 'gz'), crossed_pairs)  3.77 us
    ppermute x3, starting transfers between devices, local_window(): arrived = [lax.ppermute(rows, 'sec', [(0, target)]) for target in (1, 2, 3)]  2.63 us
    all_gather x1, blocking collectives, local_window(): joined = lax.all_gather(swap, 'gz')  2.42 us
    ppermute x1, starting transfers between devices, local_window(): ahead = lax.ppermute(straight, ('gx', 'gz'), straight_pairs)  2.08 us
    ppermute x1, waiting for transfers between devices, local_window(): swapped = lax.ppermute(sent, 'gz', turn)  1.03 us
    ppermute x1, starting transfers between devices, local_window(): swapped = lax.ppermute(sent, 'gz', turn)  0.82 us
  transfers between devices with their start and end apart: 6, of which 3 were waited for; matrix products, arithmetic and copies ran while one was open for 0% of the time, Pallas kernels for 2%

profile of v9, /device:TPU:19, one launch (start us, length us, event | category | flops | bytes accessed | tf_op | source)
XLA Modules:
  0.0 25.7 jit_solution(9872058853150637449)
XLA Ops:
  0.0 1.1 %shard_map.47 = (f32[8,128,128]{2,1,0:T(8,128)S(1)}, f32[288,128]{1,0:T(8,128)S(1)}, f32[288,128]{1,0:T(8,128)S(1)}, f32[8,104,128]{2,1,0:T(8,128)S(1)}) custom-call(f32[5,128,128]{2,1,0:T(8,128)} %bitcast.7, f32[3,128,128]{2,1,0:T(8,128)} %bitcast.8), custom_call_target="tpu_custom_call" | custom-call | flops 1000 | bytes 2097152 | tf_op jit(solution)/shard_map/pallas_call | solution.py:478
  1.1 0.0 copy-start
  1.1 0.0 copy-start.1
  1.1 3.8 %collective-permute-start = (f32[288,128]{1,0:T(8,128)S(1)}, f32[288,128]{1,0:T(8,128)S(1)}, u32[]{:S(2)}, u32[]{:S(2)}) collective-permute-start(f32[288,128]{1,0:T(8,128)S(1)} %get-tuple-element.32), channel_id=1, source_target_pairs={{1,2},{3,4},{2,1},{5,6},{4,3},{6,5},{9,10},{11,12},{10,9},{13,14},... | collective-permute-start | bytes 442376 | tf_op jit(solution)/shard_map/ppermute | solution.py:525
  4.9 2.1 %collective-permute-start.1 = (f32[288,128]{1,0:T(8,128)S(1)}, f32[288,128]{1,0:T(8,128)S(1)}, u32[]{:S(2)}, u32[]{:S(2)}) collective-permute-start(f32[288,128]{1,0:T(8,128)S(1)} %get-tuple-element.33), channel_id=1, source_target_pairs={{0,2},{2,4},{3,1},{4,6},{5,3},{7,5},{8,10},{10,12},{11,9},{12,14},... | collective-permute-start | bytes 442376 | tf_op jit(solution)/shard_map/ppermute | solution.py:526
  7.0 2.4 %all-gather = f32[16,104,128]{2,1,0:T(8,128)S(1)} all-gather(f32[8,104,128]{2,1,0:T(8,128)S(1)} %get-tuple-element.34), channel_id=2, replica_groups=mesh['sec'=4,'gx'=4,'gz'=2] {'gz'}, dimensions={0}, use_global_device_ids=true | all-gather | bytes 1277952 | tf_op jit(solution)/shard_map/all_gather | solution.py:527
  9.5 0.0 copy-done
  9.5 0.0 copy-done.1
  9.5 0.6 %shard_map.46 = (bf16[144,288]{1,0:T(8,128)(2,1)S(1)}, bf16[128,256]{1,0:T(8,128)(2,1)S(1)}, bf16[112,224]{1,0:T(8,128)(2,1)S(1)}, bf16[96,192]{1,0:T(8,128)(2,1...) custom-call(s32[1,16]{1,0:T(1,128)S(1)} %bitcast.5, ...), custom_call_target="tpu_custom_call" | custom-call | flops 1000000000 | bytes 2097152 | tf_op jit(solution)/shard_map/pallas_call | solution.py:478
  10.0 0.0 collective-permute-done.refs_8_
  10.0 0.7 %collective-permute-done.1.refs_9_ = f32[288,128]{1,0:T(8,128)S(1)} collective-permute-done((f32[288,128]{1,0:T(8,128)S(1)}, f32[288,128]{1,0:T(8,128)S(1)}, u32[]{:S(2)}, u32[]{:S(2)}) %collective-permute-start.1) | collective-permute-done | bytes 147488 | tf_op jit(solution)/shard_map/ppermute | solution.py:526
  10.8 0.6 %shard_map.48 = (f32[5,64,128]{2,1,0:T(8,128)S(1)}, f32[5,64,128]{2,1,0:T(8,128)S(1)}, f32[192,128]{1,0:T(8,128)S(1)}, f32[9,144,256]{2,1,0:T(8,128)S(1)}) custom-call(bf16[144,288]{1,0:T(8,128)(2,1)S(1)} %get-tuple-element.23.refs_0_, bf16[128,256]{1,0:T(8,128)(2,1)S(1)} %get-tuple-element.24.refs_1_, bf16[112,224]{1,0:T(8,128)(2,1)S(1)} %get-tuple-element.25.refs_2_, ...), custom_call_target="tpu_custom_call" | custom-call | flops 4000000000 | bytes 2097152 | tf_op jit(solution)/shard_map/pallas_call | solution.py:478
  11.4 0.7 %collective-permute-start.4 = (f32[192,128]{1,0:T(8,128)S(1)}, f32[192,128]{1,0:T(8,128)S(1)}, u32[]{:S(2)}, u32[]{:S(2)}) collective-permute-start(f32[192,128]{1,0:T(8,128)S(1)} %get-tuple-element.36), channel_id=1, source_target_pairs={{0,24},{1,25},{2,26},{3,27},{4,28},{5,29},{6,30},{7,31}} | collective-permute-start | bytes 294920 | tf_op jit(solution)/shard_map/ppermute | solution.py:547
  12.1 0.7 %collective-permute-start.3 = (f32[192,128]{1,0:T(8,128)S(1)}, f32[192,128]{1,0:T(8,128)S(1)}, u32[]{:S(2)}, u32[]{:S(2)}) collective-permute-start(f32[192,128]{1,0:T(8,128)S(1)} %get-tuple-element.36), channel_id=1, source_target_pairs={{0,16},{1,17},{2,18},{3,19},{4,20},{5,21},{6,22},{7,23}} | collective-permute-start | bytes 294920 | tf_op jit(solution)/shard_map/ppermute | solution.py:547
  12.8 1.3 %collective-permute-start.2 = (f32[192,128]{1,0:T(8,128)S(1)}, f32[192,128]{1,0:T(8,128)S(1)}, u32[]{:S(2)}, u32[]{:S(2)}) collective-permute-start(f32[192,128]{1,0:T(8,128)S(1)} %get-tuple-element.36), channel_id=1, source_target_pairs={{0,8},{1,9},{2,10},{3,11},{4,12},{5,13},{6,14},{7,15}} | collective-permute-start | bytes 294920 | tf_op jit(solution)/shard_map/ppermute | solution.py:547
  14.1 0.0 collective-permute-done.4
  14.1 0.0 collective-permute-done.3
  14.1 7.2 %collective-permute-done.2 = f32[192,128]{1,0:T(8,128)S(1)} collective-permute-done((f32[192,128]{1,0:T(8,128)S(1)}, f32[192,128]{1,0:T(8,128)S(1)}, u32[]{:S(2)}, u32[]{:S(2)}) %collective-permute-start.2) | collective-permute-done | bytes 98336 | tf_op jit(solution)/shard_map/ppermute | solution.py:547
  21.3 1.8 %shard_map.49 = (f32[5,64,128]{2,1,0:T(8,128)S(1)}, f32[5,64,128]{2,1,0:T(8,128)S(1)}) custom-call(bf16[144,288]{1,0:T(8,128)(2,1)S(1)} %get-tuple-element.23.refs_0_, bf16[128,256]{1,0:T(8,128)(2,1)S(1)} %get-tuple-element.24.refs_1_, bf16[112,224]{1,0:T(8,128)(2,1)S(1)} %get-tuple-element.25.refs_2_, bf16[96,192]{1,0:T(8,128)(2,1)S(1)} %get-tuple-element.26.refs_3_, ...), custom_call_target="tpu_custom_call" | custom-call | flops 4000000000 | bytes 2097152 | tf_op jit(solution)/shard_map/pallas_call | solution.py:478
  23.1 0.8 %collective-permute-start.5 = (f32[5,64,128]{2,1,0:T(8,128)S(1)}, f32[5,64,128]{2,1,0:T(8,128)S(1)}, u32[]{:S(2)}, u32[]{:S(2)}) collective-permute-start(f32[5,64,128]{2,1,0:T(8,128)S(1)} %get-tuple-element.40), channel_id=1, source_target_pairs={{0,1},{1,0},{2,3},{3,2},{4,5},{5,4},{6,7},{7,6},{8,9},{9,8},{10,11... | collective-permute-start | bytes 491528 | tf_op jit(solution)/shard_map/ppermute | solution.py:555
  23.9 1.0 %collective-permute-done.5.swapped = f32[5,64,128]{2,1,0:T(8,128)S(1)} collective-permute-done((f32[5,64,128]{2,1,0:T(8,128)S(1)}, f32[5,64,128]{2,1,0:T(8,128)S(1)}, u32[]{:S(2)}, u32[]{:S(2)}) %collective-permute-start.5) | collective-permute-done | bytes 163872 | tf_op jit(solution)/shard_map/ppermute | solution.py:555
  25.0 0.7 %shard_map.50 = f32[5,128,128]{2,1,0:T(8,128)} custom-call(f32[5,64,128]{2,1,0:T(8,128)S(1)} %get-tuple-element.39.held, f32[5,64,128]{2,1,0:T(8,128)S(1)} %collective-permute-done.5.swapped), custom_call_target="tpu_custom_call" | custom-call | flops 1000 | bytes 2097152 | tf_op jit(solution)/shard_map/pallas_call | solution.py:478
  (2 shorter events, 0.1 us)
Async XLA Ops:
  1.1 8.4 %copy-start = (s32[16]{0:T(128)S(1)}, s32[16]{0:T(128)}, u32[]{:S(2)}) copy-start(s32[16]{0:T(128)} %param.6) | copy-start | bytes 196
  1.1 8.4 %copy-start.1 = (s32[3]{0:T(128)S(1)}, s32[3]{0:T(128)}, u32[]{:S(2)}) copy-start(s32[3]{0:T(128)} %param.7) | copy-start | bytes 40
  1.1 8.9 %collective-permute-start = (f32[288,128]{1,0:T(8,128)S(1)}, f32[288,128]{1,0:T(8,128)S(1)}, u32[]{:S(2)}, u32[]{:S(2)}) collective-permute-start(f32[288,128]{1,0:T(8,128)S(1)} %get-tuple-element.32), channel_id=1, source_target_pairs={{1,2},{3,4},{2,1},{5,6},{4,3},{6,5},{9,10},{11,12},{10,9},{13,14},... | collective-permute-start | bytes 442376 | tf_op jit(solution)/shard_map/ppermute | solution.py:525
  4.9 5.9 %collective-permute-start.1 = (f32[288,128]{1,0:T(8,128)S(1)}, f32[288,128]{1,0:T(8,128)S(1)}, u32[]{:S(2)}, u32[]{:S(2)}) collective-permute-start(f32[288,128]{1,0:T(8,128)S(1)} %get-tuple-element.33), channel_id=1, source_target_pairs={{0,2},{2,4},{3,1},{4,6},{5,3},{7,5},{8,10},{10,12},{11,9},{12,14},... | collective-permute-start | bytes 442376 | tf_op jit(solution)/shard_map/ppermute | solution.py:526
  11.4 2.7 %collective-permute-start.4 = (f32[192,128]{1,0:T(8,128)S(1)}, f32[192,128]{1,0:T(8,128)S(1)}, u32[]{:S(2)}, u32[]{:S(2)}) collective-permute-start(f32[192,128]{1,0:T(8,128)S(1)} %get-tuple-element.36), channel_id=1, source_target_pairs={{0,24},{1,25},{2,26},{3,27},{4,28},{5,29},{6,30},{7,31}} | collective-permute-start | bytes 294920 | tf_op jit(solution)/shard_map/ppermute | solution.py:547
  12.1 2.0 %collective-permute-start.3 = (f32[192,128]{1,0:T(8,128)S(1)}, f32[192,128]{1,0:T(8,128)S(1)}, u32[]{:S(2)}, u32[]{:S(2)}) collective-permute-start(f32[192,128]{1,0:T(8,128)S(1)} %get-tuple-element.36), channel_id=1, source_target_pairs={{0,16},{1,17},{2,18},{3,19},{4,20},{5,21},{6,22},{7,23}} | collective-permute-start | bytes 294920 | tf_op jit(solution)/shard_map/ppermute | solution.py:547
  12.8 8.6 %collective-permute-start.2 = (f32[192,128]{1,0:T(8,128)S(1)}, f32[192,128]{1,0:T(8,128)S(1)}, u32[]{:S(2)}, u32[]{:S(2)}) collective-permute-start(f32[192,128]{1,0:T(8,128)S(1)} %get-tuple-element.36), channel_id=1, source_target_pairs={{0,8},{1,9},{2,10},{3,11},{4,12},{5,13},{6,14},{7,15}} | collective-permute-start | bytes 294920 | tf_op jit(solution)/shard_map/ppermute | solution.py:547
  23.1 1.8 %collective-permute-start.5 = (f32[5,64,128]{2,1,0:T(8,128)S(1)}, f32[5,64,128]{2,1,0:T(8,128)S(1)}, u32[]{:S(2)}, u32[]{:S(2)}) collective-permute-start(f32[5,64,128]{2,1,0:T(8,128)S(1)} %get-tuple-element.40), channel_id=1, source_target_pairs={{0,1},{1,0},{2,3},{3,2},{4,5},{5,4},{6,7},{7,6},{8,9},{9,8},{10,11... | collective-permute-start | bytes 491528 | tf_op jit(solution)/shard_map/ppermute | solution.py:555

commit v10 on v9

--- a/solution.py
+++ b/solution.py
@@ -544,7 +544,8 @@
         [*bands, pick, block, behind, ahead, other],
         4_000_000_000,
     )
-    arrived = [lax.ppermute(rows, "sec", [(0, target)]) for target in (1, 2, 3)]
+    routes = ([(0, 4), (1, 3)], [(0, 2), (1, 5)], [(0, 6), (1, 7)])
+    arrived = [lax.ppermute(rows, ("sec", "gz"), route) for route in routes]
     rows = arrived[0] + arrived[1] + arrived[2]
     held, sent = call(
         second_kernel,

time: 25.9 us -> 25.3 us (0.977)
  starting transfers between devices: 9.29 us -> 8.64 us
    ppermute x1, starting transfers between devices: 0.82 us -> 0.17 us  [local_window(): swapped = lax.ppermute(sent, 'gz', turn)]
    ppermute x3, waiting for transfers between devices: 7.24 us -> 6.81 us  [local_window(): arrived = [lax.ppermute(rows, ('sec', 'gz'), route) for route in routes]]
    ppermute x1, waiting for transfers between devices: 1.03 us -> 1.29 us  [local_window(): swapped = lax.ppermute(sent, 'gz', turn)]
where the time goes in v10:
time: 25.3 us; the launch traced here: 24.9 us
  waiting for transfers between devices  8.84 us (35%)
  starting transfers between devices  8.64 us (34%)
  Pallas kernels  4.79 us (19%)
  blocking collectives  2.42 us (10%)
    ppermute x3, waiting for transfers between devices, local_window(): arrived = [lax.ppermute(rows, ('sec', 'gz'), route) for route in routes]  6.81 us
    pallas_call x5, Pallas kernels, call(): pl.pallas_call(kernel, out_shape=outs, in_specs=[pl.BlockSpec(memory_spac...  4.79 us
    ppermute x1, starting transfers between devices, local_window(): behind = lax.ppermute(crossed, ('gx', 'gz'), crossed_pairs)  3.77 us
    ppermute x3, starting transfers between devices, local_window(): arrived = [lax.ppermute(rows, ('sec', 'gz'), route) for route in routes]  2.63 us
    all_gather x1, blocking collectives, local_window(): joined = lax.all_gather(swap, 'gz')  2.42 us
    ppermute x1, starting transfers between devices, local_window(): ahead = lax.ppermute(straight, ('gx', 'gz'), straight_pairs)  2.08 us
    ppermute x1, waiting for transfers between devices, local_window(): swapped = lax.ppermute(sent, 'gz', turn)  1.29 us
    ppermute x1, waiting for transfers between devices, local_window(): ahead = lax.ppermute(straight, ('gx', 'gz'), straight_pairs)  0.74 us
  transfers between devices with their start and end apart: 6, of which 3 were waited for; matrix products, arithmetic and copies ran while one was open for 0% of the time, Pallas kernels for 2%

profile of v10, /device:TPU:19, one launch (start us, length us, event | category | flops | bytes accessed | tf_op | source)
XLA Modules:
  0.0 24.9 jit_solution(14601322026262913154)
XLA Ops:
  0.0 1.1 %shard_map.47 = (f32[8,128,128]{2,1,0:T(8,128)S(1)}, f32[288,128]{1,0:T(8,128)S(1)}, f32[288,128]{1,0:T(8,128)S(1)}, f32[8,104,128]{2,1,0:T(8,128)S(1)}) custom-call(f32[5,128,128]{2,1,0:T(8,128)} %bitcast.7, f32[3,128,128]{2,1,0:T(8,128)} %bitcast.8), custom_call_target="tpu_custom_call" | custom-call | flops 1000 | bytes 2097152 | tf_op jit(solution)/shard_map/pallas_call | solution.py:478
  1.1 0.0 copy-start
  1.1 0.0 copy-start.1
  1.1 3.8 %collective-permute-start = (f32[288,128]{1,0:T(8,128)S(1)}, f32[288,128]{1,0:T(8,128)S(1)}, u32[]{:S(2)}, u32[]{:S(2)}) collective-permute-start(f32[288,128]{1,0:T(8,128)S(1)} %get-tuple-element.32), channel_id=1, source_target_pairs={{1,2},{3,4},{2,1},{5,6},{4,3},{6,5},{9,10},{11,12},{10,9},{13,14},... | collective-permute-start | bytes 442376 | tf_op jit(solution)/shard_map/ppermute | solution.py:525
  4.9 2.1 %collective-permute-start.1 = (f32[288,128]{1,0:T(8,128)S(1)}, f32[288,128]{1,0:T(8,128)S(1)}, u32[]{:S(2)}, u32[]{:S(2)}) collective-permute-start(f32[288,128]{1,0:T(8,128)S(1)} %get-tuple-element.33), channel_id=1, source_target_pairs={{0,2},{2,4},{3,1},{4,6},{5,3},{7,5},{8,10},{10,12},{11,9},{12,14},... | collective-permute-start | bytes 442376 | tf_op jit(solution)/shard_map/ppermute | solution.py:526
  7.0 2.4 %all-gather = f32[16,104,128]{2,1,0:T(8,128)S(1)} all-gather(f32[8,104,128]{2,1,0:T(8,128)S(1)} %get-tuple-element.34), channel_id=2, replica_groups=mesh['sec'=4,'gx'=4,'gz'=2] {'gz'}, dimensions={0}, use_global_device_ids=true | all-gather | bytes 1277952 | tf_op jit(solution)/shard_map/all_gather | solution.py:527
  9.5 0.0 copy-done
  9.5 0.0 copy-done.1
  9.5 0.6 %shard_map.46 = (bf16[144,288]{1,0:T(8,128)(2,1)S(1)}, bf16[128,256]{1,0:T(8,128)(2,1)S(1)}, bf16[112,224]{1,0:T(8,128)(2,1)S(1)}, bf16[96,192]{1,0:T(8,128)(2,1...) custom-call(s32[1,16]{1,0:T(1,128)S(1)} %bitcast.5, ...), custom_call_target="tpu_custom_call" | custom-call | flops 1000000000 | bytes 2097152 | tf_op jit(solution)/shard_map/pallas_call | solution.py:478
  10.0 0.0 collective-permute-done.refs_8_
  10.0 0.7 %collective-permute-done.1.refs_9_ = f32[288,128]{1,0:T(8,128)S(1)} collective-permute-done((f32[288,128]{1,0:T(8,128)S(1)}, f32[288,128]{1,0:T(8,128)S(1)}, u32[]{:S(2)}, u32[]{:S(2)}) %collective-permute-start.1) | collective-permute-done | bytes 147488 | tf_op jit(solution)/shard_map/ppermute | solution.py:526
  10.8 0.6 %shard_map.48 = (f32[5,64,128]{2,1,0:T(8,128)S(1)}, f32[5,64,128]{2,1,0:T(8,128)S(1)}, f32[192,128]{1,0:T(8,128)S(1)}, f32[9,144,256]{2,1,0:T(8,128)S(1)}) custom-call(bf16[144,288]{1,0:T(8,128)(2,1)S(1)} %get-tuple-element.23.refs_0_, bf16[128,256]{1,0:T(8,128)(2,1)S(1)} %get-tuple-element.24.refs_1_, bf16[112,224]{1,0:T(8,128)(2,1)S(1)} %get-tuple-element.25.refs_2_, ...), custom_call_target="tpu_custom_call" | custom-call | flops 4000000000 | bytes 2097152 | tf_op jit(solution)/shard_map/pallas_call | solution.py:478
  11.4 0.7 %collective-permute-start.4 = (f32[192,128]{1,0:T(8,128)S(1)}, f32[192,128]{1,0:T(8,128)S(1)}, u32[]{:S(2)}, u32[]{:S(2)}) collective-permute-start(f32[192,128]{1,0:T(8,128)S(1)} %get-tuple-element.36), channel_id=1, source_target_pairs={{0,24},{1,25},{2,26},{3,27},{4,28},{5,29},{6,30},{7,31}} | collective-permute-start | bytes 294920 | tf_op jit(solution)/shard_map/ppermute | solution.py:548
  12.1 0.7 %collective-permute-start.3 = (f32[192,128]{1,0:T(8,128)S(1)}, f32[192,128]{1,0:T(8,128)S(1)}, u32[]{:S(2)}, u32[]{:S(2)}) collective-permute-start(f32[192,128]{1,0:T(8,128)S(1)} %get-tuple-element.36), channel_id=1, source_target_pairs={{0,8},{1,17},{2,10},{3,19},{4,12},{5,21},{6,14},{7,23}} | collective-permute-start | bytes 294920 | tf_op jit(solution)/shard_map/ppermute | solution.py:548
  12.8 1.3 %collective-permute-start.2 = (f32[192,128]{1,0:T(8,128)S(1)}, f32[192,128]{1,0:T(8,128)S(1)}, u32[]{:S(2)}, u32[]{:S(2)}) collective-permute-start(f32[192,128]{1,0:T(8,128)S(1)} %get-tuple-element.36), channel_id=1, source_target_pairs={{0,16},{1,9},{2,18},{3,11},{4,20},{5,13},{6,22},{7,15}} | collective-permute-start | bytes 294920 | tf_op jit(solution)/shard_map/ppermute | solution.py:548
  14.1 0.0 collective-permute-done.4
  14.1 0.0 collective-permute-done.3
  14.1 6.8 %collective-permute-done.2 = f32[192,128]{1,0:T(8,128)S(1)} collective-permute-done((f32[192,128]{1,0:T(8,128)S(1)}, f32[192,128]{1,0:T(8,128)S(1)}, u32[]{:S(2)}, u32[]{:S(2)}) %collective-permute-start.2) | collective-permute-done | bytes 98336 | tf_op jit(solution)/shard_map/ppermute | solution.py:548
  20.9 1.8 %shard_map.49 = (f32[5,64,128]{2,1,0:T(8,128)S(1)}, f32[5,64,128]{2,1,0:T(8,128)S(1)}) custom-call(bf16[144,288]{1,0:T(8,128)(2,1)S(1)} %get-tuple-element.23.refs_0_, bf16[128,256]{1,0:T(8,128)(2,1)S(1)} %get-tuple-element.24.refs_1_, bf16[112,224]{1,0:T(8,128)(2,1)S(1)} %get-tuple-element.25.refs_2_, bf16[96,192]{1,0:T(8,128)(2,1)S(1)} %get-tuple-element.26.refs_3_, ...), custom_call_target="tpu_custom_call" | custom-call | flops 4000000000 | bytes 2097152 | tf_op jit(solution)/shard_map/pallas_call | solution.py:478
  22.7 0.2 collective-permute-start.5
  22.9 1.3 %collective-permute-done.5.swapped = f32[5,64,128]{2,1,0:T(8,128)S(1)} collective-permute-done((f32[5,64,128]{2,1,0:T(8,128)S(1)}, f32[5,64,128]{2,1,0:T(8,128)S(1)}, u32[]{:S(2)}, u32[]{:S(2)}) %collective-permute-start.5) | collective-permute-done | bytes 163872 | tf_op jit(solution)/shard_map/ppermute | solution.py:556
  24.2 0.7 %shard_map.50 = f32[5,128,128]{2,1,0:T(8,128)} custom-call(f32[5,64,128]{2,1,0:T(8,128)S(1)} %get-tuple-element.39.held, f32[5,64,128]{2,1,0:T(8,128)S(1)} %collective-permute-done.5.swapped), custom_call_target="tpu_custom_call" | custom-call | flops 1000 | bytes 2097152 | tf_op jit(solution)/shard_map/pallas_call | solution.py:478
  (2 shorter events, 0.1 us)
Async XLA Ops:
  1.1 8.4 %copy-start = (s32[16]{0:T(128)S(1)}, s32[16]{0:T(128)}, u32[]{:S(2)}) copy-start(s32[16]{0:T(128)} %param.6) | copy-start | bytes 196
  1.1 8.4 %copy-start.1 = (s32[3]{0:T(128)S(1)}, s32[3]{0:T(128)}, u32[]{:S(2)}) copy-start(s32[3]{0:T(128)} %param.7) | copy-start | bytes 40
  1.1 8.9 %collective-permute-start = (f32[288,128]{1,0:T(8,128)S(1)}, f32[288,128]{1,0:T(8,128)S(1)}, u32[]{:S(2)}, u32[]{:S(2)}) collective-permute-start(f32[288,128]{1,0:T(8,128)S(1)} %get-tuple-element.32), channel_id=1, source_target_pairs={{1,2},{3,4},{2,1},{5,6},{4,3},{6,5},{9,10},{11,12},{10,9},{13,14},... | collective-permute-start | bytes 442376 | tf_op jit(solution)/shard_map/ppermute | solution.py:525
  4.9 5.9 %collective-permute-start.1 = (f32[288,128]{1,0:T(8,128)S(1)}, f32[288,128]{1,0:T(8,128)S(1)}, u32[]{:S(2)}, u32[]{:S(2)}) collective-permute-start(f32[288,128]{1,0:T(8,128)S(1)} %get-tuple-element.33), channel_id=1, source_target_pairs={{0,2},{2,4},{3,1},{4,6},{5,3},{7,5},{8,10},{10,12},{11,9},{12,14},... | collective-permute-start | bytes 442376 | tf_op jit(solution)/shard_map/ppermute | solution.py:526
  11.4 2.7 %collective-permute-start.4 = (f32[192,128]{1,0:T(8,128)S(1)}, f32[192,128]{1,0:T(8,128)S(1)}, u32[]{:S(2)}, u32[]{:S(2)}) collective-permute-start(f32[192,128]{1,0:T(8,128)S(1)} %get-tuple-element.36), channel_id=1, source_target_pairs={{0,24},{1,25},{2,26},{3,27},{4,28},{5,29},{6,30},{7,31}} | collective-permute-start | bytes 294920 | tf_op jit(solution)/shard_map/ppermute | solution.py:548
  12.1 2.0 %collective-permute-start.3 = (f32[192,128]{1,0:T(8,128)S(1)}, f32[192,128]{1,0:T(8,128)S(1)}, u32[]{:S(2)}, u32[]{:S(2)}) collective-permute-start(f32[192,128]{1,0:T(8,128)S(1)} %get-tuple-element.36), channel_id=1, source_target_pairs={{0,8},{1,17},{2,10},{3,19},{4,12},{5,21},{6,14},{7,23}} | collective-permute-start | bytes 294920 | tf_op jit(solution)/shard_map/ppermute | solution.py:548
  12.8 8.1 %collective-permute-start.2 = (f32[192,128]{1,0:T(8,128)S(1)}, f32[192,128]{1,0:T(8,128)S(1)}, u32[]{:S(2)}, u32[]{:S(2)}) collective-permute-start(f32[192,128]{1,0:T(8,128)S(1)} %get-tuple-element.36), channel_id=1, source_target_pairs={{0,16},{1,9},{2,18},{3,11},{4,20},{5,13},{6,22},{7,15}} | collective-permute-start | bytes 294920 | tf_op jit(solution)/shard_map/ppermute | solution.py:548
  22.7 1.5 %collective-permute-start.5 = (f32[5,64,128]{2,1,0:T(8,128)S(1)}, f32[5,64,128]{2,1,0:T(8,128)S(1)}, u32[]{:S(2)}, u32[]{:S(2)}) collective-permute-start(f32[5,64,128]{2,1,0:T(8,128)S(1)} %get-tuple-element.40), channel_id=1, source_target_pairs={{0,1},{1,0},{2,3},{3,2},{4,5},{5,4},{6,7},{7,6},{8,9},{9,8},{10,11... | collective-permute-start | bytes 491528 | tf_op jit(solution)/shard_map/ppermute | solution.py:556

commit v11 on v10

--- a/solution.py
+++ b/solution.py
@@ -544,7 +544,7 @@
         [*bands, pick, block, behind, ahead, other],
         4_000_000_000,
     )
-    routes = ([(0, 4), (1, 3)], [(0, 2), (1, 5)], [(0, 6), (1, 7)])
+    routes = ([(0, 4), (1, 3)], [(0, 6), (1, 7)], [(0, 2), (1, 5)])
     arrived = [lax.ppermute(rows, ("sec", "gz"), route) for route in routes]
     rows = arrived[0] + arrived[1] + arrived[2]
     held, sent = call(

time: 25.3 us -> 24.9 us (0.984)
  no operation moved by 1% of the time
where the time goes in v11:
time: 24.9 us; the launch traced here: 24.7 us
  waiting for transfers between devices  8.71 us (35%)
  starting transfers between devices  8.54 us (34%)
  Pallas kernels  4.79 us (19%)
  blocking collectives  2.42 us (10%)
    ppermute x3, waiting for transfers between devices, local_window(): arrived = [lax.ppermute(rows, ('sec', 'gz'), route) for route in routes]  6.59 us
    pallas_call x5, Pallas kernels, call(): pl.pallas_call(kernel, out_shape=outs, in_specs=[pl.BlockSpec(memory_spac...  4.79 us
    ppermute x1, starting transfers between devices, local_window(): behind = lax.ppermute(crossed, ('gx', 'gz'), crossed_pairs)  3.77 us
    ppermute x3, starting transfers between devices, local_window(): arrived = [lax.ppermute(rows, ('sec', 'gz'), route) for route in routes]  2.63 us
    all_gather x1, blocking collectives, local_window(): joined = lax.all_gather(swap, 'gz')  2.42 us
    ppermute x1, starting transfers between devices, local_window(): ahead = lax.ppermute(straight, ('gx', 'gz'), straight_pairs)  2.08 us
    ppermute x1, waiting for transfers between devices, local_window(): swapped = lax.ppermute(sent, 'gz', turn)  1.38 us
    ppermute x1, waiting for transfers between devices, local_window(): ahead = lax.ppermute(straight, ('gx', 'gz'), straight_pairs)  0.74 us
  transfers between devices with their start and end apart: 6, of which 3 were waited for; matrix products, arithmetic and copies ran while one was open for 0% of the time, Pallas kernels for 2%

profile of v11, /device:TPU:19, one launch (start us, length us, event | category | flops | bytes accessed | tf_op | source)
XLA Modules:
  0.0 24.7 jit_solution(970285597533450898)
XLA Ops:
  0.0 1.1 %shard_map.47 = (f32[8,128,128]{2,1,0:T(8,128)S(1)}, f32[288,128]{1,0:T(8,128)S(1)}, f32[288,128]{1,0:T(8,128)S(1)}, f32[8,104,128]{2,1,0:T(8,128)S(1)}) custom-call(f32[5,128,128]{2,1,0:T(8,128)} %bitcast.7, f32[3,128,128]{2,1,0:T(8,128)} %bitcast.8), custom_call_target="tpu_custom_call" | custom-call | flops 1000 | bytes 2097152 | tf_op jit(solution)/shard_map/pallas_call | solution.py:478
  1.1 0.0 copy-start
  1.1 0.0 copy-start.1
  1.1 3.8 %collective-permute-start = (f32[288,128]{1,0:T(8,128)S(1)}, f32[288,128]{1,0:T(8,128)S(1)}, u32[]{:S(2)}, u32[]{:S(2)}) collective-permute-start(f32[288,128]{1,0:T(8,128)S(1)} %get-tuple-element.32), channel_id=1, source_target_pairs={{1,2},{3,4},{2,1},{5,6},{4,3},{6,5},{9,10},{11,12},{10,9},{13,14},... | collective-permute-start | bytes 442376 | tf_op jit(solution)/shard_map/ppermute | solution.py:525
  4.9 2.1 %collective-permute-start.1 = (f32[288,128]{1,0:T(8,128)S(1)}, f32[288,128]{1,0:T(8,128)S(1)}, u32[]{:S(2)}, u32[]{:S(2)}) collective-permute-start(f32[288,128]{1,0:T(8,128)S(1)} %get-tuple-element.33), channel_id=1, source_target_pairs={{0,2},{2,4},{3,1},{4,6},{5,3},{7,5},{8,10},{10,12},{11,9},{12,14},... | collective-permute-start | bytes 442376 | tf_op jit(solution)/shard_map/ppermute | solution.py:526
  7.0 2.4 %all-gather = f32[16,104,128]{2,1,0:T(8,128)S(1)} all-gather(f32[8,104,128]{2,1,0:T(8,128)S(1)} %get-tuple-element.34), channel_id=2, replica_groups=mesh['sec'=4,'gx'=4,'gz'=2] {'gz'}, dimensions={0}, use_global_device_ids=true | all-gather | bytes 1277952 | tf_op jit(solution)/shard_map/all_gather | solution.py:527
  9.5 0.0 copy-done
  9.5 0.0 copy-done.1
  9.5 0.6 %shard_map.46 = (bf16[144,288]{1,0:T(8,128)(2,1)S(1)}, bf16[128,256]{1,0:T(8,128)(2,1)S(1)}, bf16[112,224]{1,0:T(8,128)(2,1)S(1)}, bf16[96,192]{1,0:T(8,128)(2,1...) custom-call(s32[1,16]{1,0:T(1,128)S(1)} %bitcast.5, ...), custom_call_target="tpu_custom_call" | custom-call | flops 1000000000 | bytes 2097152 | tf_op jit(solution)/shard_map/pallas_call | solution.py:478
  10.0 0.0 collective-permute-done.refs_8_
  10.0 0.7 %collective-permute-done.1.refs_9_ = f32[288,128]{1,0:T(8,128)S(1)} collective-permute-done((f32[288,128]{1,0:T(8,128)S(1)}, f32[288,128]{1,0:T(8,128)S(1)}, u32[]{:S(2)}, u32[]{:S(2)}) %collective-permute-start.1) | collective-permute-done | bytes 147488 | tf_op jit(solution)/shard_map/ppermute | solution.py:526
  10.8 0.6 %shard_map.48 = (f32[5,64,128]{2,1,0:T(8,128)S(1)}, f32[5,64,128]{2,1,0:T(8,128)S(1)}, f32[192,128]{1,0:T(8,128)S(1)}, f32[9,144,256]{2,1,0:T(8,128)S(1)}) custom-call(bf16[144,288]{1,0:T(8,128)(2,1)S(1)} %get-tuple-element.23.refs_0_, bf16[128,256]{1,0:T(8,128)(2,1)S(1)} %get-tuple-element.24.refs_1_, bf16[112,224]{1,0:T(8,128)(2,1)S(1)} %get-tuple-element.25.refs_2_, ...), custom_call_target="tpu_custom_call" | custom-call | flops 4000000000 | bytes 2097152 | tf_op jit(solution)/shard_map/pallas_call | solution.py:478
  11.4 0.7 %collective-permute-start.4 = (f32[192,128]{1,0:T(8,128)S(1)}, f32[192,128]{1,0:T(8,128)S(1)}, u32[]{:S(2)}, u32[]{:S(2)}) collective-permute-start(f32[192,128]{1,0:T(8,128)S(1)} %get-tuple-element.36), channel_id=1, source_target_pairs={{0,8},{1,17},{2,10},{3,19},{4,12},{5,21},{6,14},{7,23}} | collective-permute-start | bytes 294920 | tf_op jit(solution)/shard_map/ppermute | solution.py:548
  12.1 0.7 %collective-permute-start.3 = (f32[192,128]{1,0:T(8,128)S(1)}, f32[192,128]{1,0:T(8,128)S(1)}, u32[]{:S(2)}, u32[]{:S(2)}) collective-permute-start(f32[192,128]{1,0:T(8,128)S(1)} %get-tuple-element.36), channel_id=1, source_target_pairs={{0,24},{1,25},{2,26},{3,27},{4,28},{5,29},{6,30},{7,31}} | collective-permute-start | bytes 294920 | tf_op jit(solution)/shard_map/ppermute | solution.py:548
  12.8 1.3 %collective-permute-start.2 = (f32[192,128]{1,0:T(8,128)S(1)}, f32[192,128]{1,0:T(8,128)S(1)}, u32[]{:S(2)}, u32[]{:S(2)}) collective-permute-start(f32[192,128]{1,0:T(8,128)S(1)} %get-tuple-element.36), channel_id=1, source_target_pairs={{0,16},{1,9},{2,18},{3,11},{4,20},{5,13},{6,22},{7,15}} | collective-permute-start | bytes 294920 | tf_op jit(solution)/shard_map/ppermute | solution.py:548
  14.1 0.0 collective-permute-done.4
  14.1 0.0 collective-permute-done.3
  14.1 6.6 %collective-permute-done.2 = f32[192,128]{1,0:T(8,128)S(1)} collective-permute-done((f32[192,128]{1,0:T(8,128)S(1)}, f32[192,128]{1,0:T(8,128)S(1)}, u32[]{:S(2)}, u32[]{:S(2)}) %collective-permute-start.2) | collective-permute-done | bytes 98336 | tf_op jit(solution)/shard_map/ppermute | solution.py:548
  20.7 1.8 %shard_map.49 = (f32[5,64,128]{2,1,0:T(8,128)S(1)}, f32[5,64,128]{2,1,0:T(8,128)S(1)}) custom-call(bf16[144,288]{1,0:T(8,128)(2,1)S(1)} %get-tuple-element.23.refs_0_, bf16[128,256]{1,0:T(8,128)(2,1)S(1)} %get-tuple-element.24.refs_1_, bf16[112,224]{1,0:T(8,128)(2,1)S(1)} %get-tuple-element.25.refs_2_, bf16[96,192]{1,0:T(8,128)(2,1)S(1)} %get-tuple-element.26.refs_3_, ...), custom_call_target="tpu_custom_call" | custom-call | flops 4000000000 | bytes 2097152 | tf_op jit(solution)/shard_map/pallas_call | solution.py:478
  22.5 0.1 collective-permute-start.5
  22.6 1.4 %collective-permute-done.5.swapped = f32[5,64,128]{2,1,0:T(8,128)S(1)} collective-permute-done((f32[5,64,128]{2,1,0:T(8,128)S(1)}, f32[5,64,128]{2,1,0:T(8,128)S(1)}, u32[]{:S(2)}, u32[]{:S(2)}) %collective-permute-start.5) | collective-permute-done | bytes 163872 | tf_op jit(solution)/shard_map/ppermute | solution.py:556
  23.9 0.7 %shard_map.50 = f32[5,128,128]{2,1,0:T(8,128)} custom-call(f32[5,64,128]{2,1,0:T(8,128)S(1)} %get-tuple-element.39.held, f32[5,64,128]{2,1,0:T(8,128)S(1)} %collective-permute-done.5.swapped), custom_call_target="tpu_custom_call" | custom-call | flops 1000 | bytes 2097152 | tf_op jit(solution)/shard_map/pallas_call | solution.py:478
  (2 shorter events, 0.1 us)
Async XLA Ops:
  1.1 8.4 %copy-start = (s32[16]{0:T(128)S(1)}, s32[16]{0:T(128)}, u32[]{:S(2)}) copy-start(s32[16]{0:T(128)} %param.6) | copy-start | bytes 196
  1.1 8.4 %copy-start.1 = (s32[3]{0:T(128)S(1)}, s32[3]{0:T(128)}, u32[]{:S(2)}) copy-start(s32[3]{0:T(128)} %param.7) | copy-start | bytes 40
  1.1 8.9 %collective-permute-start = (f32[288,128]{1,0:T(8,128)S(1)}, f32[288,128]{1,0:T(8,128)S(1)}, u32[]{:S(2)}, u32[]{:S(2)}) collective-permute-start(f32[288,128]{1,0:T(8,128)S(1)} %get-tuple-element.32), channel_id=1, source_target_pairs={{1,2},{3,4},{2,1},{5,6},{4,3},{6,5},{9,10},{11,12},{10,9},{13,14},... | collective-permute-start | bytes 442376 | tf_op jit(solution)/shard_map/ppermute | solution.py:525
  4.9 5.9 %collective-permute-start.1 = (f32[288,128]{1,0:T(8,128)S(1)}, f32[288,128]{1,0:T(8,128)S(1)}, u32[]{:S(2)}, u32[]{:S(2)}) collective-permute-start(f32[288,128]{1,0:T(8,128)S(1)} %get-tuple-element.33), channel_id=1, source_target_pairs={{0,2},{2,4},{3,1},{4,6},{5,3},{7,5},{8,10},{10,12},{11,9},{12,14},... | collective-permute-start | bytes 442376 | tf_op jit(solution)/shard_map/ppermute | solution.py:526
  11.4 2.7 %collective-permute-start.4 = (f32[192,128]{1,0:T(8,128)S(1)}, f32[192,128]{1,0:T(8,128)S(1)}, u32[]{:S(2)}, u32[]{:S(2)}) collective-permute-start(f32[192,128]{1,0:T(8,128)S(1)} %get-tuple-element.36), channel_id=1, source_target_pairs={{0,8},{1,17},{2,10},{3,19},{4,12},{5,21},{6,14},{7,23}} | collective-permute-start | bytes 294920 | tf_op jit(solution)/shard_map/ppermute | solution.py:548
  12.1 2.0 %collective-permute-start.3 = (f32[192,128]{1,0:T(8,128)S(1)}, f32[192,128]{1,0:T(8,128)S(1)}, u32[]{:S(2)}, u32[]{:S(2)}) collective-permute-start(f32[192,128]{1,0:T(8,128)S(1)} %get-tuple-element.36), channel_id=1, source_target_pairs={{0,24},{1,25},{2,26},{3,27},{4,28},{5,29},{6,30},{7,31}} | collective-permute-start | bytes 294920 | tf_op jit(solution)/shard_map/ppermute | solution.py:548
  12.8 7.9 %collective-permute-start.2 = (f32[192,128]{1,0:T(8,128)S(1)}, f32[192,128]{1,0:T(8,128)S(1)}, u32[]{:S(2)}, u32[]{:S(2)}) collective-permute-start(f32[192,128]{1,0:T(8,128)S(1)} %get-tuple-element.36), channel_id=1, source_target_pairs={{0,16},{1,9},{2,18},{3,11},{4,20},{5,13},{6,22},{7,15}} | collective-permute-start | bytes 294920 | tf_op jit(solution)/shard_map/ppermute | solution.py:548
  22.5 1.5 %collective-permute-start.5 = (f32[5,64,128]{2,1,0:T(8,128)S(1)}, f32[5,64,128]{2,1,0:T(8,128)S(1)}, u32[]{:S(2)}, u32[]{:S(2)}) collective-permute-start(f32[5,64,128]{2,1,0:T(8,128)S(1)} %get-tuple-element.40), channel_id=1, source_target_pairs={{0,1},{1,0},{2,3},{3,2},{4,5},{5,4},{6,7},{7,6},{8,9},{9,8},{10,11... | collective-permute-start | bytes 491528 | tf_op jit(solution)/shard_map/ppermute | solution.py:556

commit v12 on v11

--- a/solution.py
+++ b/solution.py
@@ -544,7 +544,7 @@
         [*bands, pick, block, behind, ahead, other],
         4_000_000_000,
     )
-    routes = ([(0, 4), (1, 3)], [(0, 6), (1, 7)], [(0, 2), (1, 5)])
+    routes = ([(0, 2), (1, 5)], [(0, 6), (1, 7)], [(0, 4), (1, 3)])
     arrived = [lax.ppermute(rows, ("sec", "gz"), route) for route in routes]
     rows = arrived[0] + arrived[1] + arrived[2]
     held, sent = call(

time: 24.9 us -> 25.2 us (1.012)
  starting transfers between devices: 8.54 us -> 12.6 us
  waiting for transfers between devices: 8.71 us -> 4.97 us
    ppermute x1, starting transfers between devices: 0.07 us -> 4.15 us  [local_window(): swapped = lax.ppermute(sent, 'gz', turn)]
    ppermute x3, waiting for transfers between devices: 6.59 us -> 3.2 us  [local_window(): arrived = [lax.ppermute(rows, ('sec', 'gz'), route) for route in routes]]
    ppermute x1, waiting for transfers between devices: 1.38 us -> 1.03 us  [local_window(): swapped = lax.ppermute(sent, 'gz', turn)]
where the time goes in v12:
time: 25.2 us; the launch traced here: 25 us
  starting transfers between devices  12.6 us (50%)
  waiting for transfers between devices  4.97 us (20%)
  Pallas kernels  4.78 us (19%)
  blocking collectives  2.42 us (10%)
    pallas_call x5, Pallas kernels, call(): pl.pallas_call(kernel, out_shape=outs, in_specs=[pl.BlockSpec(memory_spac...  4.78 us
    ppermute x1, starting transfers between devices, local_window(): swapped = lax.ppermute(sent, 'gz', turn)  4.15 us
    ppermute x1, starting transfers between devices, local_window(): behind = lax.ppermute(crossed, ('gx', 'gz'), crossed_pairs)  3.77 us
    ppermute x3, waiting for transfers between devices, local_window(): arrived = [lax.ppermute(rows, ('sec', 'gz'), route) for route in routes]  3.2 us
    ppermute x3, starting transfers between devices, local_window(): arrived = [lax.ppermute(rows, ('sec', 'gz'), route) for route in routes]  2.63 us
    all_gather x1, blocking collectives, local_window(): joined = lax.all_gather(swap, 'gz')  2.42 us
    ppermute x1, starting transfers between devices, local_window(): ahead = lax.ppermute(straight, ('gx', 'gz'), straight_pairs)  2.08 us
    ppermute x1, waiting for transfers between devices, local_window(): swapped = lax.ppermute(sent, 'gz', turn)  1.03 us
  transfers between devices with their start and end apart: 6, of which 3 were waited for; matrix products, arithmetic and copies ran while one was open for 0% of the time, Pallas kernels for 2%

profile of v12, /device:TPU:19, one launch (start us, length us, event | category | flops | bytes accessed | tf_op | source)
XLA Modules:
  0.0 25.0 jit_solution(9933631144613649461)
XLA Ops:
  0.0 1.1 %shard_map.47 = (f32[8,128,128]{2,1,0:T(8,128)S(1)}, f32[288,128]{1,0:T(8,128)S(1)}, f32[288,128]{1,0:T(8,128)S(1)}, f32[8,104,128]{2,1,0:T(8,128)S(1)}) custom-call(f32[5,128,128]{2,1,0:T(8,128)} %bitcast.7, f32[3,128,128]{2,1,0:T(8,128)} %bitcast.8), custom_call_target="tpu_custom_call" | custom-call | flops 1000 | bytes 2097152 | tf_op jit(solution)/shard_map/pallas_call | solution.py:478
  1.1 0.0 copy-start
  1.1 0.0 copy-start.1
  1.1 3.8 %collective-permute-start = (f32[288,128]{1,0:T(8,128)S(1)}, f32[288,128]{1,0:T(8,128)S(1)}, u32[]{:S(2)}, u32[]{:S(2)}) collective-permute-start(f32[288,128]{1,0:T(8,128)S(1)} %get-tuple-element.32), channel_id=1, source_target_pairs={{1,2},{3,4},{2,1},{5,6},{4,3},{6,5},{9,10},{11,12},{10,9},{13,14},... | collective-permute-start | bytes 442376 | tf_op jit(solution)/shard_map/ppermute | solution.py:525
  4.9 2.1 %collective-permute-start.1 = (f32[288,128]{1,0:T(8,128)S(1)}, f32[288,128]{1,0:T(8,128)S(1)}, u32[]{:S(2)}, u32[]{:S(2)}) collective-permute-start(f32[288,128]{1,0:T(8,128)S(1)} %get-tuple-element.33), channel_id=1, source_target_pairs={{0,2},{2,4},{3,1},{4,6},{5,3},{7,5},{8,10},{10,12},{11,9},{12,14},... | collective-permute-start | bytes 442376 | tf_op jit(solution)/shard_map/ppermute | solution.py:526
  7.0 2.4 %all-gather = f32[16,104,128]{2,1,0:T(8,128)S(1)} all-gather(f32[8,104,128]{2,1,0:T(8,128)S(1)} %get-tuple-element.34), channel_id=2, replica_groups=mesh['sec'=4,'gx'=4,'gz'=2] {'gz'}, dimensions={0}, use_global_device_ids=true | all-gather | bytes 1277952 | tf_op jit(solution)/shard_map/all_gather | solution.py:527
  9.5 0.0 copy-done
  9.5 0.0 copy-done.1
  9.5 0.6 %shard_map.46 = (bf16[144,288]{1,0:T(8,128)(2,1)S(1)}, bf16[128,256]{1,0:T(8,128)(2,1)S(1)}, bf16[112,224]{1,0:T(8,128)(2,1)S(1)}, bf16[96,192]{1,0:T(8,128)(2,1...) custom-call(s32[1,16]{1,0:T(1,128)S(1)} %bitcast.5, ...), custom_call_target="tpu_custom_call" | custom-call | flops 1000000000 | bytes 2097152 | tf_op jit(solution)/shard_map/pallas_call | solution.py:478
  10.0 0.0 collective-permute-done.refs_8_
  10.0 0.7 %collective-permute-done.1.refs_9_ = f32[288,128]{1,0:T(8,128)S(1)} collective-permute-done((f32[288,128]{1,0:T(8,128)S(1)}, f32[288,128]{1,0:T(8,128)S(1)}, u32[]{:S(2)}, u32[]{:S(2)}) %collective-permute-start.1) | collective-permute-done | bytes 147488 | tf_op jit(solution)/shard_map/ppermute | solution.py:526
  10.8 0.6 %shard_map.48 = (f32[5,64,128]{2,1,0:T(8,128)S(1)}, f32[5,64,128]{2,1,0:T(8,128)S(1)}, f32[192,128]{1,0:T(8,128)S(1)}, f32[9,144,256]{2,1,0:T(8,128)S(1)}) custom-call(bf16[144,288]{1,0:T(8,128)(2,1)S(1)} %get-tuple-element.23.refs_0_, bf16[128,256]{1,0:T(8,128)(2,1)S(1)} %get-tuple-element.24.refs_1_, bf16[112,224]{1,0:T(8,128)(2,1)S(1)} %get-tuple-element.25.refs_2_, ...), custom_call_target="tpu_custom_call" | custom-call | flops 4000000000 | bytes 2097152 | tf_op jit(solution)/shard_map/pallas_call | solution.py:478
  11.4 1.3 %collective-permute-start.4 = (f32[192,128]{1,0:T(8,128)S(1)}, f32[192,128]{1,0:T(8,128)S(1)}, u32[]{:S(2)}, u32[]{:S(2)}) collective-permute-start(f32[192,128]{1,0:T(8,128)S(1)} %get-tuple-element.36), channel_id=1, source_target_pairs={{0,16},{1,9},{2,18},{3,11},{4,20},{5,13},{6,22},{7,15}} | collective-permute-start | bytes 294920 | tf_op jit(solution)/shard_map/ppermute | solution.py:548
  12.7 0.7 %collective-permute-start.3 = (f32[192,128]{1,0:T(8,128)S(1)}, f32[192,128]{1,0:T(8,128)S(1)}, u32[]{:S(2)}, u32[]{:S(2)}) collective-permute-start(f32[192,128]{1,0:T(8,128)S(1)} %get-tuple-element.36), channel_id=1, source_target_pairs={{0,24},{1,25},{2,26},{3,27},{4,28},{5,29},{6,30},{7,31}} | collective-permute-start | bytes 294920 | tf_op jit(solution)/shard_map/ppermute | solution.py:548
  13.4 0.7 %collective-permute-start.2 = (f32[192,128]{1,0:T(8,128)S(1)}, f32[192,128]{1,0:T(8,128)S(1)}, u32[]{:S(2)}, u32[]{:S(2)}) collective-permute-start(f32[192,128]{1,0:T(8,128)S(1)} %get-tuple-element.36), channel_id=1, source_target_pairs={{0,8},{1,17},{2,10},{3,19},{4,12},{5,21},{6,14},{7,23}} | collective-permute-start | bytes 294920 | tf_op jit(solution)/shard_map/ppermute | solution.py:548
  14.1 3.2 %collective-permute-done.4 = f32[192,128]{1,0:T(8,128)S(1)} collective-permute-done((f32[192,128]{1,0:T(8,128)S(1)}, f32[192,128]{1,0:T(8,128)S(1)}, u32[]{:S(2)}, u32[]{:S(2)}) %collective-permute-start.4) | collective-permute-done | bytes 98336 | tf_op jit(solution)/shard_map/ppermute | solution.py:548
  17.2 0.0 collective-permute-done.3
  17.3 0.0 collective-permute-done.2
  17.3 1.8 %shard_map.49 = (f32[5,64,128]{2,1,0:T(8,128)S(1)}, f32[5,64,128]{2,1,0:T(8,128)S(1)}) custom-call(bf16[144,288]{1,0:T(8,128)(2,1)S(1)} %get-tuple-element.23.refs_0_, bf16[128,256]{1,0:T(8,128)(2,1)S(1)} %get-tuple-element.24.refs_1_, bf16[112,224]{1,0:T(8,128)(2,1)S(1)} %get-tuple-element.25.refs_2_, bf16[96,192]{1,0:T(8,128)(2,1)S(1)} %get-tuple-element.26.refs_3_, ...), custom_call_target="tpu_custom_call" | custom-call | flops 4000000000 | bytes 2097152 | tf_op jit(solution)/shard_map/pallas_call | solution.py:478
  19.1 4.1 %collective-permute-start.5 = (f32[5,64,128]{2,1,0:T(8,128)S(1)}, f32[5,64,128]{2,1,0:T(8,128)S(1)}, u32[]{:S(2)}, u32[]{:S(2)}) collective-permute-start(f32[5,64,128]{2,1,0:T(8,128)S(1)} %get-tuple-element.40), channel_id=1, source_target_pairs={{0,1},{1,0},{2,3},{3,2},{4,5},{5,4},{6,7},{7,6},{8,9},{9,8},{10,11... | collective-permute-start | bytes 491528 | tf_op jit(solution)/shard_map/ppermute | solution.py:556
  23.2 1.0 %collective-permute-done.5.swapped = f32[5,64,128]{2,1,0:T(8,128)S(1)} collective-permute-done((f32[5,64,128]{2,1,0:T(8,128)S(1)}, f32[5,64,128]{2,1,0:T(8,128)S(1)}, u32[]{:S(2)}, u32[]{:S(2)}) %collective-permute-start.5) | collective-permute-done | bytes 163872 | tf_op jit(solution)/shard_map/ppermute | solution.py:556
  24.2 0.7 %shard_map.50 = f32[5,128,128]{2,1,0:T(8,128)} custom-call(f32[5,64,128]{2,1,0:T(8,128)S(1)} %get-tuple-element.39.held, f32[5,64,128]{2,1,0:T(8,128)S(1)} %collective-permute-done.5.swapped), custom_call_target="tpu_custom_call" | custom-call | flops 1000 | bytes 2097152 | tf_op jit(solution)/shard_map/pallas_call | solution.py:478
  (2 shorter events, 0.1 us)
Async XLA Ops:
  1.1 8.4 %copy-start = (s32[16]{0:T(128)S(1)}, s32[16]{0:T(128)}, u32[]{:S(2)}) copy-start(s32[16]{0:T(128)} %param.6) | copy-start | bytes 196
  1.1 8.4 %copy-start.1 = (s32[3]{0:T(128)S(1)}, s32[3]{0:T(128)}, u32[]{:S(2)}) copy-start(s32[3]{0:T(128)} %param.7) | copy-start | bytes 40
  1.1 8.9 %collective-permute-start = (f32[288,128]{1,0:T(8,128)S(1)}, f32[288,128]{1,0:T(8,128)S(1)}, u32[]{:S(2)}, u32[]{:S(2)}) collective-permute-start(f32[288,128]{1,0:T(8,128)S(1)} %get-tuple-element.32), channel_id=1, source_target_pairs={{1,2},{3,4},{2,1},{5,6},{4,3},{6,5},{9,10},{11,12},{10,9},{13,14},... | collective-permute-start | bytes 442376 | tf_op jit(solution)/shard_map/ppermute | solution.py:525
  4.9 5.9 %collective-permute-start.1 = (f32[288,128]{1,0:T(8,128)S(1)}, f32[288,128]{1,0:T(8,128)S(1)}, u32[]{:S(2)}, u32[]{:S(2)}) collective-permute-start(f32[288,128]{1,0:T(8,128)S(1)} %get-tuple-element.33), channel_id=1, source_target_pairs={{0,2},{2,4},{3,1},{4,6},{5,3},{7,5},{8,10},{10,12},{11,9},{12,14},... | collective-permute-start | bytes 442376 | tf_op jit(solution)/shard_map/ppermute | solution.py:526
  11.4 5.8 %collective-permute-start.4 = (f32[192,128]{1,0:T(8,128)S(1)}, f32[192,128]{1,0:T(8,128)S(1)}, u32[]{:S(2)}, u32[]{:S(2)}) collective-permute-start(f32[192,128]{1,0:T(8,128)S(1)} %get-tuple-element.36), channel_id=1, source_target_pairs={{0,16},{1,9},{2,18},{3,11},{4,20},{5,13},{6,22},{7,15}} | collective-permute-start | bytes 294920 | tf_op jit(solution)/shard_map/ppermute | solution.py:548
  12.7 4.5 %collective-permute-start.3 = (f32[192,128]{1,0:T(8,128)S(1)}, f32[192,128]{1,0:T(8,128)S(1)}, u32[]{:S(2)}, u32[]{:S(2)}) collective-permute-start(f32[192,128]{1,0:T(8,128)S(1)} %get-tuple-element.36), channel_id=1, source_target_pairs={{0,24},{1,25},{2,26},{3,27},{4,28},{5,29},{6,30},{7,31}} | collective-permute-start | bytes 294920 | tf_op jit(solution)/shard_map/ppermute | solution.py:548
  13.4 3.9 %collective-permute-start.2 = (f32[192,128]{1,0:T(8,128)S(1)}, f32[192,128]{1,0:T(8,128)S(1)}, u32[]{:S(2)}, u32[]{:S(2)}) collective-permute-start(f32[192,128]{1,0:T(8,128)S(1)} %get-tuple-element.36), channel_id=1, source_target_pairs={{0,8},{1,17},{2,10},{3,19},{4,12},{5,21},{6,14},{7,23}} | collective-permute-start | bytes 294920 | tf_op jit(solution)/shard_map/ppermute | solution.py:548
  19.1 5.2 %collective-permute-start.5 = (f32[5,64,128]{2,1,0:T(8,128)S(1)}, f32[5,64,128]{2,1,0:T(8,128)S(1)}, u32[]{:S(2)}, u32[]{:S(2)}) collective-permute-start(f32[5,64,128]{2,1,0:T(8,128)S(1)} %get-tuple-element.40), channel_id=1, source_target_pairs={{0,1},{1,0},{2,3},{3,2},{4,5},{5,4},{6,7},{7,6},{8,9},{9,8},{10,11... | collective-permute-start | bytes 491528 | tf_op jit(solution)/shard_map/ppermute | solution.py:556

commit v13 on v11

--- a/solution.py
+++ b/solution.py
@@ -368,8 +368,8 @@
 
 
 def first_kernel(*refs):
-    bands_x, (band_z, pick, block, behind, ahead, other) = refs[:COUNTS], refs[COUNTS:-4]
-    held, sent, rows, carry = refs[-4:]
+    bands_x, (band_z, pick, block, behind, ahead, other) = refs[:COUNTS], refs[COUNTS:-2]
+    rows, carry = refs[-2:]
     band_x = {band.shape[0]: band for band in bands_x}
     assemble(carry, block, ahead, behind, other)
     section = lax.axis_index("sec")
@@ -406,7 +406,8 @@
             strain_x, strain_z = diff_x(band_x, parts_x), along_depth(band_z, parts_z)
             sxx = sxx + (both * strain_x + lame * strain_z)
             szz = szz + (lame * strain_x + both * strain_z)
-            sxz = sxz + shear * (along_depth(band_z, parts_x) + diff_x(band_x, parts_z))
+            if step < STEPS - 1:
+                sxz = sxz + shear * (along_depth(band_z, parts_x) + diff_x(band_x, parts_z))
             low = 2 * RADIUS * (step + 1) - at
             for component, (parts, factor) in enumerate(
                 ((parts_x, COUPLING), (parts_z, COUPLING), (halves(sxx + szz), -0.5 * COUPLING))
@@ -416,18 +417,21 @@
                 group, base = SLOT[step][component]
                 spot = pl.ds(base, picked.shape[0])
                 rows[spot] = jnp.where(lanes_of(picked.shape) == group, picked, rows[spot])
-        place([vx, vz, sxx, szz, sxz], held, sent)
+        for index, array in enumerate((vx, vz, sxx, szz, sxz, shear)):
+            carry[index, : array.shape[0]] = array
 
 
 def second_kernel(*refs):
-    bands_x, (band_z, land, carry, rows, held_in, sent_in, held, sent) = refs[:COUNTS], refs[COUNTS:]
+    bands_x, (band_z, land, carry, rows, held, sent) = refs[:COUNTS], refs[COUNTS:]
     band_x = {band.shape[0]: band for band in bands_x}
     section = lax.axis_index("sec")
 
     @pl.when(section == 0)
     def _():
-        held[...] = held_in[...]
-        sent[...] = sent_in[...]
+        count = WINDOWS[-1]
+        vx, vz, sxx, szz, sxz, shear = [carry[index, :count] for index in range(6)]
+        slope = along_depth(band_z, halves(vx)) + diff_x(band_x, halves(vz))
+        place([vx, vz, sxx, szz, sxz + shear * slope], held, sent)
 
     @pl.when(section > 0)
     def _():
@@ -533,14 +537,9 @@
         [plane_rows[None], box_offset[None]],
         1_000_000_000,
     )
-    held, sent, rows, carry = call(
+    rows, carry = call(
         first_kernel,
-        [
-            full(5, HALF, CELLS),
-            full(5, HALF, CELLS),
-            full(ROWS, CELLS),
-            full(9, WINDOW, DEPTH),
-        ],
+        [full(ROWS, CELLS), full(9, WINDOW, DEPTH)],
         [*bands, pick, block, behind, ahead, other],
         4_000_000_000,
     )
@@ -550,7 +549,7 @@
     held, sent = call(
         second_kernel,
         [full(5, HALF, CELLS), full(5, HALF, CELLS)],
-        [*bands, land, carry, rows, held, sent],
+        [*bands, land, carry, rows],
         4_000_000_000,
     )
     swapped = lax.ppermute(sent, "gz", turn)

time: 24.9 us -> 24.9 us (level)
  no operation moved by 1% of the time
where the time goes in v13:
time: 24.9 us; the launch traced here: 24.6 us
  waiting for transfers between devices  8.67 us (35%)
  starting transfers between devices  8.54 us (34%)
  Pallas kernels  4.79 us (19%)
  blocking collectives  2.42 us (10%)
    ppermute x3, waiting for transfers between devices, local_window(): arrived = [lax.ppermute(rows, ('sec', 'gz'), route) for route in routes]  6.55 us
    pallas_call x5, Pallas kernels, call(): pl.pallas_call(kernel, out_shape=outs, in_specs=[pl.BlockSpec(memory_spac...  4.79 us
    ppermute x1, starting transfers between devices, local_window(): behind = lax.ppermute(crossed, ('gx', 'gz'), crossed_pairs)  3.77 us
    ppermute x3, starting transfers between devices, local_window(): arrived = [lax.ppermute(rows, ('sec', 'gz'), route) for route in routes]  2.63 us
    all_gather x1, blocking collectives, local_window(): joined = lax.all_gather(swap, 'gz')  2.42 us
    ppermute x1, starting transfers between devices, local_window(): ahead = lax.ppermute(straight, ('gx', 'gz'), straight_pairs)  2.08 us
    ppermute x1, waiting for transfers between devices, local_window(): swapped = lax.ppermute(sent, 'gz', turn)  1.38 us
    ppermute x1, waiting for transfers between devices, local_window(): ahead = lax.ppermute(straight, ('gx', 'gz'), straight_pairs)  0.74 us
  transfers between devices with their start and end apart: 6, of which 3 were waited for; matrix products, arithmetic and copies ran while one was open for 0% of the time, Pallas kernels for 2%

profile of v13, /device:TPU:19, one launch (start us, length us, event | category | flops | bytes accessed | tf_op | source)
XLA Modules:
  0.0 24.6 jit_solution(2052707053452458713)
XLA Ops:
  0.0 1.1 %shard_map.47 = (f32[8,128,128]{2,1,0:T(8,128)S(1)}, f32[288,128]{1,0:T(8,128)S(1)}, f32[288,128]{1,0:T(8,128)S(1)}, f32[8,104,128]{2,1,0:T(8,128)S(1)}) custom-call(f32[5,128,128]{2,1,0:T(8,128)} %bitcast.7, f32[3,128,128]{2,1,0:T(8,128)} %bitcast.8), custom_call_target="tpu_custom_call" | custom-call | flops 1000 | bytes 2097152 | tf_op jit(solution)/shard_map/pallas_call | solution.py:482
  1.1 0.0 copy-start
  1.1 0.0 copy-start.1
  1.1 3.8 %collective-permute-start = (f32[288,128]{1,0:T(8,128)S(1)}, f32[288,128]{1,0:T(8,128)S(1)}, u32[]{:S(2)}, u32[]{:S(2)}) collective-permute-start(f32[288,128]{1,0:T(8,128)S(1)} %get-tuple-element.30), channel_id=1, source_target_pairs={{1,2},{3,4},{2,1},{5,6},{4,3},{6,5},{9,10},{11,12},{10,9},{13,14},... | collective-permute-start | bytes 442376 | tf_op jit(solution)/shard_map/ppermute | solution.py:529
  4.9 2.1 %collective-permute-start.1 = (f32[288,128]{1,0:T(8,128)S(1)}, f32[288,128]{1,0:T(8,128)S(1)}, u32[]{:S(2)}, u32[]{:S(2)}) collective-permute-start(f32[288,128]{1,0:T(8,128)S(1)} %get-tuple-element.31), channel_id=1, source_target_pairs={{0,2},{2,4},{3,1},{4,6},{5,3},{7,5},{8,10},{10,12},{11,9},{12,14},... | collective-permute-start | bytes 442376 | tf_op jit(solution)/shard_map/ppermute | solution.py:530
  7.0 2.4 %all-gather = f32[16,104,128]{2,1,0:T(8,128)S(1)} all-gather(f32[8,104,128]{2,1,0:T(8,128)S(1)} %get-tuple-element.32), channel_id=2, replica_groups=mesh['sec'=4,'gx'=4,'gz'=2] {'gz'}, dimensions={0}, use_global_device_ids=true | all-gather | bytes 1277952 | tf_op jit(solution)/shard_map/all_gather | solution.py:531
  9.5 0.0 copy-done
  9.5 0.0 copy-done.1
  9.5 0.6 %shard_map.46 = (bf16[144,288]{1,0:T(8,128)(2,1)S(1)}, bf16[128,256]{1,0:T(8,128)(2,1)S(1)}, bf16[112,224]{1,0:T(8,128)(2,1)S(1)}, bf16[96,192]{1,0:T(8,128)(2,1...) custom-call(s32[1,16]{1,0:T(1,128)S(1)} %bitcast.5, ...), custom_call_target="tpu_custom_call" | custom-call | flops 1000000000 | bytes 2097152 | tf_op jit(solution)/shard_map/pallas_call | solution.py:482
  10.0 0.0 collective-permute-done.refs_8_
  10.0 0.7 %collective-permute-done.1.refs_9_ = f32[288,128]{1,0:T(8,128)S(1)} collective-permute-done((f32[288,128]{1,0:T(8,128)S(1)}, f32[288,128]{1,0:T(8,128)S(1)}, u32[]{:S(2)}, u32[]{:S(2)}) %collective-permute-start.1) | collective-permute-done | bytes 147488 | tf_op jit(solution)/shard_map/ppermute | solution.py:530
  10.8 0.6 %shard_map.48 = (f32[192,128]{1,0:T(8,128)S(1)}, f32[9,144,256]{2,1,0:T(8,128)S(1)}) custom-call(bf16[144,288]{1,0:T(8,128)(2,1)S(1)} %get-tuple-element.21.refs_0_, bf16[128,256]{1,0:T(8,128)(2,1)S(1)} %get-tuple-element.22.refs_1_, bf16[112,224]{1,0:T(8,128)(2,1)S(1)} %get-tuple-element.23.refs_2_, bf16[96,192]{1,0:T(8,128)(2,1)S(1)} %get-tuple-element.24.refs_3_, ...), custom_call_target="tpu_custom_call" | custom-call | flops 4000000000 | bytes 2097152 | tf_op jit(solution)/shard_map/pallas_call | solution.py:482
  11.4 0.7 %collective-permute-start.4 = (f32[192,128]{1,0:T(8,128)S(1)}, f32[192,128]{1,0:T(8,128)S(1)}, u32[]{:S(2)}, u32[]{:S(2)}) collective-permute-start(f32[192,128]{1,0:T(8,128)S(1)} %get-tuple-element.34), channel_id=1, source_target_pairs={{0,8},{1,17},{2,10},{3,19},{4,12},{5,21},{6,14},{7,23}} | collective-permute-start | bytes 294920 | tf_op jit(solution)/shard_map/ppermute | solution.py:547
  12.1 0.7 %collective-permute-start.3 = (f32[192,128]{1,0:T(8,128)S(1)}, f32[192,128]{1,0:T(8,128)S(1)}, u32[]{:S(2)}, u32[]{:S(2)}) collective-permute-start(f32[192,128]{1,0:T(8,128)S(1)} %get-tuple-element.34), channel_id=1, source_target_pairs={{0,24},{1,25},{2,26},{3,27},{4,28},{5,29},{6,30},{7,31}} | collective-permute-start | bytes 294920 | tf_op jit(solution)/shard_map/ppermute | solution.py:547
  12.8 1.3 %collective-permute-start.2 = (f32[192,128]{1,0:T(8,128)S(1)}, f32[192,128]{1,0:T(8,128)S(1)}, u32[]{:S(2)}, u32[]{:S(2)}) collective-permute-start(f32[192,128]{1,0:T(8,128)S(1)} %get-tuple-element.34), channel_id=1, source_target_pairs={{0,16},{1,9},{2,18},{3,11},{4,20},{5,13},{6,22},{7,15}} | collective-permute-start | bytes 294920 | tf_op jit(solution)/shard_map/ppermute | solution.py:547
  14.1 0.0 collective-permute-done.4
  14.1 0.0 collective-permute-done.3
  14.1 6.5 %collective-permute-done.2 = f32[192,128]{1,0:T(8,128)S(1)} collective-permute-done((f32[192,128]{1,0:T(8,128)S(1)}, f32[192,128]{1,0:T(8,128)S(1)}, u32[]{:S(2)}, u32[]{:S(2)}) %collective-permute-start.2) | collective-permute-done | bytes 98336 | tf_op jit(solution)/shard_map/ppermute | solution.py:547
  20.6 1.8 %shard_map.49 = (f32[5,64,128]{2,1,0:T(8,128)S(1)}, f32[5,64,128]{2,1,0:T(8,128)S(1)}) custom-call(bf16[144,288]{1,0:T(8,128)(2,1)S(1)} %get-tuple-element.21.refs_0_, bf16[128,256]{1,0:T(8,128)(2,1)S(1)} %get-tuple-element.22.refs_1_, bf16[112,224]{1,0:T(8,128)(2,1)S(1)} %get-tuple-element.23.refs_2_, bf16[96,192]{1,0:T(8,128)(2,1)S(1)} %get-tuple-element.24.refs_3_, ...), custom_call_target="tpu_custom_call" | custom-call | flops 4000000000 | bytes 2097152 | tf_op jit(solution)/shard_map/pallas_call | solution.py:482
  22.4 0.1 collective-permute-start.5
  22.5 1.4 %collective-permute-done.5.swapped = f32[5,64,128]{2,1,0:T(8,128)S(1)} collective-permute-done((f32[5,64,128]{2,1,0:T(8,128)S(1)}, f32[5,64,128]{2,1,0:T(8,128)S(1)}, u32[]{:S(2)}, u32[]{:S(2)}) %collective-permute-start.5) | collective-permute-done | bytes 163872 | tf_op jit(solution)/shard_map/ppermute | solution.py:555
  23.9 0.7 %shard_map.50 = f32[5,128,128]{2,1,0:T(8,128)} custom-call(f32[5,64,128]{2,1,0:T(8,128)S(1)} %get-tuple-element.35.held, f32[5,64,128]{2,1,0:T(8,128)S(1)} %collective-permute-done.5.swapped), custom_call_target="tpu_custom_call" | custom-call | flops 1000 | bytes 2097152 | tf_op jit(solution)/shard_map/pallas_call | solution.py:482
  (2 shorter events, 0.1 us)
Async XLA Ops:
  1.1 8.4 %copy-start = (s32[16]{0:T(128)S(1)}, s32[16]{0:T(128)}, u32[]{:S(2)}) copy-start(s32[16]{0:T(128)} %param.6) | copy-start | bytes 196
  1.1 8.4 %copy-start.1 = (s32[3]{0:T(128)S(1)}, s32[3]{0:T(128)}, u32[]{:S(2)}) copy-start(s32[3]{0:T(128)} %param.7) | copy-start | bytes 40
  1.1 8.9 %collective-permute-start = (f32[288,128]{1,0:T(8,128)S(1)}, f32[288,128]{1,0:T(8,128)S(1)}, u32[]{:S(2)}, u32[]{:S(2)}) collective-permute-start(f32[288,128]{1,0:T(8,128)S(1)} %get-tuple-element.30), channel_id=1, source_target_pairs={{1,2},{3,4},{2,1},{5,6},{4,3},{6,5},{9,10},{11,12},{10,9},{13,14},... | collective-permute-start | bytes 442376 | tf_op jit(solution)/shard_map/ppermute | solution.py:529
  4.9 5.9 %collective-permute-start.1 = (f32[288,128]{1,0:T(8,128)S(1)}, f32[288,128]{1,0:T(8,128)S(1)}, u32[]{:S(2)}, u32[]{:S(2)}) collective-permute-start(f32[288,128]{1,0:T(8,128)S(1)} %get-tuple-element.31), channel_id=1, source_target_pairs={{0,2},{2,4},{3,1},{4,6},{5,3},{7,5},{8,10},{10,12},{11,9},{12,14},... | collective-permute-start | bytes 442376 | tf_op jit(solution)/shard_map/ppermute | solution.py:530
  11.4 2.7 %collective-permute-start.4 = (f32[192,128]{1,0:T(8,128)S(1)}, f32[192,128]{1,0:T(8,128)S(1)}, u32[]{:S(2)}, u32[]{:S(2)}) collective-permute-start(f32[192,128]{1,0:T(8,128)S(1)} %get-tuple-element.34), channel_id=1, source_target_pairs={{0,8},{1,17},{2,10},{3,19},{4,12},{5,21},{6,14},{7,23}} | collective-permute-start | bytes 294920 | tf_op jit(solution)/shard_map/ppermute | solution.py:547
  12.1 2.0 %collective-permute-start.3 = (f32[192,128]{1,0:T(8,128)S(1)}, f32[192,128]{1,0:T(8,128)S(1)}, u32[]{:S(2)}, u32[]{:S(2)}) collective-permute-start(f32[192,128]{1,0:T(8,128)S(1)} %get-tuple-element.34), channel_id=1, source_target_pairs={{0,24},{1,25},{2,26},{3,27},{4,28},{5,29},{6,30},{7,31}} | collective-permute-start | bytes 294920 | tf_op jit(solution)/shard_map/ppermute | solution.py:547
  12.8 7.9 %collective-permute-start.2 = (f32[192,128]{1,0:T(8,128)S(1)}, f32[192,128]{1,0:T(8,128)S(1)}, u32[]{:S(2)}, u32[]{:S(2)}) collective-permute-start(f32[192,128]{1,0:T(8,128)S(1)} %get-tuple-element.34), channel_id=1, source_target_pairs={{0,16},{1,9},{2,18},{3,11},{4,20},{5,13},{6,22},{7,15}} | collective-permute-start | bytes 294920 | tf_op jit(solution)/shard_map/ppermute | solution.py:547
  22.4 1.5 %collective-permute-start.5 = (f32[5,64,128]{2,1,0:T(8,128)S(1)}, f32[5,64,128]{2,1,0:T(8,128)S(1)}, u32[]{:S(2)}, u32[]{:S(2)}) collective-permute-start(f32[5,64,128]{2,1,0:T(8,128)S(1)} %get-tuple-element.36), channel_id=1, source_target_pairs={{0,1},{1,0},{2,3},{3,2},{4,5},{5,4},{6,7},{7,6},{8,9},{9,8},{10,11... | collective-permute-start | bytes 491528 | tf_op jit(solution)/shard_map/ppermute | solution.py:555
